TPU v7x, 256 devices: a whole 4x4x8 slice. The times are simulated.
256 devices in a mesh: row: 16 (over z_lo, y), col: 4 (over x), dp: 4 (over z_hi, core).
Axes of the slice: x: 4, y: 4, z: 8 (z_hi: 2, z_lo: 4; z = z_hi * 4 + z_lo), core: 2. Of those that a mesh axis runs over, the one named last changes fastest.
Arguments:
- image: bfloat16 [4, 256, 384, 512], P('dp', None, 'row', 'col'), may hold values from -6 to 6
- labels: int32 [4, 16, 8], P('dp', 'row', 'col'), may hold values from 0 to 7
- weights: float32 [141312], replicated, may hold values from -0.375 to 0.375
- momentum: float32 [141312], P(('row', 'col', 'dp')), may hold values from -0.006 to 0.006
Outputs:
- new_weights: float32 [141312], P(('row', 'col', 'dp'))
- new_momentum: float32 [141312], P(('row', 'col', 'dp'))
- update: float32 [141312], P(('row', 'col', 'dp'))
- loss: float32 [], replicated
All inputs are finite; a program needn't handle non-finite values. Where the computation divides by a largest or mean magnitude, that divisor is 1e-20 or more.
Results may differ from a plain program's by a relative error of at most 0.0011.
Values may be sent and summed in bfloat16 or wider, within the bound.
No kernel may reach another device: no remote copies, remote signals or barrier semaphores. Data moves between devices by JAX's collectives and lax.ppermute only.
A program may use at most 64 MiB of HBM per device.

v0:
```python
import jax
import jax.numpy as jnp
from jax import lax
from jax.sharding import PartitionSpec as P

C = 256
MID = 64
CLASSES = 8
TILE_ROWS = 24
TILE_COLS = 64


beta_one = 0.9
beta_two = 0.99
learn_rate = 0.0001
weight_decay = 0.1


def extended(block, sides, width):
    for axis, dim in sides:
        count = lax.axis_size(axis)
        forward = [(i, i + 1) for i in range(count - 1)]
        backward = [(target, source) for source, target in forward]
        low = lax.ppermute(
            lax.slice_in_dim(block, block.shape[dim] - width, None, axis=dim), axis, forward
        )
        high = lax.ppermute(lax.slice_in_dim(block, 0, width, axis=dim), axis, backward)
        block = jnp.concatenate([low, block, high], axis=dim)
    return block


def unpack(weights):
    offset = 0
    blocks_list = []
    for number in range(2):
        w_in = weights[offset : offset + C * MID].reshape(C, MID)
        offset = offset + C * MID
        w_mid = weights[offset : offset + 9 * MID * MID].reshape(9, MID, MID)
        offset = offset + 9 * MID * MID
        w_out = weights[offset : offset + MID * C].reshape(MID, C)
        offset = offset + MID * C
        blocks_list.append(
            (w_in.astype(jnp.bfloat16), w_mid.astype(jnp.bfloat16), w_out.astype(jnp.bfloat16))
        )
    head = weights[offset:].reshape(C, CLASSES)
    return (blocks_list, head)


def forward_rim(field):
    return extended(field, (("row", 1), ("col", 2)), 1)


def backward_rim(field):
    return extended(field, (("row", 1), ("col", 2)), 1)


def conv_taps(w_mid, padded, height, width):
    total = jnp.zeros((w_mid.shape[2], height, width), jnp.float32)
    for position in range(9):
        shift_row = position // 3
        shift_col = position % 3
        total = total + jnp.einsum(
            "io,ihw->ohw",
            w_mid[position],
            padded[:, shift_row : shift_row + height, shift_col : shift_col + width],
            preferred_element_type=jnp.float32,
        )
    return total


def local(image, labels, weights, momentum):
    inputs = image[0]
    label_grid = labels[0]
    height, width = (inputs.shape[1], inputs.shape[2])
    blocks_list, head = unpack(weights)
    total_tiles = (
        label_grid.shape[0]
        * label_grid.shape[1]
        * lax.axis_size("row")
        * lax.axis_size("col")
        * lax.axis_size("dp")
    )
    stored = []
    for w_in, w_mid, w_out in blocks_list:
        h_first = jnp.maximum(
            jnp.einsum("io,ihw->ohw", w_in, inputs, preferred_element_type=jnp.float32), 0.0
        ).astype(jnp.bfloat16)
        padded = forward_rim(h_first)
        h_second = jnp.maximum(conv_taps(w_mid, padded, height, width), 0.0).astype(jnp.bfloat16)
        output = jnp.maximum(
            jnp.einsum("io,ihw->ohw", w_out, h_second, preferred_element_type=jnp.float32)
            + inputs.astype(jnp.float32),
            0.0,
        ).astype(jnp.bfloat16)
        kept = padded
        stored.append((inputs, kept, h_second, output))
        inputs = output
    tiles_a = height // TILE_ROWS
    tiles_b = width // TILE_COLS
    pooled = jnp.mean(
        inputs.astype(jnp.float32).reshape(C, tiles_a, TILE_ROWS, tiles_b, TILE_COLS), axis=(2, 4)
    )
    logits = jnp.einsum("cab,ck->abk", pooled, head, precision=lax.Precision.HIGHEST)
    highest = jnp.max(logits, axis=-1, keepdims=True)
    logsum = jnp.log(jnp.sum(jnp.exp(logits - highest), axis=-1, keepdims=True)) + highest
    onehot = (label_grid[:, :, None] == jnp.arange(CLASSES, dtype=jnp.int32)).astype(jnp.float32)
    loss_part = jnp.sum(logsum[:, :, 0] - jnp.sum(onehot * logits, axis=-1))
    dlogits = (jnp.exp(logits - logsum) - onehot) / total_tiles
    grad_head = jnp.einsum("cab,abk->ck", pooled, dlogits, precision=lax.Precision.HIGHEST)
    dpooled = jnp.einsum("abk,ck->cab", dlogits, head, precision=lax.Precision.HIGHEST) / (
        TILE_ROWS * TILE_COLS
    )
    upstream = (
        jnp.broadcast_to(dpooled[:, :, None, :, None], (C, tiles_a, TILE_ROWS, tiles_b, TILE_COLS))
        .reshape(C, height, width)
        .astype(jnp.bfloat16)
    )
    grads = [None, None]
    for number in (1, 0):
        w_in, w_mid, w_out = blocks_list[number]
        inputs, kept, h_second, output = stored[number]
        padded = kept
        d_sum = jnp.where(output > 0, upstream, jnp.zeros_like(upstream))
        grad_out = jnp.einsum("ihw,ohw->io", h_second, d_sum, preferred_element_type=jnp.float32)
        d_second = jnp.einsum("io,ohw->ihw", w_out, d_sum, preferred_element_type=jnp.float32)
        d_second = jnp.where(h_second > 0, d_second, 0.0).astype(jnp.bfloat16)
        spread_back = backward_rim(d_second)
        grad_mid = jnp.stack(
            [
                jnp.einsum(
                    "ihw,ohw->io",
                    padded[
                        :,
                        position // 3 : position // 3 + height,
                        position % 3 : position % 3 + width,
                    ],
                    d_second,
                    preferred_element_type=jnp.float32,
                )
                for position in range(9)
            ]
        )
        d_first = jnp.zeros((MID, height, width), jnp.float32)
        for position in range(9):
            shift_row = 2 - position // 3
            shift_col = 2 - position % 3
            d_first = d_first + jnp.einsum(
                "io,ohw->ihw",
                w_mid[position],
                spread_back[:, shift_row : shift_row + height, shift_col : shift_col + width],
                preferred_element_type=jnp.float32,
            )
        h_first = padded[:, 1:-1, 1:-1]
        d_first = jnp.where(h_first > 0, d_first, 0.0).astype(jnp.bfloat16)
        grad_in = jnp.einsum("ihw,ohw->io", inputs, d_first, preferred_element_type=jnp.float32)
        if number == 1:
            upstream = (
                jnp.einsum("io,ohw->ihw", w_in, d_first, preferred_element_type=jnp.float32)
                + d_sum.astype(jnp.float32)
            ).astype(jnp.bfloat16)
        grads[number] = jnp.concatenate([grad_in.ravel(), grad_mid.ravel(), grad_out.ravel()])
    flat = jnp.concatenate([grads[0], grads[1], grad_head.ravel()])
    share = momentum.shape[0]
    start = lax.axis_index(("row", "col", "dp")) * share
    total = lax.psum(flat, ("row", "col", "dp"))
    grad = lax.dynamic_slice_in_dim(total, start, share, 0)
    weight_share = lax.dynamic_slice_in_dim(weights, start, share, 0)
    mixed = beta_one * momentum + (1.0 - beta_one) * grad
    abs_total, loss_total = lax.psum((jnp.sum(jnp.abs(mixed)), loss_part), ("row", "col", "dp"))
    scale_tau = abs_total / weights.shape[0] + 1e-06
    update = mixed / (jnp.abs(mixed) + scale_tau)
    new_weights = weight_share - learn_rate * (update + weight_decay * weight_share)
    new_momentum = beta_two * momentum + (1.0 - beta_two) * grad
    return (new_weights, new_momentum, update, loss_total / total_tiles)


def solution(mesh):
    in_specs = (P("dp", None, "row", "col"), P("dp", "row", "col"), P(), P(("row", "col", "dp")))
    out_specs = (P(("row", "col", "dp")), P(("row", "col", "dp")), P(("row", "col", "dp")), P())
    return jax.shard_map(local, mesh=mesh, in_specs=in_specs, out_specs=out_specs, check_vma=False)
```

profile of v0, /device:TPU:1, one launch (start us, length us, event | category | flops | bytes accessed | tf_op | source)
XLA Modules:
  0.0 507.8 jit_solution(5712481853332794097)
XLA Ops:
  7.2 1.1 convert.8
  9.7 2.1 copy.93
  11.9 2.3 convert_reduce_fusion.1
  14.8 4.6 collective-permute-start
  19.4 1.3 collective-permute-start.1
  22.1 1.9 fusion.157
  24.0 1.6 and_convert_fusion
  25.8 1.9 copy.59
  40.3 3.1 collective-permute-start.2
  43.5 1.3 collective-permute-start.3
  44.8 1.0 fusion.139
  45.8 1.0 fusion.138
  46.8 4.8 collective-permute-done.2
  51.6 3.8 collective-permute-done.3
  55.4 1.4 maximum_maximum_fusion
  61.6 3.7 collective-permute-start.4
  65.3 1.3 collective-permute-start.5
  67.0 2.9 collective-permute-done.5
  70.1 3.1 collective-permute-start.6
  73.2 1.5 collective-permute-start.7
  75.3 2.9 collective-permute-done.6
  78.3 3.8 collective-permute-done.7
  91.6 1.3 collective-permute-start.9
  92.9 4.0 collective-permute-start.8
  96.9 1.1 fusion.197
  99.9 1.1 reshape.196
  101.3 1.3 collective-permute-start.10
  102.6 4.2 collective-permute-start.11
  107.3 2.8 collective-permute-done.10
  110.1 1.5 collective-permute-done.11
  114.8 1.0 copy-done.12
  122.9 1.3 collective-permute-start.13
  124.2 5.2 %collective-permute-start.12 = (bf16[64,1,128]{2,0,1:T(8,128)(2,1)}, bf16[64,1,128]{2,0,1:T(8,128)(2,1)S(1)}, u32[]{:S(2)}, u32[]{:S(2)}) collective-permute-start(bf16[64,1,128]{2,0,1:T(8,128)(2,1)} %get-tuple-element.29), channel_id=1, source_target_pairs={{0,16},{16,32},{32,48},{48,64},{64,80},{80,96},{96,112},{112,128},... | collective-permute-start | bytes 49160 | tf_op jit(solution)/shard_map/ppermute | solution.py:24
  129.3 1.1 fusion.198
  130.9 1.1 reshape.193
  133.0 1.3 collective-permute-start.14
  134.3 4.8 collective-permute-start.15
  139.3 1.1 fusion.76
  140.5 2.2 collective-permute-done.14
  142.6 1.5 collective-permute-done.15
  145.1 1.2 fusion.78
  146.6 1.2 fusion.74
  147.8 1.3 fusion.13
  149.3 2.4 fusion.49
  153.0 267.2 %all-reduce.3.cloned.1.call-done = f32[141312]{0:T(1024)} async-done(((f32[141312]{0:T(1024)}), f32[141312]{0:T(1024)}) %all-reduce.3.cloned.1.call-update) | async-done | bytes 565264 | tf_op jit(solution)/shard_map/psum | solution.py:165
  420.1 1.4 abs_reduce_fusion
  421.5 75.6 %all-reduce = (f32[]{:T(128)}, f32[]{:T(128)}) all-reduce(f32[]{:T(128)} %abs_reduce_fusion, f32[]{:T(128)} %get-tuple-element.10), channel_id=1, replica_groups=mesh['row'=16,'col'=4,'dp'=4] {'row','col','dp'}, use_global_device_ids=true, to_apply=%region_6.7 | all-reduce | flops 2 | bytes 16 | tf_op jit(solution)/shard_map/psum | solution.py:169
  498.4 1.4 multiply_subtract_fusion
  (265 shorter events, 48.0 us)
Async XLA Ops:
  7.2 413.0 %all-reduce.3.cloned.1.call-start = ((), (), s32[]{:S(2)}) async-start(), calls=%async_computation | async-start | bytes 1130496 | tf_op jit(solution)/shard_map/psum | solution.py:165
  11.9 12.1 %copy-start = (bf16[256,24,128]{0,2,1:T(8,128)(2,1)}, bf16[256,24,128]{0,2,1:T(8,128)(2,1)S(1)}, u32[]{:S(2)}) copy-start(bf16[256,24,128]{0,2,1:T(8,128)(2,1)S(1)} %copy.93) | copy-start | bytes 4718596
  11.9 8.8 %copy-start.14 = (bf16[141312]{0:T(1024)(128)(2,1)S(1)}, bf16[141312]{0:T(1024)(128)(2,1)}, u32[]{:S(2)}) copy-start(bf16[141312]{0:T(1024)(128)(2,1)} %copy-done.13) | copy-start | bytes 847876
  11.9 13.7 %copy-start.2 = (bf16[1,256,24,128]{3,2,1,0:T(8,128)(2,1)S(1)}, bf16[1,256,24,128]{3,2,1,0:T(8,128)(2,1)}, u32[]{:S(2)}) copy-start(bf16[1,256,24,128]{3,2,1,0:T(8,128)(2,1)} %param.4) | copy-start | bytes 4718596
  14.8 24.5 %collective-permute-start = (bf16[64,1,128]{2,0,1:T(8,128)(2,1)}, bf16[64,1,128]{2,0,1:T(8,128)(2,1)}, u32[]{:S(2)}, u32[]{:S(2)}) collective-permute-start(bf16[64,1,128]{2,0,1:T(8,128)(2,1)} %get-tuple-element.35), channel_id=1, source_target_pairs={{0,16},{16,32},{32,48},{48,64},{64,80},{80,96},{96,112},{112,128},... | collective-permute-start | bytes 49160 | tf_op jit(solution)/shard_map/ppermute | solution.py:24
  19.4 19.9 %collective-permute-start.1 = (bf16[64,1,128]{2,0,1:T(8,128)(2,1)}, bf16[64,1,128]{2,0,1:T(8,128)(2,1)}, u32[]{:S(2)}, u32[]{:S(2)}) collective-permute-start(bf16[64,1,128]{2,0,1:T(8,128)(2,1)} %get-tuple-element.36), channel_id=1, source_target_pairs={{16,0},{32,16},{48,32},{64,48},{80,64},{96,80},{112,96},{128,112},... | collective-permute-start | bytes 49160 | tf_op jit(solution)/shard_map/ppermute | solution.py:27
  25.6 3.3 copy-start.38
  25.7 4.1 copy-start.37
  25.7 4.8 copy-start.36
  25.7 5.6 %copy-start.35 = (bf16[4096]{0:T(1024)(128)(2,1)S(1)}, bf16[4096]{0:T(1024)(128)(2,1)}, u32[]{:S(2)}) copy-start(bf16[4096]{0:T(1024)(128)(2,1)} %get-tuple-element.38) | copy-start | bytes 24580
  25.7 6.4 %copy-start.34 = (bf16[4096]{0:T(1024)(128)(2,1)S(1)}, bf16[4096]{0:T(1024)(128)(2,1)}, u32[]{:S(2)}) copy-start(bf16[4096]{0:T(1024)(128)(2,1)} %get-tuple-element.37) | copy-start | bytes 24580
  25.7 7.1 %copy-start.33 = (bf16[4096]{0:T(1024)(128)(2,1)S(1)}, bf16[4096]{0:T(1024)(128)(2,1)}, u32[]{:S(2)}) copy-start(bf16[4096]{0:T(1024)(128)(2,1)} %get-tuple-element.53) | copy-start | bytes 24580
  25.7 7.9 %copy-start.32 = (bf16[4096]{0:T(1024)(128)(2,1)S(1)}, bf16[4096]{0:T(1024)(128)(2,1)}, u32[]{:S(2)}) copy-start(bf16[4096]{0:T(1024)(128)(2,1)} %get-tuple-element.51) | copy-start | bytes 24580
  25.7 8.6 %copy-start.31 = (bf16[4096]{0:T(1024)(128)(2,1)S(1)}, bf16[4096]{0:T(1024)(128)(2,1)}, u32[]{:S(2)}) copy-start(bf16[4096]{0:T(1024)(128)(2,1)} %get-tuple-element.52) | copy-start | bytes 24580
  25.7 9.4 %copy-start.30 = (bf16[4096]{0:T(1024)(128)(2,1)S(1)}, bf16[4096]{0:T(1024)(128)(2,1)}, u32[]{:S(2)}) copy-start(bf16[4096]{0:T(1024)(128)(2,1)} %copy-done.29) | copy-start | bytes 24580
  25.7 9.4 %copy-start.28 = (bf16[4096]{0:T(1024)(128)(2,1)S(1)}, bf16[4096]{0:T(1024)(128)(2,1)}, u32[]{:S(2)}) copy-start(bf16[4096]{0:T(1024)(128)(2,1)} %get-tuple-element.54) | copy-start | bytes 24580
  25.7 10.2 %copy-start.27 = (bf16[4096]{0:T(1024)(128)(2,1)S(1)}, bf16[4096]{0:T(1024)(128)(2,1)}, u32[]{:S(2)}) copy-start(bf16[4096]{0:T(1024)(128)(2,1)} %get-tuple-element.47) | copy-start | bytes 24580
  25.8 11.0 %copy-start.26 = (bf16[4096]{0:T(1024)(128)(2,1)S(1)}, bf16[4096]{0:T(1024)(128)(2,1)}, u32[]{:S(2)}) copy-start(bf16[4096]{0:T(1024)(128)(2,1)} %get-tuple-element.48) | copy-start | bytes 24580
  25.8 11.7 %copy-start.25 = (bf16[4096]{0:T(1024)(128)(2,1)S(1)}, bf16[4096]{0:T(1024)(128)(2,1)}, u32[]{:S(2)}) copy-start(bf16[4096]{0:T(1024)(128)(2,1)} %get-tuple-element.46) | copy-start | bytes 24580
  25.8 13.2 %copy-start.24 = (bf16[16384]{0:T(1024)(128)(2,1)S(1)}, bf16[16384]{0:T(1024)(128)(2,1)}, u32[]{:S(2)}) copy-start(bf16[16384]{0:T(1024)(128)(2,1)} %get-tuple-element.57) | copy-start | bytes 98308
  25.8 13.3 %copy-start.22 = (bf16[16384]{0:T(1024)(128)(2,1)S(1)}, bf16[16384]{0:T(1024)(128)(2,1)}, u32[]{:S(2)}) copy-start(bf16[16384]{0:T(1024)(128)(2,1)} %get-tuple-element.55) | copy-start | bytes 98308
  25.8 13.3 %copy-start.23 = (bf16[16384]{0:T(1024)(128)(2,1)S(1)}, bf16[16384]{0:T(1024)(128)(2,1)}, u32[]{:S(2)}) copy-start(bf16[16384]{0:T(1024)(128)(2,1)} %get-tuple-element.56) | copy-start | bytes 98308
  25.8 13.4 %slice-start = ((f32[141312]{0:T(1024)}), f32[2048]{0:T(1024)S(1)}, s32[]{:S(2)}) async-start(f32[141312]{0:T(1024)} %param.6), calls=%async_computation.1 | async-start | bytes 16384 | tf_op jit(solution)/shard_map/slice | solution.py:45
  40.3 11.3 %collective-permute-start.2 = (bf16[64,26,1]{2,0,1:T(8,128)(2,1)S(1)}, bf16[64,26,1]{2,0,1:T(8,128)(2,1)S(1)}, u32[]{:S(2)}, u32[]{:S(2)}) collective-permute-start(bf16[64,26,1]{2,0,1:T(8,128)(2,1)S(1)} %get-tuple-element.27), channel_id=1, source_target_pairs={{0,4},{4,8},{8,12},{1,5},{5,9},{9,13},{2,6},{6,10},{10,14},{3,7},{... | collective-permute-start | bytes 9992 | tf_op jit(solution)/shard_map/ppermute | solution.py:24
  43.5 12.0 %collective-permute-start.3 = (bf16[64,26,1]{2,0,1:T(8,128)(2,1)S(1)}, bf16[64,26,1]{2,0,1:T(8,128)(2,1)S(1)}, u32[]{:S(2)}, u32[]{:S(2)}) collective-permute-start(bf16[64,26,1]{2,0,1:T(8,128)(2,1)S(1)} %get-tuple-element.28), channel_id=1, source_target_pairs={{4,0},{8,4},{12,8},{5,1},{9,5},{13,9},{6,2},{10,6},{14,10},{7,3},{... | collective-permute-start | bytes 9992 | tf_op jit(solution)/shard_map/ppermute | solution.py:27
  61.6 5.3 %collective-permute-start.4 = (bf16[64,1,128]{2,0,1:T(8,128)(2,1)S(1)}, bf16[64,1,128]{2,0,1:T(8,128)(2,1)S(1)}, u32[]{:S(2)}, u32[]{:S(2)}) collective-permute-start(bf16[64,1,128]{2,0,1:T(8,128)(2,1)S(1)} %get-tuple-element.33), channel_id=1, source_target_pairs={{0,16},{16,32},{32,48},{48,64},{64,80},{80,96},{96,112},{112,128},... | collective-permute-start | bytes 49160 | tf_op jit(solution)/shard_map/ppermute | solution.py:24
  65.3 4.5 collective-permute-start.5
  70.1 8.2 %collective-permute-start.6 = (bf16[64,26,1]{2,0,1:T(8,128)(2,1)S(1)}, bf16[64,26,1]{2,0,1:T(8,128)(2,1)S(1)}, u32[]{:S(2)}, u32[]{:S(2)}) collective-permute-start(bf16[64,26,1]{2,0,1:T(8,128)(2,1)S(1)} %get-tuple-element.23), channel_id=1, source_target_pairs={{0,4},{4,8},{8,12},{1,5},{5,9},{9,13},{2,6},{6,10},{10,14},{3,7},{... | collective-permute-start | bytes 9992 | tf_op jit(solution)/shard_map/ppermute | solution.py:24
  73.2 8.9 %collective-permute-start.7 = (bf16[64,26,1]{2,0,1:T(8,128)(2,1)S(1)}, bf16[64,26,1]{2,0,1:T(8,128)(2,1)S(1)}, u32[]{:S(2)}, u32[]{:S(2)}) collective-permute-start(bf16[64,26,1]{2,0,1:T(8,128)(2,1)S(1)} %get-tuple-element.24), channel_id=1, source_target_pairs={{4,0},{8,4},{12,8},{5,1},{9,5},{13,9},{6,2},{10,6},{14,10},{7,3},{... | collective-permute-start | bytes 9992 | tf_op jit(solution)/shard_map/ppermute | solution.py:27
  91.6 5.3 %copy-start.19 = (f32[9,64,64]{2,1,0:T(8,128)}, f32[9,64,64]{2,1,0:T(8,128)S(1)}, u32[]{:S(2)}) copy-start(f32[9,64,64]{2,1,0:T(8,128)S(1)} %fusion.54) | copy-start | bytes 442372
  91.6 9.3 %collective-permute-start.9 = (bf16[64,1,128]{2,0,1:T(8,128)(2,1)}, bf16[64,1,128]{2,0,1:T(8,128)(2,1)S(1)}, u32[]{:S(2)}, u32[]{:S(2)}) collective-permute-start(bf16[64,1,128]{2,0,1:T(8,128)(2,1)} %get-tuple-element.32), channel_id=1, source_target_pairs={{16,0},{32,16},{48,32},{64,48},{80,64},{96,80},{112,96},{128,112},... | collective-permute-start | bytes 49160 | tf_op jit(solution)/shard_map/ppermute | solution.py:27
  92.9 8.0 %collective-permute-start.8 = (bf16[64,1,128]{2,0,1:T(8,128)(2,1)S(1)}, bf16[64,1,128]{2,0,1:T(8,128)(2,1)S(1)}, u32[]{:S(2)}, u32[]{:S(2)}) collective-permute-start(bf16[64,1,128]{2,0,1:T(8,128)(2,1)S(1)} %get-tuple-element.31), channel_id=1, source_target_pairs={{0,16},{16,32},{32,48},{48,64},{64,80},{80,96},{96,112},{112,128},... | collective-permute-start | bytes 49160 | tf_op jit(solution)/shard_map/ppermute | solution.py:24
  99.2 7.6 %copy-start.55 = (bf16[64,64,1]{1,0,2:T(8,128)(2,1)S(1)}, bf16[64,64,1]{1,0,2:T(8,128)(2,1)}, u32[]{:S(2)}) copy-start(bf16[64,64,1]{1,0,2:T(8,128)(2,1)} %reshape.222) | copy-start | bytes 24580
  101.0 6.0 %copy-start.56 = (bf16[64,64,1]{1,0,2:T(8,128)(2,1)S(1)}, bf16[64,64,1]{1,0,2:T(8,128)(2,1)}, u32[]{:S(2)}) copy-start(bf16[64,64,1]{1,0,2:T(8,128)(2,1)} %reshape.228) | copy-start | bytes 24580
  101.3 8.9 %collective-permute-start.10 = (bf16[64,26,1]{2,0,1:T(8,128)(2,1)S(1)}, bf16[64,26,1]{2,0,1:T(8,128)(2,1)S(1)}, u32[]{:S(2)}, u32[]{:S(2)}) collective-permute-start(bf16[64,26,1]{2,0,1:T(8,128)(2,1)S(1)} %get-tuple-element.19), channel_id=1, source_target_pairs={{4,0},{8,4},{12,8},{5,1},{9,5},{13,9},{6,2},{10,6},{14,10},{7,3},{... | collective-permute-start | bytes 9992 | tf_op jit(solution)/shard_map/ppermute | solution.py:27
  102.6 9.0 %collective-permute-start.11 = (bf16[64,26,1]{2,0,1:T(8,128)(2,1)S(1)}, bf16[64,26,1]{2,0,1:T(8,128)(2,1)S(1)}, u32[]{:S(2)}, u32[]{:S(2)}) collective-permute-start(bf16[64,26,1]{2,0,1:T(8,128)(2,1)S(1)} %get-tuple-element.20), channel_id=1, source_target_pairs={{0,4},{4,8},{8,12},{1,5},{5,9},{9,13},{2,6},{6,10},{10,14},{3,7},{... | collective-permute-start | bytes 9992 | tf_op jit(solution)/shard_map/ppermute | solution.py:24
  107.3 5.3 %copy-start.54 = (bf16[64,64,1]{1,0,2:T(8,128)(2,1)S(1)}, bf16[64,64,1]{1,0,2:T(8,128)(2,1)}, u32[]{:S(2)}) copy-start(bf16[64,64,1]{1,0,2:T(8,128)(2,1)} %reshape.227) | copy-start | bytes 24580
  122.8 7.6 %copy-start.18 = (f32[9,64,64]{2,1,0:T(8,128)}, f32[9,64,64]{2,1,0:T(8,128)S(1)}, u32[]{:S(2)}) copy-start(f32[9,64,64]{2,1,0:T(8,128)S(1)} %fusion.61) | copy-start | bytes 442372
  122.9 9.9 %collective-permute-start.13 = (bf16[64,1,128]{2,0,1:T(8,128)(2,1)}, bf16[64,1,128]{2,0,1:T(8,128)(2,1)S(1)}, u32[]{:S(2)}, u32[]{:S(2)}) collective-permute-start(bf16[64,1,128]{2,0,1:T(8,128)(2,1)} %get-tuple-element.30), channel_id=1, source_target_pairs={{16,0},{32,16},{48,32},{64,48},{80,64},{96,80},{112,96},{128,112},... | collective-permute-start | bytes 49160 | tf_op jit(solution)/shard_map/ppermute | solution.py:27
  124.2 8.6 %collective-permute-start.12 = (bf16[64,1,128]{2,0,1:T(8,128)(2,1)}, bf16[64,1,128]{2,0,1:T(8,128)(2,1)S(1)}, u32[]{:S(2)}, u32[]{:S(2)}) collective-permute-start(bf16[64,1,128]{2,0,1:T(8,128)(2,1)} %get-tuple-element.29), channel_id=1, source_target_pairs={{0,16},{16,32},{32,48},{48,64},{64,80},{80,96},{96,112},{112,128},... | collective-permute-start | bytes 49160 | tf_op jit(solution)/shard_map/ppermute | solution.py:24
  130.9 8.2 %copy-start.49 = (bf16[64,64,1]{1,0,2:T(8,128)(2,1)S(1)}, bf16[64,64,1]{1,0,2:T(8,128)(2,1)}, u32[]{:S(2)}) copy-start(bf16[64,64,1]{1,0,2:T(8,128)(2,1)} %reshape.232) | copy-start | bytes 24580
  132.8 6.5 %copy-start.50 = (bf16[64,64,1]{1,0,2:T(8,128)(2,1)S(1)}, bf16[64,64,1]{1,0,2:T(8,128)(2,1)}, u32[]{:S(2)}) copy-start(bf16[64,64,1]{1,0,2:T(8,128)(2,1)} %reshape.238) | copy-start | bytes 24580
  133.0 9.6 %collective-permute-start.14 = (bf16[64,26,1]{2,0,1:T(8,128)(2,1)S(1)}, bf16[64,26,1]{2,0,1:T(8,128)(2,1)S(1)}, u32[]{:S(2)}, u32[]{:S(2)}) collective-permute-start(bf16[64,26,1]{2,0,1:T(8,128)(2,1)S(1)} %get-tuple-element.15), channel_id=1, source_target_pairs={{4,0},{8,4},{12,8},{5,1},{9,5},{13,9},{6,2},{10,6},{14,10},{7,3},{... | collective-permute-start | bytes 9992 | tf_op jit(solution)/shard_map/ppermute | solution.py:27
  134.3 9.8 %collective-permute-start.15 = (bf16[64,26,1]{2,0,1:T(8,128)(2,1)S(1)}, bf16[64,26,1]{2,0,1:T(8,128)(2,1)S(1)}, u32[]{:S(2)}, u32[]{:S(2)}) collective-permute-start(bf16[64,26,1]{2,0,1:T(8,128)(2,1)S(1)} %get-tuple-element.16), channel_id=1, source_target_pairs={{0,4},{4,8},{8,12},{1,5},{5,9},{9,13},{2,6},{6,10},{10,14},{3,7},{... | collective-permute-start | bytes 9992 | tf_op jit(solution)/shard_map/ppermute | solution.py:24
  140.5 4.3 copy-start.45
  140.5 4.6 copy-start.48
  151.8 268.4 %copy-start.60 = (f32[552]{0:T(1024)S(1)}, f32[552]{0:T(1024)}, u32[]{:S(2)}) copy-start(f32[552]{0:T(1024)} %param.7) | copy-start | bytes 6628
  151.8 346.7 %copy-start.17 = (f32[141312]{0:T(1024)S(1)}, f32[141312]{0:T(1024)}, u32[]{:S(2)}) copy-start(f32[141312]{0:T(1024)} %param.6) | copy-start | bytes 1695748
  (32 other events, 57.0 us)
Sparse Core Ops, SparseCore 0:
  153.1 266.9 all-reduce.2
where the time goes:
time: 510 us; the launch traced here: 508 us
  waiting for transfers between devices  293 us (57%)
  blocking collectives  75.6 us (15%)
  starting transfers between devices  43.3 us (8%)
  matrix products  36.9 us (7%)
  local copies, waits for them, and re-layouts  30.3 us (6%)
  between operations  17.9 us (4%)
  other arithmetic  10.4 us (2%)
    psum x1, waiting for transfers between devices, local(): total = lax.psum(flat, ('row', 'col', 'dp'))  267 us
    psum x1, blocking collectives, local(): lax.psum((jnp.sum(jnp.abs(mixed)), loss_part), ('row', 'col', 'dp'))  75.6 us
    ppermute x8, starting transfers between devices, extended(): lax.ppermute(lax.slice_in_dim(block, block.shape[dim] - width, None, axis...  32.8 us
    ppermute x8, waiting for transfers between devices, extended(): lax.ppermute(lax.slice_in_dim(block, 0, width, axis=dim), axis, backward)  15.5 us
    ppermute x8, waiting for transfers between devices, extended(): lax.ppermute(lax.slice_in_dim(block, block.shape[dim] - width, None, axis...  10.6 us
    ppermute x8, starting transfers between devices, extended(): lax.ppermute(lax.slice_in_dim(block, 0, width, axis=dim), axis, backward)  10.5 us
    squeeze x32, local copies, waits for them, and re-layouts, conv_taps(): w_mid[position]  10.4 us
    dot_general x17, matrix products, local(): jnp.einsum('io,ohw->ihw', w_mid[position], spread_back[:, shift_row:shift...  10.4 us
  transfers between devices with their start and end apart: 17, of which 10 were waited for; matrix products, arithmetic and copies ran while one was open for 6% of the time, Pallas kernels for 0%

commit v1 on v0

v1 whole, which is shorter than its diff:
```python
import numpy as np
import jax
import jax.numpy as jnp
from jax import lax
from jax.experimental import pallas as pl
from jax.experimental.pallas import tpu as pltpu
from jax.sharding import PartitionSpec as P

C = 256
MID = 64
CLASSES = 8
TILE_ROWS = 24
TILE_COLS = 64
NTILES = 512
PARAM = 141312
SHARE = 552

HALO = 2
ROWS = TILE_ROWS + 2 * HALO
COLS = 2 * TILE_COLS + 2 * HALO
PIX = ROWS * COLS
LANES = 3840
GUARD = 256
WIDE = LANES + 2 * GUARD
CHUNK = 768

BF = jnp.bfloat16
F32 = jnp.float32

RINGS = {
    "y": ("row", 16, 4, 1),
    "z": ("row", 16, 4, 4),
    "x": ("col", 4, 4, 1),
    "core": ("dp", 4, 2, 1),
    "far": ("dp", 4, 2, 2),
}


def rotation(ring, step):
    _, size, group, stride = RINGS[ring]
    pairs = []
    for source in range(size):
        place = (source // stride) % group
        pairs.append((source, source + (((place + step) % group) - place) * stride))
    return pairs


def place_in(ring):
    axis, _, group, stride = RINGS[ring]
    return (lax.axis_index(axis) // stride) % group


def paired_sum(own, got):
    if len(got) == 1:
        return own + got[0]
    return (own + got[1]) + (got[0] + got[2])


def ring_sum(value, ring):
    axis, _, group, _ = RINGS[ring]
    got = [lax.ppermute(value, axis, rotation(ring, k)) for k in range(1, group)]
    return paired_sum(value, got)


def ring_scatter(value, ring):
    axis, _, group, _ = RINGS[ring]
    place = place_in(ring)
    got = [
        lax.ppermute(
            lax.dynamic_index_in_dim(value, (place + k) % group, 0, keepdims=False),
            axis,
            rotation(ring, k),
        )
        for k in range(1, group)
    ]
    own = lax.dynamic_index_in_dim(value, place, 0, keepdims=False)
    return paired_sum(own, got)


def unpack(weights):
    offset = 0
    blocks_list = []
    for number in range(2):
        w_in = weights[offset : offset + C * MID].reshape(C, MID)
        offset = offset + C * MID
        w_mid = weights[offset : offset + 9 * MID * MID].reshape(3, 3, MID, MID)
        offset = offset + 9 * MID * MID
        w_out = weights[offset : offset + MID * C].reshape(MID, C)
        offset = offset + MID * C
        blocks_list.append((w_in.astype(BF), w_mid.astype(BF), w_out.astype(BF)))
    head = weights[offset:].reshape(C, CLASSES)
    return (blocks_list, head)


def nn(left, right):
    return lax.dot_general(left, right, (((1,), (0,)), ((), ())), preferred_element_type=F32)


def nt(left, right):
    return lax.dot_general(left, right, (((1,), (1,)), ((), ())), preferred_element_type=F32)


CHUNKS = [(start, CHUNK) for start in range(0, LANES, CHUNK)]


def shifted(ref, rows, start, size, shift):
    first = GUARD + start + shift
    low = first // 128 * 128
    high = -(-(first + size) // 128) * 128
    return ref[rows, low:high][:, first - low : first - low + size]


def kernel(
    labels,
    x_ref,
    mask_ref,
    win_t1,
    wf1,
    wb1,
    wout_t1,
    wout1,
    win_t2,
    wf2,
    wb2,
    wout_t2,
    wout2,
    win2,
    head_ref,
    flat_ref,
    loss_ref,
    h1a,
    h1b,
    hs1,
    hs2,
    wide,
    h2a,
    h2b,
    y1,
    y2,
    dg2,
    ds,
    dg1,
    dz,
    tall,
):
    everything = slice(None)
    for ref in (h1a, h1b, dg2, wide):
        ref[:, :GUARD] = jnp.zeros((ref.shape[0], GUARD), ref.dtype)
        ref[:, GUARD + LANES :] = jnp.zeros((ref.shape[0], GUARD), ref.dtype)

    def forward(inputs, win_t, wf, wout_t, h1, hs, h2, output, masked):
        for start, size in CHUNKS:
            lanes = slice(start, start + size)
            value = jnp.maximum(nn(win_t[...], inputs[:, lanes]), 0.0)
            if masked:
                value = value * mask_ref[2:3, lanes]
            h1[:, GUARD + start : GUARD + start + size] = value.astype(BF)
        for start, size in CHUNKS:
            lanes = slice(start, start + size)
            for s in range(3):
                hs[s * MID : (s + 1) * MID, lanes] = shifted(h1, everything, start, size, s - 1)
            wide[:, GUARD + start : GUARD + start + size] = nn(wf[...], hs[:, lanes])
        for start, size in CHUNKS:
            lanes = slice(start, start + size)
            total = sum(
                shifted(wide, slice(r * MID, (r + 1) * MID), start, size, (r - 1) * COLS)
                for r in range(3)
            )
            value = jnp.maximum(total, 0.0).astype(BF)
            h2[:, lanes] = value
            output[:, lanes] = jnp.maximum(
                nn(wout_t[...], value) + inputs[:, lanes].astype(F32), 0.0
            ).astype(BF)

    forward(x_ref, win_t1, wf1, wout_t1, h1a, hs1, h2a, y1, False)
    forward(y1, win_t2, wf2, wout_t2, h1b, hs2, h2b, y2, True)

    tile_masks = mask_ref[0:8, :]
    pooled = nt(y2[...], tile_masks.astype(BF)) * (1.0 / (TILE_ROWS * TILE_COLS))
    head = head_ref[...]
    classes = lax.broadcasted_iota(jnp.int32, (1, CLASSES), 1)
    loss = jnp.zeros((1, 1), F32)
    grad_head = jnp.zeros((C, CLASSES), F32)
    spread = []
    for tile in range(2):
        column = pooled[:, tile : tile + 1]
        logits = jnp.sum(column * head, axis=0, keepdims=True)
        highest = jnp.max(logits, axis=1, keepdims=True)
        logsum = jnp.log(jnp.sum(jnp.exp(logits - highest), axis=1, keepdims=True)) + highest
        onehot = (classes == labels[tile]).astype(F32)
        loss = loss + logsum - jnp.sum(onehot * logits, axis=1, keepdims=True)
        dlogits = (jnp.exp(logits - logsum) - onehot) * (1.0 / NTILES)
        grad_head = grad_head + column * dlogits
        dpooled = jnp.sum(head * dlogits, axis=1, keepdims=True) / (TILE_ROWS * TILE_COLS)
        spread.append(dpooled.astype(BF).astype(F32))
    loss_ref[...] = jnp.broadcast_to(loss, (8, 128))

    for start, size in CHUNKS:
        lanes = slice(start, start + size)
        upstream = spread[0] * mask_ref[0:1, lanes] + spread[1] * mask_ref[1:2, lanes]
        dz[:, lanes] = jnp.where(y2[:, lanes].astype(F32) > 0, upstream, 0.0).astype(BF)

    def pack_tall(value, row):
        count = value.shape[0]
        tall[0:count, :] = value
        half = count // 2
        flat_ref[row : row + half, 0:MID] = tall[pl.ds(0, half, stride=2), :]
        flat_ref[row : row + half, MID:] = tall[pl.ds(1, half, stride=2), :]

    def backward(inputs, wb, wout, h1, hs, h2, row, then):
        grad_out = nt(h2[...], dz[...])
        flat_ref[pl.ds(row + 416, MID, stride=2), :] = grad_out[:, :128]
        flat_ref[pl.ds(row + 417, MID, stride=2), :] = grad_out[:, 128:]
        for start, size in CHUNKS:
            lanes = slice(start, start + size)
            value = nn(wout[...], dz[:, lanes])
            value = jnp.where(h2[:, lanes].astype(F32) > 0, value, 0.0)
            dg2[:, GUARD + start : GUARD + start + size] = value.astype(BF)
        for start, size in CHUNKS:
            lanes = slice(start, start + size)
            for r in range(3):
                ds[r * MID : (r + 1) * MID, lanes] = shifted(
                    dg2, everything, start, size, (1 - r) * COLS
                )
            wide[:, GUARD + start : GUARD + start + size] = nn(wb[...], ds[:, lanes])
        grad_mid = nt(hs[...], ds[...])
        for r in range(3):
            pack_tall(grad_mid[:, r * MID : (r + 1) * MID], row + 128 + r * 96)
        for start, size in CHUNKS:
            lanes = slice(start, start + size)
            total = sum(
                shifted(wide, slice(s * MID, (s + 1) * MID), start, size, 1 - s) for s in range(3)
            )
            kept = h1[:, GUARD + start : GUARD + start + size].astype(F32) > 0
            value = jnp.where(kept, total, 0.0).astype(BF)
            dg1[:, lanes] = value
            if then is not None:
                then(lanes, value)
        pack_tall(nt(inputs[...], dg1[...]), row)

    def to_first(lanes, value):
        total = nn(win2[...], value) + dz[:, lanes].astype(F32)
        dz[:, lanes] = jnp.where(y1[:, lanes].astype(F32) > 0, total, 0.0).astype(BF)

    backward(y1, wb2, wout2, h1b, hs2, h2b, 544, to_first)
    backward(x_ref, wb1, wout1, h1a, hs1, h2a, 0, None)
    tall[:, 0:CLASSES] = grad_head
    for j in range(16):
        flat_ref[1088:1104, j * CLASSES : (j + 1) * CLASSES] = tall[
            pl.ds(j, 16, stride=16), 0:CLASSES
        ]


def compute(labels, x_flat, masks, blocks_list, head):
    (win1, wmid1, wout1), (win2, wmid2, wout2) = blocks_list
    wf = [w.transpose(0, 3, 1, 2).reshape(3 * MID, 3 * MID) for w in (wmid1, wmid2)]
    wb = [w.transpose(1, 2, 0, 3).reshape(3 * MID, 3 * MID) for w in (wmid1, wmid2)]
    vmem = pl.BlockSpec(memory_space=pltpu.VMEM)
    smem = pl.BlockSpec(memory_space=pltpu.SMEM)
    return pl.pallas_call(
        kernel,
        out_shape=(
            jax.ShapeDtypeStruct((PARAM // 128, 128), F32),
            jax.ShapeDtypeStruct((8, 128), F32),
        ),
        in_specs=[smem] + [vmem] * 14,
        out_specs=(vmem, vmem),
        scratch_shapes=[
            pltpu.VMEM((MID, WIDE), BF),
            pltpu.VMEM((MID, WIDE), BF),
            pltpu.VMEM((3 * MID, LANES), BF),
            pltpu.VMEM((3 * MID, LANES), BF),
            pltpu.VMEM((3 * MID, WIDE), F32),
            pltpu.VMEM((MID, LANES), BF),
            pltpu.VMEM((MID, LANES), BF),
            pltpu.VMEM((C, LANES), BF),
            pltpu.VMEM((C, LANES), BF),
            pltpu.VMEM((MID, WIDE), BF),
            pltpu.VMEM((3 * MID, LANES), BF),
            pltpu.VMEM((MID, LANES), BF),
            pltpu.VMEM((C, LANES), BF),
            pltpu.VMEM((C, MID), F32),
        ],
        compiler_params=pltpu.CompilerParams(vmem_limit_bytes=48 * 1024 * 1024),
    )(
        labels,
        x_flat,
        masks,
        win1.T,
        wf[0],
        wb[0],
        wout1.T,
        wout1,
        win2.T,
        wf[1],
        wb[1],
        wout2.T,
        wout2,
        win2,
        head,
    )


def neighbours(low_part, high_part, axis):
    count = lax.axis_size(axis)
    up = [(i, i + 1) for i in range(count - 1)]
    down = [(target, source) for source, target in up]
    return lax.ppermute(high_part, axis, up), lax.ppermute(low_part, axis, down)


def extended(inputs):
    height, width = inputs.shape[1:]
    left, right = neighbours(
        inputs[:, :, :HALO].reshape(C, -1), inputs[:, :, width - HALO :].reshape(C, -1), "col"
    )
    wide = jnp.concatenate(
        [left.reshape(C, height, HALO), inputs, right.reshape(C, height, HALO)], axis=2
    )
    top, bottom = neighbours(
        wide[:, :HALO].reshape(C, -1), wide[:, height - HALO :].reshape(C, -1), "row"
    )
    body = wide.reshape(C, -1)
    return jnp.concatenate([top, body, bottom, jnp.zeros((C, LANES - PIX), BF)], axis=1)


def make_masks():
    pixel = np.arange(LANES)
    r, c = pixel // COLS - HALO, pixel % COLS - HALO
    inside = (pixel < PIX) & (r >= 0) & (r < TILE_ROWS)
    tiles = [inside & (c >= t * TILE_COLS) & (c < (t + 1) * TILE_COLS) for t in range(2)]
    near = (pixel < PIX) & (r >= -1) & (r <= TILE_ROWS) & (c >= -1) & (c <= 2 * TILE_COLS)
    row, col = lax.axis_index("row"), lax.axis_index("col")
    rows, cols = lax.axis_size("row"), lax.axis_size("col")
    image = (
        jnp.asarray(near)
        & (jnp.asarray(r >= 0) | (row > 0))
        & (jnp.asarray(r < TILE_ROWS) | (row < rows - 1))
        & (jnp.asarray(c >= 0) | (col > 0))
        & (jnp.asarray(c < 2 * TILE_COLS) | (col < cols - 1))
    )
    lines = [jnp.asarray(tiles[0], F32), jnp.asarray(tiles[1], F32), image.astype(F32)]
    return jnp.stack(lines + [jnp.zeros((LANES,), F32)] * 5)


def local(image, labels, weights, momentum):
    blocks_list, head = unpack(weights)
    flat, loss_part = compute(
        labels.reshape(2), extended(image[0]), make_masks(), blocks_list, head
    )

    parts = flat.reshape(16, 4, 2, 2, SHARE).transpose(3, 1, 2, 0, 4)
    loss_column = jnp.broadcast_to(loss_part[0, 0], (2, 4, 2, 16, 1))
    parts = jnp.concatenate([parts, loss_column], axis=-1).reshape(2, 4, 32, SHARE + 1)
    parts = ring_scatter(ring_scatter(parts, "core"), "x")
    mine = place_in("far") * 16 + lax.axis_index("row")
    at_home = (jnp.arange(32) == mine)[:, None]
    parts = parts + jnp.where(at_home, 9.0 * jnp.pad(momentum, (0, 1))[None], 0.0)
    for ring in ("y", "z", "far"):
        parts = ring_sum(parts, ring)
    magnitude = jnp.full((8, 128), jnp.sum(jnp.abs(parts[:, :SHARE])))
    for ring in ("core", "x"):
        magnitude = ring_sum(magnitude, ring)
    scale_tau = 0.1 * magnitude[0, 0] / PARAM + 1e-06
    own = lax.dynamic_index_in_dim(parts, mine, 0, keepdims=False)
    loss = own[SHARE] / NTILES
    own = own[:SHARE]
    mixed = 0.1 * own
    update = mixed / (jnp.abs(mixed) + scale_tau)
    start = (lax.axis_index("row") * 16 + lax.axis_index("col") * 4 + lax.axis_index("dp")) * SHARE
    weight_share = lax.dynamic_slice_in_dim(weights, start, SHARE, 0)
    new_weights = weight_share - 0.0001 * (update + 0.1 * weight_share)
    new_momentum = 0.9 * momentum + 0.01 * own
    return (new_weights, new_momentum, update, loss)


def solution(mesh):
    in_specs = (P("dp", None, "row", "col"), P("dp", "row", "col"), P(), P(("row", "col", "dp")))
    out_specs = (P(("row", "col", "dp")), P(("row", "col", "dp")), P(("row", "col", "dp")), P())
    return jax.shard_map(local, mesh=mesh, in_specs=in_specs, out_specs=out_specs, check_vma=False)
```

time: 510 us -> 113 us (0.22)
  waiting for transfers between devices: 293 us -> 18.7 us
  blocking collectives: 75.6 us -> 0 us
  matrix products: 36.9 us -> 0 us
  between operations: 17.9 us -> 3.69 us
  Pallas kernels: 0 us -> 13.7 us
    psum x1 -> x0, waiting for transfers between devices: 267 us -> none  [local(): total = lax.psum(flat, ('row', 'col', 'dp'))]
    psum x1 -> x0, blocking collectives: 75.6 us -> none  [local(): lax.psum((jnp.sum(jnp.abs(mixed)), loss_part), ('row', 'col', 'dp'))]
    dot_general x67 -> x0, matrix products: 36.9 us -> none  [the longest x17 10.4 us: local(): jnp.einsum('io,ohw->ihw', w_mid[position], spread_back[:, shift_row:shift...]
    squeeze x37 -> x2, local copies, waits for them, and re-layouts: 14.1 us -> 0.06 us  [ring_scatter(): lax.dynamic_index_in_dim(value, (place + k) % group, 0, keepdims=False)]
    pallas_call x0 -> x1, Pallas kernels: none -> 13.7 us  [compute(): pl.pallas_call(kernel, out_shape=(jax.ShapeDtypeStruct((PARAM // 128, 128...]
    ppermute x16 -> x19, waiting for transfers between devices: 26.2 us -> 18.7 us  [the longest x11 15.6 us: ring_sum(): lax.ppermute(value, axis, rotation(ring, k))]
    reshape x5 -> x15, local copies, waits for them, and re-layouts: 3 us -> 10.3 us  [the longest x1 5.31 us: extended(): body = wide.reshape(C, -1)]
    ppermute x16 -> x19, starting transfers between devices: 43.3 us -> 43.6 us  [the longest x11 24.6 us: ring_sum(): lax.ppermute(value, axis, rotation(ring, k))]
  transfers between devices with their start and end apart: 17 -> 19, of which waited for: 10 -> 9; matrix products, arithmetic and copies ran while one was open for 6% -> 9% of each run, Pallas kernels for 0% -> 0%
where the time goes in v1:
time: 113 us; the launch traced here: 112 us
  starting transfers between devices  43.6 us (39%)
  local copies, waits for them, and re-layouts  26.4 us (23%)
  waiting for transfers between devices  18.7 us (17%)
  Pallas kernels  13.7 us (12%)
  other arithmetic  6.01 us (5%)
  between operations  3.69 us (3%)
    ppermute x11, starting transfers between devices, ring_sum(): lax.ppermute(value, axis, rotation(ring, k))  24.6 us
    ppermute x11, waiting for transfers between devices, ring_sum(): lax.ppermute(value, axis, rotation(ring, k))  15.6 us
    pallas_call x1, Pallas kernels, compute(): pl.pallas_call(kernel, out_shape=(jax.ShapeDtypeStruct((PARAM // 128, 128...  13.7 us
    ppermute x4, starting transfers between devices, ring_scatter(): lax.ppermute(lax.dynamic_index_in_dim(value, (place + k) % group, 0, keep...  8.27 us
    ppermute x2, starting transfers between devices, neighbours(): lax.ppermute(high_part, axis, up)  8.03 us
    reshape x1, local copies, waits for them, and re-layouts, extended(): body = wide.reshape(C, -1)  5.31 us
    slice x2, local copies, waits for them, and re-layouts, extended(): inputs[:, :, width - HALO:].reshape(C, -1)  3.65 us
    concatenate x1, local copies, waits for them, and re-layouts, extended(): jnp.concatenate([top, body, bottom, jnp.zeros((C, LANES - PIX), BF)], axi...  3.35 us
  transfers between devices with their start and end apart: 19, of which 9 were waited for; matrix products, arithmetic and copies ran while one was open for 9% of the time, Pallas kernels for 0%

profile of v1, /device:TPU:1, one launch (start us, length us, event | category | flops | bytes accessed | tf_op | source)
XLA Modules:
  0.0 112.1 jit_solution(17850134531498806091)
XLA Ops:
  0.6 2.7 %fusion.4 = (bf16[256,24,2]{2,1,0:T(8,128)(2,1)S(1)}, bf16[256,24,2]{2,1,0:T(8,128)(2,1)S(1)}) fusion(bf16[256,24,128]{2,1,0:T(8,128)(2,1)} %bitcast.46), kind=kLoop, calls=%fused_computation.26 | loop fusion | bytes 98304 | tf_op jit(solution)/shard_map/slice | solution.py:314
  3.3 1.0 copy.21
  4.3 1.4 %collective-permute-start.1 = (bf16[256,48]{0,1:T(8,128)(2,1)S(1)}, bf16[256,48]{0,1:T(8,128)(2,1)S(1)}, u32[]{:S(2)}, u32[]{:S(2)}) collective-permute-start(bf16[256,48]{0,1:T(8,128)(2,1)S(1)} %reshape.125), channel_id=1, source_target_pairs={{4,0},{8,4},{12,8},{5,1},{9,5},{13,9},{6,2},{10,6},{14,10},{7,3},{... | collective-permute-start | bytes 73736 | tf_op jit(solution)/shard_map/ppermute | solution.py:308
  5.8 1.0 copy.20
  6.7 4.6 %collective-permute-start = (bf16[256,48]{0,1:T(8,128)(2,1)S(1)}, bf16[256,48]{0,1:T(8,128)(2,1)S(1)}, u32[]{:S(2)}, u32[]{:S(2)}) collective-permute-start(bf16[256,48]{0,1:T(8,128)(2,1)S(1)} %reshape.123), channel_id=1, source_target_pairs={{0,4},{4,8},{8,12},{1,5},{5,9},{9,13},{2,6},{6,10},{10,14},{3,7},{... | collective-permute-start | bytes 73736 | tf_op jit(solution)/shard_map/ppermute | solution.py:308
  11.5 1.0 copy.23
  12.5 1.8 %copy.22 = bf16[256,24,2]{2,1,0:T(8,128)(2,1)} copy(bf16[256,24,2]{0,2,1:T(2,128)(2,1)S(1)} %reshape.124) | data formatting | bytes 49152 | tf_op jit(solution)/shard_map/reshape | solution.py:317
  14.3 3.1 %pad_maximum_fusion = bf16[256,24,132]{2,1,0:T(8,128)(2,1)S(1)} fusion(bf16[256,24,2]{2,1,0:T(8,128)(2,1)S(1)} %copy.23, bf16[256,24,128]{2,1,0:T(8,128)(2,1)S(1)} %bitcast.47, bf16[256,24,2]{2,1,0:T(8,128)(2,1)} %copy.22), kind=kLoop, calls=%fused_computation | loop fusion | flops 4866048 | bytes 3244032 | tf_op jit(solution)/shard_map/concatenate | solution.py:316
  17.5 1.6 %copy-done.1 = bf16[256,24,132]{2,1,0:T(8,128)(2,1)} copy-done((bf16[256,24,132]{2,1,0:T(8,128)(2,1)}, bf16[256,24,132]{2,1,0:T(8,128)(2,1)S(1)}, u32[]{:S(2)}) %copy-start.1) | copy-done | bytes 1622040
  19.7 3.5 %collective-permute-start.2 = (bf16[256,264]{1,0:T(8,128)(2,1)S(1)}, bf16[256,264]{1,0:T(8,128)(2,1)S(1)}, u32[]{:S(2)}, u32[]{:S(2)}) collective-permute-start(bf16[256,264]{1,0:T(8,128)(2,1)S(1)} %reshape.137), channel_id=1, source_target_pairs={{0,16},{16,32},{32,48},{48,64},{64,80},{80,96},{96,112},{112,128},... | collective-permute-start | bytes 405512 | tf_op jit(solution)/shard_map/ppermute | solution.py:308
  23.3 1.3 %collective-permute-start.3 = (bf16[256,264]{1,0:T(8,128)(2,1)S(1)}, bf16[256,264]{1,0:T(8,128)(2,1)S(1)}, u32[]{:S(2)}, u32[]{:S(2)}) collective-permute-start(bf16[256,264]{1,0:T(8,128)(2,1)S(1)} %reshape.139), channel_id=1, source_target_pairs={{16,0},{32,16},{48,32},{64,48},{80,64},{96,80},{112,96},{128,112},... | collective-permute-start | bytes 405512 | tf_op jit(solution)/shard_map/ppermute | solution.py:308
  27.2 5.3 %reshape.138 = bf16[256,3168]{1,0:T(8,128)(2,1)} reshape(bf16[256,24,132]{2,1,0:T(8,128)(2,1)} %copy-done.1) | data formatting | bytes 3244032 | tf_op jit(solution)/shard_map/reshape | solution.py:322
  32.5 0.7 copy-done.5
  33.2 0.7 copy-done.6
  33.9 3.3 %concatenate.10.x_ref = bf16[256,3840]{1,0:T(8,128)(2,1)S(1)} concatenate(bf16[256,264]{1,0:T(8,128)(2,1)} %copy-done.5, bf16[256,3168]{1,0:T(8,128)(2,1)} %reshape.138, bf16[256,264]{1,0:T(8,128)(2,1)} %copy-done.6, bf16[256,144]{1,0:T(8,128)(2,1)S(1)} %broadcast_in_dim.29), dimensions={1} | concatenate | bytes 3932160 | tf_op jit(solution)/shard_map/concatenate | solution.py:323
  37.3 13.7 %shard_map.138 = (f32[1104,128]{1,0:T(8,128)S(1)}, f32[8,128]{1,0:T(8,128)S(1)}) custom-call(s32[2]{0:T(128)S(1)} %bitcast.45, bf16[256,3840]{1,0:T(8,128)(2,1)S(1)} %concatenate.10.x_ref, f32[8,3840]{1,0:T(8,128)S(1)} %stack.23.mask_ref, bf16[64,256]{1,0:T(8,128)(2,1)S(1)} %bitcast.43, bf16[192,192]{1,0:T(8,128)(2,1)S(1)} %reshape.130.wf1, ...), custom_call_target="tpu_custom_call" | custom-call | tf_op jit(solution)/shard_map/pallas_call | solution.py:260
  51.0 1.0 reshape.134
  52.2 0.5 slice.110
  52.7 0.7 concatenate.11
  53.5 1.9 %collective-permute-start.4 = (f32[4,32,553]{2,1,0:T(8,128)S(1)}, f32[4,32,553]{2,1,0:T(8,128)S(1)}, u32[]{:S(2)}, u32[]{:S(2)}) collective-permute-start(f32[4,32,553]{2,1,0:T(8,128)S(1)} %dynamic-slice_bitcast_fusion), channel_id=1, source_target_pairs={{0,1},{1,0},{2,3},{3,2},{4,5},{5,4},{6,7},{7,6},{8,9},{9,8},{10,11... | collective-permute-start | bytes 849416 | tf_op jit(solution)/shard_map/ppermute | solution.py:69
  55.4 1.2 %collective-permute-done.4 = f32[4,32,553]{2,1,0:T(8,128)S(1)} collective-permute-done((f32[4,32,553]{2,1,0:T(8,128)S(1)}, f32[4,32,553]{2,1,0:T(8,128)S(1)}, u32[]{:S(2)}, u32[]{:S(2)}) %collective-permute-start.4) | collective-permute-done | bytes 283168 | tf_op jit(solution)/shard_map/ppermute | solution.py:69
  56.8 3.6 %collective-permute-start.5 = (f32[32,553]{1,0:T(8,128)S(1)}, f32[32,553]{1,0:T(8,128)S(1)}, u32[]{:S(2)}, u32[]{:S(2)}) collective-permute-start(f32[32,553]{1,0:T(8,128)S(1)} %get-tuple-element.18), channel_id=1, source_target_pairs={{0,8},{4,12},{8,0},{12,4},{1,9},{5,13},{9,1},{13,5},{2,10},{6,14},... | collective-permute-start | bytes 212360 | tf_op jit(solution)/shard_map/ppermute | solution.py:69
  60.4 0.6 collective-permute-start.6
  61.0 2.1 %collective-permute-start.7 = (f32[32,553]{1,0:T(8,128)S(1)}, f32[32,553]{1,0:T(8,128)S(1)}, u32[]{:S(2)}, u32[]{:S(2)}) collective-permute-start(f32[32,553]{1,0:T(8,128)S(1)} %get-tuple-element.16), channel_id=1, source_target_pairs={{0,12},{4,0},{8,4},{12,8},{1,13},{5,1},{9,5},{13,9},{2,14},{6,2},{... | collective-permute-start | bytes 212360 | tf_op jit(solution)/shard_map/ppermute | solution.py:69
  63.1 1.8 %collective-permute-done.6 = f32[32,553]{1,0:T(8,128)S(1)} collective-permute-done((f32[32,553]{1,0:T(8,128)S(1)}, f32[32,553]{1,0:T(8,128)S(1)}, u32[]{:S(2)}, u32[]{:S(2)}) %collective-permute-start.6) | collective-permute-done | bytes 70816 | tf_op jit(solution)/shard_map/ppermute | solution.py:69
  65.0 2.4 %collective-permute-start.9 = (f32[32,553]{1,0:T(8,128)S(1)}, f32[32,553]{1,0:T(8,128)S(1)}, u32[]{:S(2)}, u32[]{:S(2)}) collective-permute-start(f32[32,553]{1,0:T(8,128)S(1)} %fusion.2), channel_id=1, source_target_pairs={{0,16},{16,32},{32,48},{48,0},{64,80},{80,96},{96,112},{112,64},{1... | collective-permute-start | bytes 212360 | tf_op jit(solution)/shard_map/ppermute | solution.py:61
  67.4 1.5 %collective-permute-start.10 = (f32[32,553]{1,0:T(8,128)S(1)}, f32[32,553]{1,0:T(8,128)S(1)}, u32[]{:S(2)}, u32[]{:S(2)}) collective-permute-start(f32[32,553]{1,0:T(8,128)S(1)} %fusion.2), channel_id=1, source_target_pairs={{0,48},{16,0},{32,16},{48,32},{64,112},{80,64},{96,80},{112,96},{1... | collective-permute-start | bytes 212360 | tf_op jit(solution)/shard_map/ppermute | solution.py:61
  68.9 1.6 %collective-permute-start.8 = (f32[32,553]{1,0:T(8,128)S(1)}, f32[32,553]{1,0:T(8,128)S(1)}, u32[]{:S(2)}, u32[]{:S(2)}) collective-permute-start(f32[32,553]{1,0:T(8,128)S(1)} %fusion.2), channel_id=1, source_target_pairs={{0,32},{16,48},{32,0},{48,16},{64,96},{80,112},{96,64},{112,80},{1... | collective-permute-start | bytes 212360 | tf_op jit(solution)/shard_map/ppermute | solution.py:61
  70.7 3.6 %collective-permute-done.8 = f32[32,553]{1,0:T(8,128)S(1)} collective-permute-done((f32[32,553]{1,0:T(8,128)S(1)}, f32[32,553]{1,0:T(8,128)S(1)}, u32[]{:S(2)}, u32[]{:S(2)}) %collective-permute-start.8) | collective-permute-done | bytes 70816 | tf_op jit(solution)/shard_map/ppermute | solution.py:61
  74.3 3.2 %collective-permute-start.12 = (f32[32,553]{1,0:T(8,128)S(1)}, f32[32,553]{1,0:T(8,128)S(1)}, u32[]{:S(2)}, u32[]{:S(2)}) collective-permute-start(f32[32,553]{1,0:T(8,128)S(1)} %add_add_fusion.1), channel_id=1, source_target_pairs={{0,64},{16,80},{32,96},{48,112},{64,128},{80,144},{96,160},{112,17... | collective-permute-start | bytes 212360 | tf_op jit(solution)/shard_map/ppermute | solution.py:61
  77.5 2.8 %collective-permute-start.13 = (f32[32,553]{1,0:T(8,128)S(1)}, f32[32,553]{1,0:T(8,128)S(1)}, u32[]{:S(2)}, u32[]{:S(2)}) collective-permute-start(f32[32,553]{1,0:T(8,128)S(1)} %add_add_fusion.1), channel_id=1, source_target_pairs={{0,192},{16,208},{32,224},{48,240},{64,0},{80,16},{96,32},{112,48}... | collective-permute-start | bytes 212360 | tf_op jit(solution)/shard_map/ppermute | solution.py:61
  80.5 1.6 %collective-permute-done.12 = f32[32,553]{1,0:T(8,128)S(1)} collective-permute-done((f32[32,553]{1,0:T(8,128)S(1)}, f32[32,553]{1,0:T(8,128)S(1)}, u32[]{:S(2)}, u32[]{:S(2)}) %collective-permute-start.12) | collective-permute-done | bytes 70816 | tf_op jit(solution)/shard_map/ppermute | solution.py:61
  82.1 4.5 %collective-permute-done.11 = f32[32,553]{1,0:T(8,128)S(1)} collective-permute-done((f32[32,553]{1,0:T(8,128)S(1)}, f32[32,553]{1,0:T(8,128)S(1)}, u32[]{:S(2)}, u32[]{:S(2)}) %collective-permute-start.11) | collective-permute-done | bytes 70816 | tf_op jit(solution)/shard_map/ppermute | solution.py:61
  86.6 4.0 %collective-permute-start.14 = (f32[32,553]{1,0:T(8,128)S(1)}, f32[32,553]{1,0:T(8,128)S(1)}, u32[]{:S(2)}, u32[]{:S(2)}) collective-permute-start(f32[32,553]{1,0:T(8,128)S(1)} %add_add_fusion), channel_id=1, source_target_pairs={{0,2},{1,3},{2,0},{3,1},{4,6},{5,7},{6,4},{7,5},{8,10},{9,11},{10,... | collective-permute-start | bytes 212360 | tf_op jit(solution)/shard_map/ppermute | solution.py:61
  90.7 3.3 %collective-permute-done.14 = f32[32,553]{1,0:T(8,128)S(1)} collective-permute-done((f32[32,553]{1,0:T(8,128)S(1)}, f32[32,553]{1,0:T(8,128)S(1)}, u32[]{:S(2)}, u32[]{:S(2)}) %collective-permute-start.14) | collective-permute-done | bytes 70816 | tf_op jit(solution)/shard_map/ppermute | solution.py:61
  93.9 0.6 fusion
  94.6 0.6 broadcast_in_dim.33
  95.2 4.7 %collective-permute-start.15 = (f32[8,128]{1,0:T(8,128)S(1)}, f32[8,128]{1,0:T(8,128)S(1)}, u32[]{:S(2)}, u32[]{:S(2)}) collective-permute-start(f32[8,128]{1,0:T(8,128)S(1)} %broadcast_in_dim.33), channel_id=1, source_target_pairs={{0,1},{1,0},{2,3},{3,2},{4,5},{5,4},{6,7},{7,6},{8,9},{9,8},{10,11... | collective-permute-start | bytes 12296 | tf_op jit(solution)/shard_map/ppermute | solution.py:61
  99.9 0.8 collective-permute-done.15
  100.7 0.6 broadcast_add_fusion
  101.4 0.9 collective-permute-start.17
  102.3 2.2 %collective-permute-start.18 = (f32[8,128]{1,0:T(8,128)S(1)}, f32[8,128]{1,0:T(8,128)S(1)}, u32[]{:S(2)}, u32[]{:S(2)}) collective-permute-start(f32[8,128]{1,0:T(8,128)S(1)} %broadcast_add_fusion), channel_id=1, source_target_pairs={{0,12},{4,0},{8,4},{12,8},{1,13},{5,1},{9,5},{13,9},{2,14},{6,2},{... | collective-permute-start | bytes 12296 | tf_op jit(solution)/shard_map/ppermute | solution.py:61
  104.5 1.1 collective-permute-start.16
  105.6 0.6 dynamic-slice.1
  106.9 1.6 %collective-permute-done.16 = f32[8,128]{1,0:T(8,128)S(1)} collective-permute-done((f32[8,128]{1,0:T(8,128)S(1)}, f32[8,128]{1,0:T(8,128)S(1)}, u32[]{:S(2)}, u32[]{:S(2)}) %collective-permute-start.16) | collective-permute-done | bytes 4128 | tf_op jit(solution)/shard_map/ppermute | solution.py:61
  108.5 0.7 add_add_fusion.2
  109.1 0.5 slice.113
  110.3 0.7 multiply_subtract_fusion
  (87 shorter events, 4.2 us)
Async XLA Ops:
  4.3 7.0 %copy-start.3 = (f32[141312]{0:T(1024)S(1)}, f32[141312]{0:T(1024)}, u32[]{:S(2)}) copy-start(f32[141312]{0:T(1024)} %param.13) | copy-start | bytes 1695748
  4.3 7.1 %collective-permute-start.1 = (bf16[256,48]{0,1:T(8,128)(2,1)S(1)}, bf16[256,48]{0,1:T(8,128)(2,1)S(1)}, u32[]{:S(2)}, u32[]{:S(2)}) collective-permute-start(bf16[256,48]{0,1:T(8,128)(2,1)S(1)} %reshape.125), channel_id=1, source_target_pairs={{4,0},{8,4},{12,8},{5,1},{9,5},{13,9},{6,2},{10,6},{14,10},{7,3},{... | collective-permute-start | bytes 73736 | tf_op jit(solution)/shard_map/ppermute | solution.py:308
  6.7 5.7 %collective-permute-start = (bf16[256,48]{0,1:T(8,128)(2,1)S(1)}, bf16[256,48]{0,1:T(8,128)(2,1)S(1)}, u32[]{:S(2)}, u32[]{:S(2)}) collective-permute-start(bf16[256,48]{0,1:T(8,128)(2,1)S(1)} %reshape.123), channel_id=1, source_target_pairs={{0,4},{4,8},{8,12},{1,5},{5,9},{9,13},{2,6},{6,10},{10,14},{3,7},{... | collective-permute-start | bytes 73736 | tf_op jit(solution)/shard_map/ppermute | solution.py:308
  11.4 2.9 %copy-start.2 = (bf16[1,256,24,128]{3,2,1,0:T(8,128)(2,1)S(1)}, bf16[1,256,24,128]{3,2,1,0:T(8,128)(2,1)}, u32[]{:S(2)}) copy-start(bf16[1,256,24,128]{3,2,1,0:T(8,128)(2,1)} %param.11) | copy-start | bytes 4718596
  17.5 1.6 %copy-start.1 = (bf16[256,24,132]{2,1,0:T(8,128)(2,1)}, bf16[256,24,132]{2,1,0:T(8,128)(2,1)S(1)}, u32[]{:S(2)}) copy-start(bf16[256,24,132]{2,1,0:T(8,128)(2,1)S(1)} %pad_maximum_fusion) | copy-start | bytes 4866052
  19.1 5.5 %copy-start.10 = (pred[3840]{0:T(1024)(128)(4,1)S(1)}, pred[3840]{0:T(1024)(128)(4,1)}, u32[]{:S(2)}) copy-start(pred[3840]{0:T(1024)(128)(4,1)} %constant.161.clone) | copy-start | bytes 11524
  19.1 5.6 %copy-start.11 = (pred[3840]{0:T(1024)(128)(4,1)S(1)}, pred[3840]{0:T(1024)(128)(4,1)}, u32[]{:S(2)}) copy-start(pred[3840]{0:T(1024)(128)(4,1)} %constant.160.clone) | copy-start | bytes 11524
  19.1 5.6 %copy-start.12 = (pred[3840]{0:T(1024)(128)(4,1)S(1)}, pred[3840]{0:T(1024)(128)(4,1)}, u32[]{:S(2)}) copy-start(pred[3840]{0:T(1024)(128)(4,1)} %constant.159.clone) | copy-start | bytes 11524
  19.1 5.6 %copy-start.13 = (pred[3840]{0:T(1024)(128)(4,1)S(1)}, pred[3840]{0:T(1024)(128)(4,1)}, u32[]{:S(2)}) copy-start(pred[3840]{0:T(1024)(128)(4,1)} %constant.157.clone) | copy-start | bytes 11524
  19.1 5.6 %copy-start.14 = (pred[3840]{0:T(1024)(128)(4,1)S(1)}, pred[3840]{0:T(1024)(128)(4,1)}, u32[]{:S(2)}) copy-start(pred[3840]{0:T(1024)(128)(4,1)} %constant.158.clone) | copy-start | bytes 11524
  19.7 12.8 %collective-permute-start.2 = (bf16[256,264]{1,0:T(8,128)(2,1)S(1)}, bf16[256,264]{1,0:T(8,128)(2,1)S(1)}, u32[]{:S(2)}, u32[]{:S(2)}) collective-permute-start(bf16[256,264]{1,0:T(8,128)(2,1)S(1)} %reshape.137), channel_id=1, source_target_pairs={{0,16},{16,32},{32,48},{48,64},{64,80},{80,96},{96,112},{112,128},... | collective-permute-start | bytes 405512 | tf_op jit(solution)/shard_map/ppermute | solution.py:308
  23.3 3.6 %slice-start = ((f32[141312]{0:T(1024)}), f32[2048]{0:T(1024)S(1)}, s32[]{:S(2)}) async-start(f32[141312]{0:T(1024)} %param.13), calls=%async_computation | async-start | bytes 16384 | tf_op jit(solution)/shard_map/slice | solution.py:91
  23.3 9.2 %collective-permute-start.3 = (bf16[256,264]{1,0:T(8,128)(2,1)S(1)}, bf16[256,264]{1,0:T(8,128)(2,1)S(1)}, u32[]{:S(2)}, u32[]{:S(2)}) collective-permute-start(bf16[256,264]{1,0:T(8,128)(2,1)S(1)} %reshape.139), channel_id=1, source_target_pairs={{16,0},{32,16},{48,32},{64,48},{80,64},{96,80},{112,96},{128,112},... | collective-permute-start | bytes 405512 | tf_op jit(solution)/shard_map/ppermute | solution.py:308
  24.7 2.3 %copy-start.8 = (f32[1,3840]{1,0:T(1,128)S(1)}, f32[1,3840]{1,0:T(1,128)}, u32[]{:S(2)}) copy-start(f32[1,3840]{1,0:T(1,128)} %constant.171) | copy-start | bytes 46084
  24.7 2.3 %copy-start.9 = (f32[1,3840]{1,0:T(1,128)S(1)}, f32[1,3840]{1,0:T(1,128)}, u32[]{:S(2)}) copy-start(f32[1,3840]{1,0:T(1,128)} %constant.172) | copy-start | bytes 46084
  32.5 0.7 copy-start.5
  33.2 0.7 copy-start.6
  33.9 3.4 %copy-start = (s32[1,1,2]{2,1,0:T(1,128)S(1)}, s32[1,1,2]{2,1,0:T(1,128)}, u32[]{:S(2)}) copy-start(s32[1,1,2]{2,1,0:T(1,128)} %param.12) | copy-start | bytes 28
  52.0 3.4 %copy-start.7 = (f32[552]{0:T(1024)S(1)}, f32[552]{0:T(1024)}, u32[]{:S(2)}) copy-start(f32[552]{0:T(1024)} %param.14) | copy-start | bytes 6628
  53.4 56.9 %copy-start.4 = (f32[141312]{0:T(1024)S(1)}, f32[141312]{0:T(1024)}, u32[]{:S(2)}) copy-start(f32[141312]{0:T(1024)} %param.13) | copy-start | bytes 1695748
  53.5 3.2 %collective-permute-start.4 = (f32[4,32,553]{2,1,0:T(8,128)S(1)}, f32[4,32,553]{2,1,0:T(8,128)S(1)}, u32[]{:S(2)}, u32[]{:S(2)}) collective-permute-start(f32[4,32,553]{2,1,0:T(8,128)S(1)} %dynamic-slice_bitcast_fusion), channel_id=1, source_target_pairs={{0,1},{1,0},{2,3},{3,2},{4,5},{5,4},{6,7},{7,6},{8,9},{9,8},{10,11... | collective-permute-start | bytes 849416 | tf_op jit(solution)/shard_map/ppermute | solution.py:69
  56.8 6.3 %collective-permute-start.5 = (f32[32,553]{1,0:T(8,128)S(1)}, f32[32,553]{1,0:T(8,128)S(1)}, u32[]{:S(2)}, u32[]{:S(2)}) collective-permute-start(f32[32,553]{1,0:T(8,128)S(1)} %get-tuple-element.18), channel_id=1, source_target_pairs={{0,8},{4,12},{8,0},{12,4},{1,9},{5,13},{9,1},{13,5},{2,10},{6,14},... | collective-permute-start | bytes 212360 | tf_op jit(solution)/shard_map/ppermute | solution.py:69
  60.4 4.5 %collective-permute-start.6 = (f32[32,553]{1,0:T(8,128)S(1)}, f32[32,553]{1,0:T(8,128)S(1)}, u32[]{:S(2)}, u32[]{:S(2)}) collective-permute-start(f32[32,553]{1,0:T(8,128)S(1)} %get-tuple-element.17), channel_id=1, source_target_pairs={{0,4},{4,8},{8,12},{12,0},{1,5},{5,9},{9,13},{13,1},{2,6},{6,10},{... | collective-permute-start | bytes 212360 | tf_op jit(solution)/shard_map/ppermute | solution.py:69
  61.0 3.9 %collective-permute-start.7 = (f32[32,553]{1,0:T(8,128)S(1)}, f32[32,553]{1,0:T(8,128)S(1)}, u32[]{:S(2)}, u32[]{:S(2)}) collective-permute-start(f32[32,553]{1,0:T(8,128)S(1)} %get-tuple-element.16), channel_id=1, source_target_pairs={{0,12},{4,0},{8,4},{12,8},{1,13},{5,1},{9,5},{13,9},{2,14},{6,2},{... | collective-permute-start | bytes 212360 | tf_op jit(solution)/shard_map/ppermute | solution.py:69
  65.0 5.7 %collective-permute-start.9 = (f32[32,553]{1,0:T(8,128)S(1)}, f32[32,553]{1,0:T(8,128)S(1)}, u32[]{:S(2)}, u32[]{:S(2)}) collective-permute-start(f32[32,553]{1,0:T(8,128)S(1)} %fusion.2), channel_id=1, source_target_pairs={{0,16},{16,32},{32,48},{48,0},{64,80},{80,96},{96,112},{112,64},{1... | collective-permute-start | bytes 212360 | tf_op jit(solution)/shard_map/ppermute | solution.py:61
  67.4 3.3 %collective-permute-start.10 = (f32[32,553]{1,0:T(8,128)S(1)}, f32[32,553]{1,0:T(8,128)S(1)}, u32[]{:S(2)}, u32[]{:S(2)}) collective-permute-start(f32[32,553]{1,0:T(8,128)S(1)} %fusion.2), channel_id=1, source_target_pairs={{0,48},{16,0},{32,16},{48,32},{64,112},{80,64},{96,80},{112,96},{1... | collective-permute-start | bytes 212360 | tf_op jit(solution)/shard_map/ppermute | solution.py:61
  68.9 5.4 %collective-permute-start.8 = (f32[32,553]{1,0:T(8,128)S(1)}, f32[32,553]{1,0:T(8,128)S(1)}, u32[]{:S(2)}, u32[]{:S(2)}) collective-permute-start(f32[32,553]{1,0:T(8,128)S(1)} %fusion.2), channel_id=1, source_target_pairs={{0,32},{16,48},{32,0},{48,16},{64,96},{80,112},{96,64},{112,80},{1... | collective-permute-start | bytes 212360 | tf_op jit(solution)/shard_map/ppermute | solution.py:61
  74.3 7.8 %collective-permute-start.12 = (f32[32,553]{1,0:T(8,128)S(1)}, f32[32,553]{1,0:T(8,128)S(1)}, u32[]{:S(2)}, u32[]{:S(2)}) collective-permute-start(f32[32,553]{1,0:T(8,128)S(1)} %add_add_fusion.1), channel_id=1, source_target_pairs={{0,64},{16,80},{32,96},{48,112},{64,128},{80,144},{96,160},{112,17... | collective-permute-start | bytes 212360 | tf_op jit(solution)/shard_map/ppermute | solution.py:61
  77.5 4.6 %collective-permute-start.13 = (f32[32,553]{1,0:T(8,128)S(1)}, f32[32,553]{1,0:T(8,128)S(1)}, u32[]{:S(2)}, u32[]{:S(2)}) collective-permute-start(f32[32,553]{1,0:T(8,128)S(1)} %add_add_fusion.1), channel_id=1, source_target_pairs={{0,192},{16,208},{32,224},{48,240},{64,0},{80,16},{96,32},{112,48}... | collective-permute-start | bytes 212360 | tf_op jit(solution)/shard_map/ppermute | solution.py:61
  80.3 6.3 %collective-permute-start.11 = (f32[32,553]{1,0:T(8,128)S(1)}, f32[32,553]{1,0:T(8,128)S(1)}, u32[]{:S(2)}, u32[]{:S(2)}) collective-permute-start(f32[32,553]{1,0:T(8,128)S(1)} %add_add_fusion.1), channel_id=1, source_target_pairs={{0,128},{16,144},{32,160},{48,176},{64,192},{80,208},{96,224},{112... | collective-permute-start | bytes 212360 | tf_op jit(solution)/shard_map/ppermute | solution.py:61
  86.6 7.3 %collective-permute-start.14 = (f32[32,553]{1,0:T(8,128)S(1)}, f32[32,553]{1,0:T(8,128)S(1)}, u32[]{:S(2)}, u32[]{:S(2)}) collective-permute-start(f32[32,553]{1,0:T(8,128)S(1)} %add_add_fusion), channel_id=1, source_target_pairs={{0,2},{1,3},{2,0},{3,1},{4,6},{5,7},{6,4},{7,5},{8,10},{9,11},{10,... | collective-permute-start | bytes 212360 | tf_op jit(solution)/shard_map/ppermute | solution.py:61
  95.2 5.5 %collective-permute-start.15 = (f32[8,128]{1,0:T(8,128)S(1)}, f32[8,128]{1,0:T(8,128)S(1)}, u32[]{:S(2)}, u32[]{:S(2)}) collective-permute-start(f32[8,128]{1,0:T(8,128)S(1)} %broadcast_in_dim.33), channel_id=1, source_target_pairs={{0,1},{1,0},{2,3},{3,2},{4,5},{5,4},{6,7},{7,6},{8,9},{9,8},{10,11... | collective-permute-start | bytes 12296 | tf_op jit(solution)/shard_map/ppermute | solution.py:61
  101.4 5.5 %collective-permute-start.17 = (f32[8,128]{1,0:T(8,128)S(1)}, f32[8,128]{1,0:T(8,128)S(1)}, u32[]{:S(2)}, u32[]{:S(2)}) collective-permute-start(f32[8,128]{1,0:T(8,128)S(1)} %broadcast_add_fusion), channel_id=1, source_target_pairs={{0,4},{4,8},{8,12},{12,0},{1,5},{5,9},{9,13},{13,1},{2,6},{6,10},{... | collective-permute-start | bytes 12296 | tf_op jit(solution)/shard_map/ppermute | solution.py:61
  102.3 4.6 %collective-permute-start.18 = (f32[8,128]{1,0:T(8,128)S(1)}, f32[8,128]{1,0:T(8,128)S(1)}, u32[]{:S(2)}, u32[]{:S(2)}) collective-permute-start(f32[8,128]{1,0:T(8,128)S(1)} %broadcast_add_fusion), channel_id=1, source_target_pairs={{0,12},{4,0},{8,4},{12,8},{1,13},{5,1},{9,5},{13,9},{2,14},{6,2},{... | collective-permute-start | bytes 12296 | tf_op jit(solution)/shard_map/ppermute | solution.py:61
  104.5 4.0 %collective-permute-start.16 = (f32[8,128]{1,0:T(8,128)S(1)}, f32[8,128]{1,0:T(8,128)S(1)}, u32[]{:S(2)}, u32[]{:S(2)}) collective-permute-start(f32[8,128]{1,0:T(8,128)S(1)} %broadcast_add_fusion), channel_id=1, source_target_pairs={{0,8},{4,12},{8,0},{12,4},{1,9},{5,13},{9,1},{13,5},{2,10},{6,14},... | collective-permute-start | bytes 12296 | tf_op jit(solution)/shard_map/ppermute | solution.py:61

commit v2 on v1

--- a/solution.py
+++ b/solution.py
@@ -27,54 +27,59 @@
 BF = jnp.bfloat16
 F32 = jnp.float32
 
-RINGS = {
-    "y": ("row", 16, 4, 1),
-    "z": ("row", 16, 4, 4),
-    "x": ("col", 4, 4, 1),
-    "core": ("dp", 4, 2, 1),
-    "far": ("dp", 4, 2, 2),
-}
-
-
-def rotation(ring, step):
-    _, size, group, stride = RINGS[ring]
+SHARES = 32
+PAD = 640
+
+
+def exchange(size, partner):
+    return [(source, partner(source)) for source in range(size)]
+
+
+def neighbours(size, odd, wrap=False):
     pairs = []
-    for source in range(size):
-        place = (source // stride) % group
-        pairs.append((source, source + (((place + step) % group) - place) * stride))
+    for low in range(1 if odd else 0, size - 1, 2):
+        pairs += [(low, low + 1), (low + 1, low)]
+    if odd and wrap:
+        pairs += [(0, size - 1), (size - 1, 0)]
     return pairs
 
 
-def place_in(ring):
-    axis, _, group, stride = RINGS[ring]
-    return (lax.axis_index(axis) // stride) % group
+def along_z(partner):
+    pairs = []
+    for row in range(16):
+        for dp in range(4):
+            z = partner(dp // 2 * 4 + row // 4)
+            pairs.append((row * 4 + dp, (z % 4 * 4 + row % 4) * 4 + z // 4 * 2 + dp % 2))
+    return pairs
+
+
+def z_near(z):
+    return (3, 2, 1, 0, 7, 6, 5, 4)[z]
+
+
+CORE = ("dp", [exchange(4, lambda i: i ^ 1)])
+X_RING = ("col", [exchange(4, lambda i, k=k: i ^ k) for k in (1, 3, 2)])
+Y_RING = ("row", [exchange(16, lambda i, k=k: i ^ k) for k in (1, 3, 2)])
+Z_PAIR = (("row", "dp"), [along_z(lambda z: z ^ 1)])
+Z_RING = (
+    ("row", "dp"),
+    [along_z(z_near), along_z(lambda z: 7 - z), along_z(lambda z: z_near(7 - z))],
+)
+
+
+def received(values, stage):
+    axis, exchanges = stage
+    return [lax.ppermute(value, axis, pairs) for value, pairs in zip(values, exchanges)]
 
 
 def paired_sum(own, got):
     if len(got) == 1:
         return own + got[0]
-    return (own + got[1]) + (got[0] + got[2])
-
-
-def ring_sum(value, ring):
-    axis, _, group, _ = RINGS[ring]
-    got = [lax.ppermute(value, axis, rotation(ring, k)) for k in range(1, group)]
-    return paired_sum(value, got)
-
-
-def ring_scatter(value, ring):
-    axis, _, group, _ = RINGS[ring]
-    place = place_in(ring)
-    got = [
-        lax.ppermute(
-            lax.dynamic_index_in_dim(value, (place + k) % group, 0, keepdims=False),
-            axis,
-            rotation(ring, k),
-        )
-        for k in range(1, group)
-    ]
-    own = lax.dynamic_index_in_dim(value, place, 0, keepdims=False)
-    return paired_sum(own, got)
+    return (own + got[0]) + (got[1] + got[2])
+
+
+def stage_sum(value, stage):
+    return paired_sum(value, received([value] * len(stage[1]), stage))
 
 
 def unpack(weights):
@@ -110,10 +115,46 @@
     return ref[rows, low:high][:, first - low : first - low + size]
 
 
+def split_kernel(image_ref, own_ref, edge_ref, tall, select):
+    tall[...] = image_ref[...].astype(F32).reshape(C * TILE_ROWS, 128)
+    lane = lax.broadcasted_iota(jnp.int32, (128, 128), 1)
+    col = lax.broadcasted_iota(jnp.int32, (128, 128), 0)
+    for r in range(TILE_ROWS):
+        own_ref[:, r * 128 : (r + 1) * 128] = tall[pl.ds(r, C, stride=TILE_ROWS), :].astype(BF)
+        wanted = jnp.where(col < HALO, col + 64, jnp.where(col >= 126, col - 126, -1000))
+        select[r * 128 : (r + 1) * 128, :] = (lane - 2 * r == wanted).astype(F32).astype(BF)
+    edge_ref[...] = nn(own_ref[...], select[...]).astype(BF)
+
+
+def rim_kernel(place, own_ref, even_ref, odd_ref, rim_ref, up_ref, down_ref):
+    row, col = place[0], place[1]
+    lane = lax.broadcasted_iota(jnp.int32, (C, 128), 1)
+    odd_col = lax.rem(col, 2)
+    from_even = even_ref[...].astype(F32)
+    from_odd = odd_ref[...].astype(F32)
+    by_even = (lane < 64).astype(jnp.int32) == odd_col
+    outside = ((lane < 64) & (col == 0)) | ((lane >= 64) & (col == 3))
+    rim = jnp.where(outside, 0.0, jnp.where(by_even, from_even, from_odd)).astype(BF)
+    rim_ref[...] = rim
+    odd_row = lax.rem(row, 2)
+    high = (TILE_ROWS - HALO) * 128
+    first = pl.multiple_of((1 - odd_row) * high, 128)
+    second = pl.multiple_of(odd_row * high, 128)
+    up_ref[:, 0:256] = own_ref[:, pl.ds(first, 256)]
+    up_ref[:, 256:384] = rim
+    down_ref[:, 0:256] = own_ref[:, pl.ds(second, 256)]
+    down_ref[:, 256:384] = rim
+
+
 def kernel(
     labels,
-    x_ref,
+    place,
+    own_ref,
+    rim_ref,
+    even_ref,
+    odd_ref,
     mask_ref,
+    momentum_ref,
     win_t1,
     wf1,
     wb1,
@@ -126,8 +167,11 @@
     wout2,
     win2,
     head_ref,
+    keep_ref,
+    send_ref,
     flat_ref,
-    loss_ref,
+    parts,
+    x_ref,
     h1a,
     h1b,
     hs1,
@@ -147,6 +191,28 @@
     for ref in (h1a, h1b, dg2, wide):
         ref[:, :GUARD] = jnp.zeros((ref.shape[0], GUARD), ref.dtype)
         ref[:, GUARD + LANES :] = jnp.zeros((ref.shape[0], GUARD), ref.dtype)
+
+    odd_row = lax.rem(place[0], 2) == 1
+    above = jnp.where(odd_row, even_ref[...].astype(F32), odd_ref[...].astype(F32)).astype(BF)
+    below = jnp.where(odd_row, odd_ref[...].astype(F32), even_ref[...].astype(F32)).astype(BF)
+    for start, size in CHUNKS:
+        lanes = slice(start, start + size)
+        source = lax.broadcasted_iota(jnp.int32, (128, size), 0).astype(F32)
+        placed = [(source == mask_ref[k : k + 1, lanes]).astype(F32).astype(BF) for k in (3, 4, 5)]
+        value = nn(rim_ref[...], placed[0])
+        if start == 0:
+            value = value + nn(above[:, 256:], placed[1])
+        if start + size == LANES:
+            value = value + nn(below[:, 256:], placed[2])
+        x_ref[:, lanes] = value.astype(BF)
+    for r in range(ROWS):
+        if r < HALO:
+            line = above[:, r * 128 : (r + 1) * 128]
+        elif r < ROWS - HALO:
+            line = own_ref[:, (r - HALO) * 128 : (r - HALO + 1) * 128]
+        else:
+            line = below[:, (r - ROWS + HALO) * 128 : (r - ROWS + HALO + 1) * 128]
+        x_ref[:, r * COLS + HALO : r * COLS + HALO + 128] = line
 
     def forward(inputs, win_t, wf, wout_t, h1, hs, h2, output, masked):
         for start, size in CHUNKS:
@@ -193,7 +259,6 @@
         grad_head = grad_head + column * dlogits
         dpooled = jnp.sum(head * dlogits, axis=1, keepdims=True) / (TILE_ROWS * TILE_COLS)
         spread.append(dpooled.astype(BF).astype(F32))
-    loss_ref[...] = jnp.broadcast_to(loss, (8, 128))
 
     for start, size in CHUNKS:
         lanes = slice(start, start + size)
@@ -250,22 +315,84 @@
             pl.ds(j, 16, stride=16), 0:CLASSES
         ]
 
-
-def compute(labels, x_flat, masks, blocks_list, head):
+    row, col, core, far = place[0], place[1], place[2], place[3]
+    lane = lax.broadcasted_iota(jnp.int32, (16, 128), 1)
+    for m in range(16):
+        m_col, m_far, m_core = m // 4, m // 2 % 2, m % 2
+        first, offset = SHARE * m // 128, SHARE * m % 128
+        lines = [
+            pltpu.roll(flat_ref[pl.ds(first + j, 16, stride=69), :], (128 - offset) % 128, 1)
+            for j in range(6)
+        ]
+        block = parts.at[m_core ^ core, m_col ^ col]
+        for j in range(5):
+            value = jnp.where(lane < 128 - offset, lines[j], lines[j + 1])
+            if j == 4:
+                value = jnp.where(lane < 40, value, jnp.where(lane == 40, loss, 0.0))
+            block[m_far * 16 : m_far * 16 + 16, j * 128 : (j + 1) * 128] = value
+    mine = far * 16 + row
+    parts[0, 0, pl.ds(mine, 1), :] = parts[0, 0, pl.ds(mine, 1), :] + 9.0 * momentum_ref[...]
+    keep_ref[...] = parts[0]
+    send_ref[...] = parts[1]
+
+
+def total_kernel(place, own, got_a, got_b, got_c, row_ref, size_ref):
+    total = (own[...] + got_a[...]) + (got_b[...] + got_c[...])
+    lane = lax.broadcasted_iota(jnp.int32, (SHARES, PAD), 1)
+    kept = jnp.where(lane < SHARE, jnp.abs(total), 0.0)
+    size = jnp.sum(jnp.sum(kept, axis=0, keepdims=True), axis=1, keepdims=True)
+    size_ref[...] = jnp.broadcast_to(size, (1, PAD))
+    mine = place[3] * 16 + place[0]
+    line = lax.broadcasted_iota(jnp.int32, (SHARES, PAD), 0)
+    row_ref[...] = jnp.sum(jnp.where(line == mine, total, 0.0), axis=0, keepdims=True)
+
+
+VMEM = pl.BlockSpec(memory_space=pltpu.VMEM)
+SMEM = pl.BlockSpec(memory_space=pltpu.SMEM)
+PARAMS = pltpu.CompilerParams(vmem_limit_bytes=48 * 1024 * 1024)
+
+
+def shape(dims, kind):
+    return jax.ShapeDtypeStruct(dims, kind)
+
+
+def split(image):
+    return pl.pallas_call(
+        split_kernel,
+        out_shape=(shape((C, TILE_ROWS * 128), BF), shape((C, 128), BF)),
+        in_specs=[VMEM],
+        out_specs=(VMEM, VMEM),
+        scratch_shapes=[
+            pltpu.VMEM((C * TILE_ROWS, 128), F32),
+            pltpu.VMEM((TILE_ROWS * 128, 128), BF),
+        ],
+        compiler_params=PARAMS,
+    )(image)
+
+
+def rim(place, own, even, odd):
+    return pl.pallas_call(
+        rim_kernel,
+        out_shape=(shape((C, 128), BF), shape((C, 384), BF), shape((C, 384), BF)),
+        in_specs=[SMEM] + [VMEM] * 3,
+        out_specs=(VMEM,) * 3,
+        compiler_params=PARAMS,
+    )(place, own, even, odd)
+
+
+def compute(labels, place, pieces, masks, momentum, blocks_list, head):
     (win1, wmid1, wout1), (win2, wmid2, wout2) = blocks_list
     wf = [w.transpose(0, 3, 1, 2).reshape(3 * MID, 3 * MID) for w in (wmid1, wmid2)]
     wb = [w.transpose(1, 2, 0, 3).reshape(3 * MID, 3 * MID) for w in (wmid1, wmid2)]
-    vmem = pl.BlockSpec(memory_space=pltpu.VMEM)
-    smem = pl.BlockSpec(memory_space=pltpu.SMEM)
     return pl.pallas_call(
         kernel,
-        out_shape=(
-            jax.ShapeDtypeStruct((PARAM // 128, 128), F32),
-            jax.ShapeDtypeStruct((8, 128), F32),
-        ),
-        in_specs=[smem] + [vmem] * 14,
-        out_specs=(vmem, vmem),
+        out_shape=(shape((4, SHARES, PAD), F32), shape((4, SHARES, PAD), F32)),
+        in_specs=[SMEM, SMEM] + [VMEM] * 18,
+        out_specs=(VMEM, VMEM),
         scratch_shapes=[
+            pltpu.VMEM((PARAM // 128 + 8, 128), F32),
+            pltpu.VMEM((2, 4, SHARES, PAD), F32),
+            pltpu.VMEM((C, LANES), BF),
             pltpu.VMEM((MID, WIDE), BF),
             pltpu.VMEM((MID, WIDE), BF),
             pltpu.VMEM((3 * MID, LANES), BF),
@@ -281,11 +408,13 @@
             pltpu.VMEM((C, LANES), BF),
             pltpu.VMEM((C, MID), F32),
         ],
-        compiler_params=pltpu.CompilerParams(vmem_limit_bytes=48 * 1024 * 1024),
+        compiler_params=PARAMS,
     )(
         labels,
-        x_flat,
+        place,
+        *pieces,
         masks,
+        momentum,
         win1.T,
         wf[0],
         wb[0],
@@ -301,35 +430,19 @@
     )
 
 
-def neighbours(low_part, high_part, axis):
-    count = lax.axis_size(axis)
-    up = [(i, i + 1) for i in range(count - 1)]
-    down = [(target, source) for source, target in up]
-    return lax.ppermute(high_part, axis, up), lax.ppermute(low_part, axis, down)
-
-
-def extended(inputs):
-    height, width = inputs.shape[1:]
-    left, right = neighbours(
-        inputs[:, :, :HALO].reshape(C, -1), inputs[:, :, width - HALO :].reshape(C, -1), "col"
-    )
-    wide = jnp.concatenate(
-        [left.reshape(C, height, HALO), inputs, right.reshape(C, height, HALO)], axis=2
-    )
-    top, bottom = neighbours(
-        wide[:, :HALO].reshape(C, -1), wide[:, height - HALO :].reshape(C, -1), "row"
-    )
-    body = wide.reshape(C, -1)
-    return jnp.concatenate([top, body, bottom, jnp.zeros((C, LANES - PIX), BF)], axis=1)
-
-
-def make_masks():
+def make_masks(row, col):
     pixel = np.arange(LANES)
     r, c = pixel // COLS - HALO, pixel % COLS - HALO
-    inside = (pixel < PIX) & (r >= 0) & (r < TILE_ROWS)
+    real = pixel < PIX
+    inside = real & (r >= 0) & (r < TILE_ROWS)
     tiles = [inside & (c >= t * TILE_COLS) & (c < (t + 1) * TILE_COLS) for t in range(2)]
-    near = (pixel < PIX) & (r >= -1) & (r <= TILE_ROWS) & (c >= -1) & (c <= 2 * TILE_COLS)
-    row, col = lax.axis_index("row"), lax.axis_index("col")
+    near = real & (r >= -1) & (r <= TILE_ROWS) & (c >= -1) & (c <= 2 * TILE_COLS)
+    lane = np.where(c < 0, 2 * r + c + HALO, np.where(c >= 128, 64 + 2 * r + c - 128, -1000))
+    sources = [
+        np.where(inside, lane, -1000),
+        np.where(real & (r < 0) & (lane > -500), lane + 2 * TILE_ROWS, -1000),
+        np.where(real & (r >= TILE_ROWS) & (lane > -500), lane - 2 * TILE_ROWS, -1000),
+    ]
     rows, cols = lax.axis_size("row"), lax.axis_size("col")
     image = (
         jnp.asarray(near)
@@ -339,37 +452,50 @@
         & (jnp.asarray(c < 2 * TILE_COLS) | (col < cols - 1))
     )
     lines = [jnp.asarray(tiles[0], F32), jnp.asarray(tiles[1], F32), image.astype(F32)]
-    return jnp.stack(lines + [jnp.zeros((LANES,), F32)] * 5)
+    lines += [jnp.asarray(source, F32) for source in sources]
+    return jnp.stack(lines + [jnp.zeros((LANES,), F32)] * 2)
 
 
 def local(image, labels, weights, momentum):
+    row, col, dp = lax.axis_index("row"), lax.axis_index("col"), lax.axis_index("dp")
+    place = jnp.stack([row, col, dp % 2, dp // 2]).astype(jnp.int32)
     blocks_list, head = unpack(weights)
-    flat, loss_part = compute(
-        labels.reshape(2), extended(image[0]), make_masks(), blocks_list, head
+    masks = make_masks(row, col)
+    padded_momentum = jnp.pad(momentum, (0, PAD - SHARE)).reshape(1, PAD)
+
+    own, edge = split(image[0])
+    even = lax.ppermute(edge, "col", neighbours(4, False))
+    odd = lax.ppermute(edge, "col", neighbours(4, True, True))
+    beyond, up, down = rim(place, own, even, odd)
+    even = lax.ppermute(up, "row", neighbours(16, False))
+    odd = lax.ppermute(down, "row", neighbours(16, True))
+    keep, send = compute(
+        labels.reshape(2), place, (own, beyond, even, odd), masks, padded_momentum, blocks_list, head
     )
 
-    parts = flat.reshape(16, 4, 2, 2, SHARE).transpose(3, 1, 2, 0, 4)
-    loss_column = jnp.broadcast_to(loss_part[0, 0], (2, 4, 2, 16, 1))
-    parts = jnp.concatenate([parts, loss_column], axis=-1).reshape(2, 4, 32, SHARE + 1)
-    parts = ring_scatter(ring_scatter(parts, "core"), "x")
-    mine = place_in("far") * 16 + lax.axis_index("row")
-    at_home = (jnp.arange(32) == mine)[:, None]
-    parts = parts + jnp.where(at_home, 9.0 * jnp.pad(momentum, (0, 1))[None], 0.0)
-    for ring in ("y", "z", "far"):
-        parts = ring_sum(parts, ring)
-    magnitude = jnp.full((8, 128), jnp.sum(jnp.abs(parts[:, :SHARE])))
-    for ring in ("core", "x"):
-        magnitude = ring_sum(magnitude, ring)
-    scale_tau = 0.1 * magnitude[0, 0] / PARAM + 1e-06
-    own = lax.dynamic_index_in_dim(parts, mine, 0, keepdims=False)
-    loss = own[SHARE] / NTILES
-    own = own[:SHARE]
-    mixed = 0.1 * own
+    parts = keep + received([send], CORE)[0]
+    parts = paired_sum(parts[0], received([parts[1], parts[3], parts[2]], X_RING))
+    for stage in (Y_RING, Z_PAIR):
+        parts = stage_sum(parts, stage)
+    got = received([parts] * 3, Z_RING)
+    share, magnitude = pl.pallas_call(
+        total_kernel,
+        out_shape=(shape((1, PAD), F32), shape((1, PAD), F32)),
+        in_specs=[SMEM] + [VMEM] * 4,
+        out_specs=(VMEM, VMEM),
+        compiler_params=PARAMS,
+    )(place, parts, *got)
+    for stage in (CORE, X_RING):
+        magnitude = stage_sum(magnitude, stage)
+    scale_tau = 0.1 * magnitude[0, :SHARE] / PARAM + 1e-06
+    loss = share[0, SHARE] / NTILES
+    share = share[0, :SHARE]
+    mixed = 0.1 * share
     update = mixed / (jnp.abs(mixed) + scale_tau)
-    start = (lax.axis_index("row") * 16 + lax.axis_index("col") * 4 + lax.axis_index("dp")) * SHARE
+    start = (row * 16 + col * 4 + dp) * SHARE
     weight_share = lax.dynamic_slice_in_dim(weights, start, SHARE, 0)
     new_weights = weight_share - 0.0001 * (update + 0.1 * weight_share)
-    new_momentum = 0.9 * momentum + 0.01 * own
+    new_momentum = 0.9 * momentum + 0.01 * share
     return (new_weights, new_momentum, update, loss)
 
 

time: 113 us -> 83.9 us (0.74)
  local copies, waits for them, and re-layouts: 26.4 us -> 5.82 us
  starting transfers between devices: 43.6 us -> 34.7 us
  other arithmetic: 6.01 us -> 1.54 us
  Pallas kernels: 13.7 us -> 17.5 us
  waiting for transfers between devices: 18.7 us -> 21.2 us
    reshape x11 -> x1, local copies, waits for them, and re-layouts: 9.66 us -> 0.01 us  [local(): padded_momentum = jnp.pad(momentum, (0, PAD - SHARE)).reshape(1, PAD)]
    ppermute x19, starting transfers between devices: 43.6 us -> 34.7 us  [the longest x15 28.9 us: received(): lax.ppermute(value, axis, pairs)]
    slice x7 -> x1, local copies, waits for them, and re-layouts: 6.63 us -> 0.58 us  [local(): loss = share[0, SHARE] / NTILES]
    concatenate x2 -> x0, local copies, waits for them, and re-layouts: 4.03 us -> none  [the longest x1 3.35 us: extended(): jnp.concatenate([top, body, bottom, jnp.zeros((C, LANES - PIX), BF)], axi...]
    pallas_call x1 -> x4, Pallas kernels: 13.7 us -> 17.5 us  [the longest x1 15.1 us: compute(): pl.pallas_call(kernel, out_shape=(shape((4, SHARES, PAD), F32), shape((4,...]
    concatenate x1 -> x0, other arithmetic: 3.15 us -> none  [extended(): jnp.concatenate([left.reshape(C, height, HALO), inputs, right.reshape(C,...]
    ppermute x19, waiting for transfers between devices: 18.7 us -> 21.2 us  [the longest x15 18.3 us: received(): lax.ppermute(value, axis, pairs)]
    unnamed x30 -> x22, local copies, waits for them, and re-layouts: 3.03 us -> 1.45 us
  transfers between devices with their start and end apart: 19 -> 19, of which waited for: 9 -> 13; matrix products, arithmetic and copies ran while one was open for 9% -> 6% of each run, Pallas kernels for 0% -> 0%
where the time goes in v2:
time: 83.9 us; the launch traced here: 83.6 us
  starting transfers between devices  34.7 us (41%)
  waiting for transfers between devices  21.2 us (25%)
  Pallas kernels  17.5 us (21%)
  local copies, waits for them, and re-layouts  5.82 us (7%)
  between operations  2.86 us (3%)
  other arithmetic  1.54 us (2%)
    ppermute x15, starting transfers between devices, received(): lax.ppermute(value, axis, pairs)  28.9 us
    ppermute x15, waiting for transfers between devices, received(): lax.ppermute(value, axis, pairs)  18.3 us
    pallas_call x1, Pallas kernels, compute(): pl.pallas_call(kernel, out_shape=(shape((4, SHARES, PAD), F32), shape((4,...  15.1 us
    ppermute x1, starting transfers between devices, local(): odd = lax.ppermute(edge, 'col', neighbours(4, True, True))  3.39 us
  transfers between devices with their start and end apart: 19, of which 13 were waited for; matrix products, arithmetic and copies ran while one was open for 6% of the time, Pallas kernels for 0%

profile of v2, /device:TPU:1, one launch (start us, length us, event | category | flops | bytes accessed | tf_op | source)
XLA Modules:
  0.0 83.6 jit_solution(6950091223053280833)
XLA Ops:
  0.6 1.4 %copy-done = bf16[1,256,24,128]{3,2,1,0:T(8,128)(2,1)S(1)} copy-done((bf16[1,256,24,128]{3,2,1,0:T(8,128)(2,1)S(1)}, bf16[1,256,24,128]{3,2,1,0:T(8,128)(2,1)}, u32[]{:S(2)}) %copy-start) | copy-done | bytes 1572888
  2.0 1.2 %shard_map.165 = (bf16[256,3072]{1,0:T(8,128)(2,1)S(1)}, bf16[256,128]{1,0:T(8,128)(2,1)S(1)}) custom-call(bf16[256,24,128]{2,1,0:T(8,128)(2,1)S(1)} %bitcast.27), custom_call_target="tpu_custom_call" | custom-call | tf_op jit(solution)/shard_map/pallas_call | solution.py:360
  3.2 3.4 %collective-permute-start.1 = (bf16[256,128]{1,0:T(8,128)(2,1)S(1)}, bf16[256,128]{1,0:T(8,128)(2,1)S(1)}, u32[]{:S(2)}, u32[]{:S(2)}) collective-permute-start(bf16[256,128]{1,0:T(8,128)(2,1)S(1)} %get-tuple-element.14), channel_id=1, source_target_pairs={{4,8},{8,4},{0,12},{12,0},{5,9},{9,5},{1,13},{13,1},{6,10},{10,6},... | collective-permute-start | bytes 196616 | tf_op jit(solution)/shard_map/ppermute | solution.py:468
  6.9 1.4 %collective-permute-done.1.odd_ref = bf16[256,128]{1,0:T(8,128)(2,1)S(1)} collective-permute-done((bf16[256,128]{1,0:T(8,128)(2,1)S(1)}, bf16[256,128]{1,0:T(8,128)(2,1)S(1)}, u32[]{:S(2)}, u32[]{:S(2)}) %collective-permute-start.1) | collective-permute-done | bytes 65568 | tf_op jit(solution)/shard_map/ppermute | solution.py:468
  8.3 1.5 %collective-permute-done.even_ref = bf16[256,128]{1,0:T(8,128)(2,1)S(1)} collective-permute-done((bf16[256,128]{1,0:T(8,128)(2,1)S(1)}, bf16[256,128]{1,0:T(8,128)(2,1)S(1)}, u32[]{:S(2)}, u32[]{:S(2)}) %collective-permute-start) | collective-permute-done | bytes 65568 | tf_op jit(solution)/shard_map/ppermute | solution.py:467
  9.7 0.6 shard_map.166
  10.3 1.5 %collective-permute-start.2 = (bf16[256,384]{1,0:T(8,128)(2,1)S(1)}, bf16[256,384]{1,0:T(8,128)(2,1)S(1)}, u32[]{:S(2)}, u32[]{:S(2)}) collective-permute-start(bf16[256,384]{1,0:T(8,128)(2,1)S(1)} %get-tuple-element.16), channel_id=1, source_target_pairs={{0,16},{16,0},{32,48},{48,32},{64,80},{80,64},{96,112},{112,96},{1... | collective-permute-start | bytes 589832 | tf_op jit(solution)/shard_map/ppermute | solution.py:470
  11.9 0.8 %collective-permute-start.3 = (bf16[256,384]{1,0:T(8,128)(2,1)S(1)}, bf16[256,384]{1,0:T(8,128)(2,1)S(1)}, u32[]{:S(2)}, u32[]{:S(2)}) collective-permute-start(bf16[256,384]{1,0:T(8,128)(2,1)S(1)} %get-tuple-element.17), channel_id=1, source_target_pairs={{16,32},{32,16},{48,64},{64,48},{80,96},{96,80},{112,128},{128,112... | collective-permute-start | bytes 589832 | tf_op jit(solution)/shard_map/ppermute | solution.py:471
  12.8 0.6 reshape.95
  14.4 0.2 copy.24
  14.6 0.2 reshape.91.wf1
  14.8 0.1 copy.25
  14.9 0.2 reshape.92.wb1
  15.1 0.2 copy.27
  15.3 0.2 reshape.93.wf2
  15.4 0.1 copy.28
  15.6 0.2 reshape.94.wb2
  15.7 0.9 %stack.55.mask_ref = f32[8,3840]{1,0:T(8,128)S(1)} concatenate(f32[1,3840]{1,0:T(1,128)} %constant.105, f32[1,3840]{1,0:T(1,128)} %constant.106, f32[1,3840]{1,0:T(1,128)S(1)} %copy-done.4, f32[1,3840]{1,0:T(1,128)} %constant.107, f32[1,3840]{1,0:T(1,128)} %constant.108, f32[1,3840]{1,0:T(1,128)} %constant.109, f32[2,3840]{1,0:T(2,128)S(1)} %stack.54), dimensions={0} | concatenate | bytes 245760 | tf_op jit(solution)/shard_map/stack | solution.py:456
  16.7 15.1 %shard_map.167 = (f32[4,32,640]{2,1,0:T(8,128)S(1)}, f32[4,32,640]{2,1,0:T(8,128)S(1)}) custom-call(s32[2]{0:T(128)S(1)} %bitcast.32, s32[4]{0:T(128)S(1)} %pad_add_fusion.place, bf16[256,3072]{1,0:T(8,128)(2,1)S(1)} %get-tuple-element.13.own_ref, bf16[256,128]{1,0:T(8,128)(2,1)S(1)} %get-tuple-element.15.rim_ref, ...), custom_call_target="tpu_custom_call" | custom-call | tf_op jit(solution)/shard_map/pallas_call | solution.py:387
  31.9 2.3 %collective-permute-start.4 = (f32[4,32,640]{2,1,0:T(8,128)S(1)}, f32[4,32,640]{2,1,0:T(8,128)S(1)}, u32[]{:S(2)}, u32[]{:S(2)}) collective-permute-start(f32[4,32,640]{2,1,0:T(8,128)S(1)} %get-tuple-element.19), channel_id=1, source_target_pairs={{0,1},{1,0},{2,3},{3,2},{4,5},{5,4},{6,7},{7,6},{8,9},{9,8},{10,11... | collective-permute-start | bytes 983048 | tf_op jit(solution)/shard_map/ppermute | solution.py:72
  34.2 1.3 %collective-permute-done.4 = f32[4,32,640]{2,1,0:T(8,128)S(1)} collective-permute-done((f32[4,32,640]{2,1,0:T(8,128)S(1)}, f32[4,32,640]{2,1,0:T(8,128)S(1)}, u32[]{:S(2)}, u32[]{:S(2)}) %collective-permute-start.4) | collective-permute-done | bytes 327712 | tf_op jit(solution)/shard_map/ppermute | solution.py:72
  35.5 0.7 collective-permute-start.7
  36.2 1.7 %collective-permute-start.6 = (f32[32,640]{1,0:T(8,128)S(1)}, f32[32,640]{1,0:T(8,128)S(1)}, u32[]{:S(2)}, u32[]{:S(2)}) collective-permute-start(f32[32,640]{1,0:T(8,128)S(1)} %get-tuple-element.27), channel_id=1, source_target_pairs={{0,12},{4,8},{8,4},{12,0},{1,13},{5,9},{9,5},{13,1},{2,14},{6,10},... | collective-permute-start | bytes 245768 | tf_op jit(solution)/shard_map/ppermute | solution.py:72
  37.9 0.3 collective-permute-start.5
  38.2 2.5 %collective-permute-done.7 = f32[32,640]{1,0:T(8,128)S(1)} collective-permute-done((f32[32,640]{1,0:T(8,128)S(1)}, f32[32,640]{1,0:T(8,128)S(1)}, u32[]{:S(2)}, u32[]{:S(2)}) %collective-permute-start.7) | collective-permute-done | bytes 81952 | tf_op jit(solution)/shard_map/ppermute | solution.py:72
  40.7 2.5 %collective-permute-done.6 = f32[32,640]{1,0:T(8,128)S(1)} collective-permute-done((f32[32,640]{1,0:T(8,128)S(1)}, f32[32,640]{1,0:T(8,128)S(1)}, u32[]{:S(2)}, u32[]{:S(2)}) %collective-permute-start.6) | collective-permute-done | bytes 81952 | tf_op jit(solution)/shard_map/ppermute | solution.py:72
  43.2 5.4 %collective-permute-start.10 = (f32[32,640]{1,0:T(8,128)S(1)}, f32[32,640]{1,0:T(8,128)S(1)}, u32[]{:S(2)}, u32[]{:S(2)}) collective-permute-start(f32[32,640]{1,0:T(8,128)S(1)} %fusion.1), channel_id=1, source_target_pairs={{0,32},{16,48},{32,0},{48,16},{64,96},{80,112},{96,64},{112,80},{1... | collective-permute-start | bytes 245768 | tf_op jit(solution)/shard_map/ppermute | solution.py:72
  48.7 1.5 %collective-permute-start.9 = (f32[32,640]{1,0:T(8,128)S(1)}, f32[32,640]{1,0:T(8,128)S(1)}, u32[]{:S(2)}, u32[]{:S(2)}) collective-permute-start(f32[32,640]{1,0:T(8,128)S(1)} %fusion.1), channel_id=1, source_target_pairs={{0,48},{16,32},{32,16},{48,0},{64,112},{80,96},{96,80},{112,64},{1... | collective-permute-start | bytes 245768 | tf_op jit(solution)/shard_map/ppermute | solution.py:72
  50.1 0.5 collective-permute-start.8
  50.6 0.4 collective-permute-done.10
  51.0 2.7 %collective-permute-done.9 = f32[32,640]{1,0:T(8,128)S(1)} collective-permute-done((f32[32,640]{1,0:T(8,128)S(1)}, f32[32,640]{1,0:T(8,128)S(1)}, u32[]{:S(2)}, u32[]{:S(2)}) %collective-permute-start.9) | collective-permute-done | bytes 81952 | tf_op jit(solution)/shard_map/ppermute | solution.py:72
  53.7 0.9 %collective-permute-done.8 = f32[32,640]{1,0:T(8,128)S(1)} collective-permute-done((f32[32,640]{1,0:T(8,128)S(1)}, f32[32,640]{1,0:T(8,128)S(1)}, u32[]{:S(2)}, u32[]{:S(2)}) %collective-permute-start.8) | collective-permute-done | bytes 81952 | tf_op jit(solution)/shard_map/ppermute | solution.py:72
  54.6 2.9 %collective-permute-start.11 = (f32[32,640]{1,0:T(8,128)S(1)}, f32[32,640]{1,0:T(8,128)S(1)}, u32[]{:S(2)}, u32[]{:S(2)}) collective-permute-start(f32[32,640]{1,0:T(8,128)S(1)} %add_add_fusion), channel_id=1, source_target_pairs={{0,64},{1,65},{2,66},{3,67},{16,80},{17,81},{18,82},{19,83},{32,96... | collective-permute-start | bytes 245768 | tf_op jit(solution)/shard_map/ppermute | solution.py:72
  57.5 2.3 %collective-permute-done.11 = f32[32,640]{1,0:T(8,128)S(1)} collective-permute-done((f32[32,640]{1,0:T(8,128)S(1)}, f32[32,640]{1,0:T(8,128)S(1)}, u32[]{:S(2)}, u32[]{:S(2)}) %collective-permute-start.11) | collective-permute-done | bytes 81952 | tf_op jit(solution)/shard_map/ppermute | solution.py:72
  59.9 5.6 %collective-permute-start.14 = (f32[32,640]{1,0:T(8,128)S(1)}, f32[32,640]{1,0:T(8,128)S(1)}, u32[]{:S(2)}, u32[]{:S(2)}) collective-permute-start(f32[32,640]{1,0:T(8,128)S(1)} %add.81.own), channel_id=1, source_target_pairs={{0,2},{1,3},{2,0},{3,1},{16,18},{17,19},{18,16},{19,17},{32,34},{3... | collective-permute-start | bytes 245768 | tf_op jit(solution)/shard_map/ppermute | solution.py:72
  65.4 0.5 collective-permute-start.13
  66.0 1.8 %collective-permute-start.12 = (f32[32,640]{1,0:T(8,128)S(1)}, f32[32,640]{1,0:T(8,128)S(1)}, u32[]{:S(2)}, u32[]{:S(2)}) collective-permute-start(f32[32,640]{1,0:T(8,128)S(1)} %add.81.own), channel_id=1, source_target_pairs={{0,192},{1,193},{2,194},{3,195},{16,208},{17,209},{18,210},{19,211... | collective-permute-start | bytes 245768 | tf_op jit(solution)/shard_map/ppermute | solution.py:72
  67.8 3.8 %collective-permute-done.13.got_b = f32[32,640]{1,0:T(8,128)S(1)} collective-permute-done((f32[32,640]{1,0:T(8,128)S(1)}, f32[32,640]{1,0:T(8,128)S(1)}, u32[]{:S(2)}, u32[]{:S(2)}) %collective-permute-start.13) | collective-permute-done | bytes 81952 | tf_op jit(solution)/shard_map/ppermute | solution.py:72
  71.6 0.6 collective-permute-done.12.got_a
  72.2 0.6 shard_map.168
  72.9 3.0 %collective-permute-start.15 = (f32[1,640]{1,0:T(1,128)S(1)}, f32[1,640]{1,0:T(1,128)S(1)}, u32[]{:S(2)}, u32[]{:S(2)}) collective-permute-start(f32[1,640]{1,0:T(1,128)S(1)} %get-tuple-element.21), channel_id=1, source_target_pairs={{0,1},{1,0},{2,3},{3,2},{4,5},{5,4},{6,7},{7,6},{8,9},{9,8},{10,11... | collective-permute-start | bytes 7688 | tf_op jit(solution)/shard_map/ppermute | solution.py:72
  75.9 0.8 collective-permute-done.15
  76.8 2.2 %collective-permute-start.17 = (f32[1,640]{1,0:T(1,128)S(1)}, f32[1,640]{1,0:T(1,128)S(1)}, u32[]{:S(2)}, u32[]{:S(2)}) collective-permute-start(f32[1,640]{1,0:T(1,128)S(1)} %add.82), channel_id=1, source_target_pairs={{0,12},{4,8},{8,4},{12,0},{1,13},{5,9},{9,5},{13,1},{2,14},{6,10},... | collective-permute-start | bytes 7688 | tf_op jit(solution)/shard_map/ppermute | solution.py:72
  79.0 0.3 collective-permute-start.16
  79.4 0.6 multiply_add_fusion
  79.9 0.6 slice.104
  81.2 0.6 collective-permute-done.16
  81.8 0.7 multiply_subtract_fusion
  (58 shorter events, 1.5 us)
Async XLA Ops:
  0.6 1.4 %copy-start = (bf16[1,256,24,128]{3,2,1,0:T(8,128)(2,1)S(1)}, bf16[1,256,24,128]{3,2,1,0:T(8,128)(2,1)}, u32[]{:S(2)}) copy-start(bf16[1,256,24,128]{3,2,1,0:T(8,128)(2,1)} %param.14) | copy-start | bytes 4718596
  2.0 4.6 %copy-start.2 = (f32[141312]{0:T(1024)S(1)}, f32[141312]{0:T(1024)}, u32[]{:S(2)}) copy-start(f32[141312]{0:T(1024)} %param.16) | copy-start | bytes 1695748
  2.0 4.8 %copy-start.5 = (f32[552]{0:T(1024)S(1)}, f32[552]{0:T(1024)}, u32[]{:S(2)}) copy-start(f32[552]{0:T(1024)} %param.17) | copy-start | bytes 6628
  3.2 5.1 %collective-permute-start.1 = (bf16[256,128]{1,0:T(8,128)(2,1)S(1)}, bf16[256,128]{1,0:T(8,128)(2,1)S(1)}, u32[]{:S(2)}, u32[]{:S(2)}) collective-permute-start(bf16[256,128]{1,0:T(8,128)(2,1)S(1)} %get-tuple-element.14), channel_id=1, source_target_pairs={{4,8},{8,4},{0,12},{12,0},{5,9},{9,5},{1,13},{13,1},{6,10},{10,6},... | collective-permute-start | bytes 196616 | tf_op jit(solution)/shard_map/ppermute | solution.py:468
  6.6 3.1 %collective-permute-start = (bf16[256,128]{1,0:T(8,128)(2,1)S(1)}, bf16[256,128]{1,0:T(8,128)(2,1)S(1)}, u32[]{:S(2)}, u32[]{:S(2)}) collective-permute-start(bf16[256,128]{1,0:T(8,128)(2,1)S(1)} %get-tuple-element.14), channel_id=1, source_target_pairs={{0,4},{4,0},{8,12},{12,8},{1,5},{5,1},{9,13},{13,9},{2,6},{6,2},{1... | collective-permute-start | bytes 196616 | tf_op jit(solution)/shard_map/ppermute | solution.py:467
  6.6 6.1 %copy-start.6 = (pred[3840]{0:T(1024)(128)(4,1)S(1)}, pred[3840]{0:T(1024)(128)(4,1)}, u32[]{:S(2)}) copy-start(pred[3840]{0:T(1024)(128)(4,1)} %constant.94.clone) | copy-start | bytes 11524
  6.6 6.1 %copy-start.7 = (pred[3840]{0:T(1024)(128)(4,1)S(1)}, pred[3840]{0:T(1024)(128)(4,1)}, u32[]{:S(2)}) copy-start(pred[3840]{0:T(1024)(128)(4,1)} %constant.93.clone) | copy-start | bytes 11524
  6.6 6.1 %copy-start.8 = (pred[3840]{0:T(1024)(128)(4,1)S(1)}, pred[3840]{0:T(1024)(128)(4,1)}, u32[]{:S(2)}) copy-start(pred[3840]{0:T(1024)(128)(4,1)} %constant.92.clone) | copy-start | bytes 11524
  6.7 6.1 %copy-start.9 = (pred[3840]{0:T(1024)(128)(4,1)S(1)}, pred[3840]{0:T(1024)(128)(4,1)}, u32[]{:S(2)}) copy-start(pred[3840]{0:T(1024)(128)(4,1)} %constant.91.clone) | copy-start | bytes 11524
  6.7 6.1 %copy-start.10 = (pred[3840]{0:T(1024)(128)(4,1)S(1)}, pred[3840]{0:T(1024)(128)(4,1)}, u32[]{:S(2)}) copy-start(pred[3840]{0:T(1024)(128)(4,1)} %constant.90.clone) | copy-start | bytes 11524
  6.7 6.7 %slice-start = ((f32[141312]{0:T(1024)}), f32[2048]{0:T(1024)S(1)}, s32[]{:S(2)}) async-start(f32[141312]{0:T(1024)} %param.16), calls=%async_computation | async-start | bytes 16384 | tf_op jit(solution)/shard_map/slice | solution.py:96
  10.3 6.3 %collective-permute-start.2 = (bf16[256,384]{1,0:T(8,128)(2,1)S(1)}, bf16[256,384]{1,0:T(8,128)(2,1)S(1)}, u32[]{:S(2)}, u32[]{:S(2)}) collective-permute-start(bf16[256,384]{1,0:T(8,128)(2,1)S(1)} %get-tuple-element.16), channel_id=1, source_target_pairs={{0,16},{16,0},{32,48},{48,32},{64,80},{80,64},{96,112},{112,96},{1... | collective-permute-start | bytes 589832 | tf_op jit(solution)/shard_map/ppermute | solution.py:470
  11.9 4.8 %collective-permute-start.3 = (bf16[256,384]{1,0:T(8,128)(2,1)S(1)}, bf16[256,384]{1,0:T(8,128)(2,1)S(1)}, u32[]{:S(2)}, u32[]{:S(2)}) collective-permute-start(bf16[256,384]{1,0:T(8,128)(2,1)S(1)} %get-tuple-element.17), channel_id=1, source_target_pairs={{16,32},{32,16},{48,64},{64,48},{80,96},{96,80},{112,128},{128,112... | collective-permute-start | bytes 589832 | tf_op jit(solution)/shard_map/ppermute | solution.py:471
  14.1 1.6 %copy-start.4 = (f32[1,3840]{1,0:T(1,128)S(1)}, f32[1,3840]{1,0:T(1,128)}, u32[]{:S(2)}) copy-start(f32[1,3840]{1,0:T(1,128)} %reshape.95) | copy-start | bytes 46084
  14.3 2.4 %copy-start.1 = (s32[1,1,2]{2,1,0:T(1,128)S(1)}, s32[1,1,2]{2,1,0:T(1,128)}, u32[]{:S(2)}) copy-start(s32[1,1,2]{2,1,0:T(1,128)} %param.15) | copy-start | bytes 28
  31.8 50.0 %copy-start.3 = (f32[141312]{0:T(1024)S(1)}, f32[141312]{0:T(1024)}, u32[]{:S(2)}) copy-start(f32[141312]{0:T(1024)} %param.16) | copy-start | bytes 1695748
  31.9 3.6 %collective-permute-start.4 = (f32[4,32,640]{2,1,0:T(8,128)S(1)}, f32[4,32,640]{2,1,0:T(8,128)S(1)}, u32[]{:S(2)}, u32[]{:S(2)}) collective-permute-start(f32[4,32,640]{2,1,0:T(8,128)S(1)} %get-tuple-element.19), channel_id=1, source_target_pairs={{0,1},{1,0},{2,3},{3,2},{4,5},{5,4},{6,7},{7,6},{8,9},{9,8},{10,11... | collective-permute-start | bytes 983048 | tf_op jit(solution)/shard_map/ppermute | solution.py:72
  35.5 5.2 %collective-permute-start.7 = (f32[32,640]{1,0:T(8,128)S(1)}, f32[32,640]{1,0:T(8,128)S(1)}, u32[]{:S(2)}, u32[]{:S(2)}) collective-permute-start(f32[32,640]{1,0:T(8,128)S(1)} %get-tuple-element.26), channel_id=1, source_target_pairs={{0,8},{4,12},{8,0},{12,4},{1,9},{5,13},{9,1},{13,5},{2,10},{6,14},... | collective-permute-start | bytes 245768 | tf_op jit(solution)/shard_map/ppermute | solution.py:72
  36.2 7.0 %collective-permute-start.6 = (f32[32,640]{1,0:T(8,128)S(1)}, f32[32,640]{1,0:T(8,128)S(1)}, u32[]{:S(2)}, u32[]{:S(2)}) collective-permute-start(f32[32,640]{1,0:T(8,128)S(1)} %get-tuple-element.27), channel_id=1, source_target_pairs={{0,12},{4,8},{8,4},{12,0},{1,13},{5,9},{9,5},{13,1},{2,14},{6,10},... | collective-permute-start | bytes 245768 | tf_op jit(solution)/shard_map/ppermute | solution.py:72
  37.9 5.3 %collective-permute-start.5 = (f32[32,640]{1,0:T(8,128)S(1)}, f32[32,640]{1,0:T(8,128)S(1)}, u32[]{:S(2)}, u32[]{:S(2)}) collective-permute-start(f32[32,640]{1,0:T(8,128)S(1)} %get-tuple-element.28), channel_id=1, source_target_pairs={{0,4},{4,0},{8,12},{12,8},{1,5},{5,1},{9,13},{13,9},{2,6},{6,2},{1... | collective-permute-start | bytes 245768 | tf_op jit(solution)/shard_map/ppermute | solution.py:72
  43.2 7.8 %collective-permute-start.10 = (f32[32,640]{1,0:T(8,128)S(1)}, f32[32,640]{1,0:T(8,128)S(1)}, u32[]{:S(2)}, u32[]{:S(2)}) collective-permute-start(f32[32,640]{1,0:T(8,128)S(1)} %fusion.1), channel_id=1, source_target_pairs={{0,32},{16,48},{32,0},{48,16},{64,96},{80,112},{96,64},{112,80},{1... | collective-permute-start | bytes 245768 | tf_op jit(solution)/shard_map/ppermute | solution.py:72
  48.7 5.1 %collective-permute-start.9 = (f32[32,640]{1,0:T(8,128)S(1)}, f32[32,640]{1,0:T(8,128)S(1)}, u32[]{:S(2)}, u32[]{:S(2)}) collective-permute-start(f32[32,640]{1,0:T(8,128)S(1)} %fusion.1), channel_id=1, source_target_pairs={{0,48},{16,32},{32,16},{48,0},{64,112},{80,96},{96,80},{112,64},{1... | collective-permute-start | bytes 245768 | tf_op jit(solution)/shard_map/ppermute | solution.py:72
  50.1 4.5 %collective-permute-start.8 = (f32[32,640]{1,0:T(8,128)S(1)}, f32[32,640]{1,0:T(8,128)S(1)}, u32[]{:S(2)}, u32[]{:S(2)}) collective-permute-start(f32[32,640]{1,0:T(8,128)S(1)} %fusion.1), channel_id=1, source_target_pairs={{0,16},{16,0},{32,48},{48,32},{64,80},{80,64},{96,112},{112,96},{1... | collective-permute-start | bytes 245768 | tf_op jit(solution)/shard_map/ppermute | solution.py:72
  54.6 5.2 %collective-permute-start.11 = (f32[32,640]{1,0:T(8,128)S(1)}, f32[32,640]{1,0:T(8,128)S(1)}, u32[]{:S(2)}, u32[]{:S(2)}) collective-permute-start(f32[32,640]{1,0:T(8,128)S(1)} %add_add_fusion), channel_id=1, source_target_pairs={{0,64},{1,65},{2,66},{3,67},{16,80},{17,81},{18,82},{19,83},{32,96... | collective-permute-start | bytes 245768 | tf_op jit(solution)/shard_map/ppermute | solution.py:72
  59.9 8.0 %collective-permute-start.14 = (f32[32,640]{1,0:T(8,128)S(1)}, f32[32,640]{1,0:T(8,128)S(1)}, u32[]{:S(2)}, u32[]{:S(2)}) collective-permute-start(f32[32,640]{1,0:T(8,128)S(1)} %add.81.own), channel_id=1, source_target_pairs={{0,2},{1,3},{2,0},{3,1},{16,18},{17,19},{18,16},{19,17},{32,34},{3... | collective-permute-start | bytes 245768 | tf_op jit(solution)/shard_map/ppermute | solution.py:72
  65.4 6.2 %collective-permute-start.13 = (f32[32,640]{1,0:T(8,128)S(1)}, f32[32,640]{1,0:T(8,128)S(1)}, u32[]{:S(2)}, u32[]{:S(2)}) collective-permute-start(f32[32,640]{1,0:T(8,128)S(1)} %add.81.own), channel_id=1, source_target_pairs={{0,194},{1,195},{2,192},{3,193},{16,210},{17,211},{18,208},{19,209... | collective-permute-start | bytes 245768 | tf_op jit(solution)/shard_map/ppermute | solution.py:72
  66.0 6.2 %collective-permute-start.12 = (f32[32,640]{1,0:T(8,128)S(1)}, f32[32,640]{1,0:T(8,128)S(1)}, u32[]{:S(2)}, u32[]{:S(2)}) collective-permute-start(f32[32,640]{1,0:T(8,128)S(1)} %add.81.own), channel_id=1, source_target_pairs={{0,192},{1,193},{2,194},{3,195},{16,208},{17,209},{18,210},{19,211... | collective-permute-start | bytes 245768 | tf_op jit(solution)/shard_map/ppermute | solution.py:72
  72.9 3.8 %collective-permute-start.15 = (f32[1,640]{1,0:T(1,128)S(1)}, f32[1,640]{1,0:T(1,128)S(1)}, u32[]{:S(2)}, u32[]{:S(2)}) collective-permute-start(f32[1,640]{1,0:T(1,128)S(1)} %get-tuple-element.21), channel_id=1, source_target_pairs={{0,1},{1,0},{2,3},{3,2},{4,5},{5,4},{6,7},{7,6},{8,9},{9,8},{10,11... | collective-permute-start | bytes 7688 | tf_op jit(solution)/shard_map/ppermute | solution.py:72
  76.7 4.5 %collective-permute-start.18 = (f32[1,640]{1,0:T(1,128)S(1)}, f32[1,640]{1,0:T(1,128)S(1)}, u32[]{:S(2)}, u32[]{:S(2)}) collective-permute-start(f32[1,640]{1,0:T(1,128)S(1)} %add.82), channel_id=1, source_target_pairs={{0,8},{4,12},{8,0},{12,4},{1,9},{5,13},{9,1},{13,5},{2,10},{6,14},... | collective-permute-start | bytes 7688 | tf_op jit(solution)/shard_map/ppermute | solution.py:72
  76.8 4.4 %collective-permute-start.17 = (f32[1,640]{1,0:T(1,128)S(1)}, f32[1,640]{1,0:T(1,128)S(1)}, u32[]{:S(2)}, u32[]{:S(2)}) collective-permute-start(f32[1,640]{1,0:T(1,128)S(1)} %add.82), channel_id=1, source_target_pairs={{0,12},{4,8},{8,4},{12,0},{1,13},{5,9},{9,5},{13,1},{2,14},{6,10},... | collective-permute-start | bytes 7688 | tf_op jit(solution)/shard_map/ppermute | solution.py:72
  79.0 2.7 %collective-permute-start.16 = (f32[1,640]{1,0:T(1,128)S(1)}, f32[1,640]{1,0:T(1,128)S(1)}, u32[]{:S(2)}, u32[]{:S(2)}) collective-permute-start(f32[1,640]{1,0:T(1,128)S(1)} %add.82), channel_id=1, source_target_pairs={{0,4},{4,0},{8,12},{12,8},{1,5},{5,1},{9,13},{13,9},{2,6},{6,2},{1... | collective-permute-start | bytes 7688 | tf_op jit(solution)/shard_map/ppermute | solution.py:72

commit v3 on v2

v3 whole, which is shorter than its diff:
```python
import numpy as np
import jax
import jax.numpy as jnp
from jax import lax
from jax.experimental import pallas as pl
from jax.experimental.pallas import tpu as pltpu
from jax.sharding import PartitionSpec as P

C = 256
MID = 64
CLASSES = 8
TILE_ROWS = 24
TILE_COLS = 64
NTILES = 512
PARAM = 141312
SHARE = 552

HALO = 2
ROWS = TILE_ROWS + 2 * HALO
COLS = 2 * TILE_COLS + 2 * HALO
PIX = ROWS * COLS
LANES = 3840
GUARD = 256
WIDE = LANES + 2 * GUARD
CHUNK = 768
INNER, OUTER = CHUNK, LANES - CHUNK

BF = jnp.bfloat16
F32 = jnp.float32
ZERO = np.zeros((), BF)

SHARES = 32
PAD = 640


def exchange(size, partner):
    return [(source, partner(source)) for source in range(size)]


def neighbours(size, odd, wrap=False):
    pairs = []
    for low in range(1 if odd else 0, size - 1, 2):
        pairs += [(low, low + 1), (low + 1, low)]
    if odd and wrap:
        pairs += [(0, size - 1), (size - 1, 0)]
    return pairs


def along_z(partner):
    pairs = []
    for row in range(16):
        for dp in range(4):
            z = partner(dp // 2 * 4 + row // 4)
            pairs.append((row * 4 + dp, (z % 4 * 4 + row % 4) * 4 + z // 4 * 2 + dp % 2))
    return pairs


def z_near(z):
    return (3, 2, 1, 0, 7, 6, 5, 4)[z]


CORE = ("dp", [exchange(4, lambda i: i ^ 1)])
X_RING = ("col", [exchange(4, lambda i, k=k: i ^ k) for k in (1, 3, 2)])
Y_RING = ("row", [exchange(16, lambda i, k=k: i ^ k) for k in (1, 3, 2)])
Z_PAIR = (("row", "dp"), [along_z(lambda z: z ^ 1)])
Z_RING = (
    ("row", "dp"),
    [along_z(z_near), along_z(lambda z: 7 - z), along_z(lambda z: z_near(7 - z))],
)


def received(values, stage):
    axis, exchanges = stage
    return [lax.ppermute(value, axis, pairs) for value, pairs in zip(values, exchanges)]


def paired_sum(own, got):
    if len(got) == 1:
        return own + got[0]
    return (own + got[0]) + (got[1] + got[2])


def stage_sum(value, stage):
    return paired_sum(value, received([value] * len(stage[1]), stage))


def nn(left, right):
    return lax.dot_general(left, right, (((1,), (0,)), ((), ())), preferred_element_type=F32)


def nt(left, right):
    return lax.dot_general(left, right, (((1,), (1,)), ((), ())), preferred_element_type=F32)


ALL_ROWS = slice(None)


def cut(start, stop, most=CHUNK):
    tiles = (stop - start) // 128
    count = -(-tiles // (most // 128))
    edges = [start + tiles * k // count * 128 for k in range(count + 1)]
    return list(zip(edges[:-1], edges[1:]))


class Lanes:
    def __init__(self, *segments):
        self.segments = segments

    def get(self, start, stop, rows=ALL_ROWS):
        found = []
        for low, high, ref, base in self.segments:
            a, b = max(start, low), min(stop, high)
            if a < b:
                found.append(ref[rows, a - base : b - base])
        return found[0] if len(found) == 1 else jnp.concatenate(found, axis=1)

    def shifted(self, start, stop, shift, rows=ALL_ROWS):
        low = (start + shift) // 128 * 128
        high = -(-(stop + shift) // 128) * 128
        return self.get(low, high, rows)[:, start + shift - low : stop + shift - low]

    def put(self, start, stop, value, rows=ALL_ROWS):
        for low, high, ref, base in self.segments:
            if low <= start and stop <= high:
                ref[rows, start - base : stop - base] = value
                return
        raise ValueError("no segment")


def whole(ref, base=0):
    return Lanes((base, base + ref.shape[1], ref, base))


def split_kernel(image_ref, own_ref, edge_ref, landed, tall, select, arrived):
    count = landed.shape[0]
    part = C // count
    copies = [
        pltpu.make_async_copy(
            image_ref.at[0, pl.ds(k * part, part)], landed.at[k], arrived.at[k]
        )
        for k in range(count)
    ]
    for copy in copies:
        copy.start()
    lane = lax.broadcasted_iota(jnp.int32, (128, 128), 1)
    col = lax.broadcasted_iota(jnp.int32, (128, 128), 0)
    wanted = jnp.where(col < HALO, col + 64, jnp.where(col >= 126, col - 126, -1000))
    for r in range(TILE_ROWS):
        select[r * 128 : (r + 1) * 128, :] = (lane - 2 * r == wanted).astype(F32).astype(BF)
    for k, copy in enumerate(copies):
        copy.wait()
        rows = slice(k * part, (k + 1) * part)
        tall[k] = landed[k].astype(F32).reshape(part * TILE_ROWS, 128)
        for r in range(TILE_ROWS):
            own_ref[rows, r * 128 : (r + 1) * 128] = tall[
                k, pl.ds(r, part, stride=TILE_ROWS), :
            ].astype(BF)
        edge_ref[rows, :] = nn(own_ref[rows, :], select[...]).astype(BF)


def prepare_kernel(
    own_ref,
    weights_ref,
    flat_ref,
    win_t1,
    wf1,
    wb1,
    wout_t1,
    wout1,
    win_t2,
    wf2,
    wb2,
    wout_t2,
    wout2,
    win2,
    head_ref,
    tall,
):
    for r in range(TILE_ROWS):
        lane = (r + HALO) * COLS + HALO
        flat_ref[:, lane : lane + 128] = own_ref[:, r * 128 : (r + 1) * 128]
        flat_ref[:, lane - 2 * HALO : lane] = jnp.zeros((C, 2 * HALO), BF)
    first = HALO * COLS - HALO
    flat_ref[:, 0:first] = jnp.zeros((C, first), BF)
    last = (ROWS - HALO) * COLS - HALO
    flat_ref[:, last:] = jnp.zeros((C, LANES - last), BF)

    def unpacked(row, count):
        half = count // 2
        lines = weights_ref[row : row + half, :]
        tall[pl.ds(0, half, stride=2), :] = lines[:, :MID]
        tall[pl.ds(1, half, stride=2), :] = lines[:, MID:]
        return tall[0:count, :]

    for row, win_t, wf, wb, wout_t, wout, win in (
        (0, win_t1, wf1, wb1, wout_t1, wout1, None),
        (544, win_t2, wf2, wb2, wout_t2, wout2, win2),
    ):
        value = unpacked(row, C)
        win_t[...] = value.T.astype(BF)
        if win is not None:
            win[...] = value.astype(BF)
        value = jnp.concatenate([unpacked(row + 128 + r * 96, 3 * MID) for r in range(3)], axis=1)
        wb[...] = value.astype(BF)
        wf[...] = value.T.astype(BF)
        value = jnp.concatenate(
            [weights_ref[pl.ds(row + 416 + k, MID, stride=2), :] for k in range(2)], axis=1
        )
        wout[...] = value.astype(BF)
        wout_t[...] = value.T.astype(BF)
    for j in range(16):
        tall[pl.ds(j, 16, stride=16), 0:CLASSES] = weights_ref[
            1088:1104, j * CLASSES : (j + 1) * CLASSES
        ]
    head_ref[...] = tall[:, 0:CLASSES]


def rim_kernel(place, own_ref, even_ref, odd_ref, _, rim_ref, up_ref, down_ref):
    row, col = place[0], place[1]
    lane = lax.broadcasted_iota(jnp.int32, (C, 128), 1)
    odd_col = lax.rem(col, 2)
    from_even = even_ref[...].astype(F32)
    from_odd = odd_ref[...].astype(F32)
    by_even = (lane < 64).astype(jnp.int32) == odd_col
    outside = ((lane < 64) & (col == 0)) | ((lane >= 64) & (col == 3))
    rim = jnp.where(outside, 0.0, jnp.where(by_even, from_even, from_odd)).astype(BF)
    rim_ref[...] = rim
    odd_row = lax.rem(row, 2)
    high = (TILE_ROWS - HALO) * 128
    first = pl.multiple_of((1 - odd_row) * high, 128)
    second = pl.multiple_of(odd_row * high, 128)
    up_ref[:, 0:256] = own_ref[:, pl.ds(first, 256)]
    up_ref[:, 256:384] = rim
    down_ref[:, 0:256] = own_ref[:, pl.ds(second, 256)]
    down_ref[:, 256:384] = rim


def placed(rim, table, k, start, stop):
    source = lax.broadcasted_iota(jnp.int32, (128, stop - start), 0).astype(F32)
    return nn(rim, (source == table[k : k + 1, start:stop]).astype(F32).astype(BF))


def in_image(place, table, start, stop):
    row, col = place[0], place[1]
    r, c = table[6:7, start:stop], table[7:8, start:stop]
    r_low = jnp.where(row > 0, -HALO, 0).astype(F32)
    r_high = jnp.where(row < 15, TILE_ROWS + HALO, TILE_ROWS).astype(F32)
    c_low = jnp.where(col > 0, -HALO, 0).astype(F32)
    c_high = jnp.where(col < 3, 2 * TILE_COLS + HALO, 2 * TILE_COLS).astype(F32)
    inside = (r >= r_low) & (r < r_high) & (c >= c_low) & (c < c_high)
    return jnp.where(inside, table[2:3, start:stop], 0.0)


def enter(inputs, win_t, h1, ranges, mask):
    for start, stop in ranges:
        value = jnp.maximum(nn(win_t[...], inputs.get(start, stop)).astype(BF), ZERO)
        if mask is not None:
            value = value * mask(start, stop).astype(BF)
        h1.put(start, stop, value)


def spread(h1, hs, ranges):
    for start, stop in ranges:
        for s in range(3):
            hs.put(start, stop, h1.shifted(start, stop, s - 1), slice(s * MID, (s + 1) * MID))


def widen(wf, hs, wide, ranges):
    for start, stop in ranges:
        wide.put(start, stop, nn(wf[...], hs.get(start, stop)))


def leave(inputs, wide, wout_t, h2, output, ranges):
    for start, stop in ranges:
        total = sum(
            wide.shifted(start, stop, (r - 1) * COLS, slice(r * MID, (r + 1) * MID))
            for r in range(3)
        )
        value = jnp.maximum(total.astype(BF), ZERO)
        h2.put(start, stop, value)
        total = nn(wout_t[...], value) + inputs.get(start, stop).astype(F32)
        output.put(start, stop, jnp.maximum(total.astype(BF), ZERO))


X_SPAN = (INNER - 512, OUTER + 512)
HS1_SPAN = (INNER - 384, OUTER + 384)
Y1_SPAN = (INNER - 256, OUTER + 256)
Y2_SPAN = (INNER, OUTER)


def inner_kernel(
    place,
    flat_ref,
    rim_ref,
    table,
    win_t1,
    wf1,
    wout_t1,
    win_t2,
    wf2,
    wout_t2,
    x_ref,
    h1a_ref,
    hs1_ref,
    h2a_ref,
    y1_ref,
    h1b_ref,
    hs2_ref,
    h2b_ref,
    y2_ref,
    wide_ref,
):
    x, h1a = whole(x_ref, X_SPAN[0]), whole(h1a_ref, X_SPAN[0])
    hs1 = whole(hs1_ref, HS1_SPAN[0])
    h2a, y1 = whole(h2a_ref, Y1_SPAN[0]), whole(y1_ref, Y1_SPAN[0])
    h1b, hs2 = whole(h1b_ref, Y1_SPAN[0] - 128), whole(hs2_ref, Y1_SPAN[0])
    h2b, y2 = whole(h2b_ref, Y2_SPAN[0]), whole(y2_ref, Y2_SPAN[0])
    wide = whole(wide_ref, X_SPAN[0])
    wide_ref[:, 0:128] = jnp.zeros((3 * MID, 128), F32)
    wide_ref[:, wide_ref.shape[1] - 128 :] = jnp.zeros((3 * MID, 128), F32)
    h1b_ref[:, 0:128] = jnp.zeros((MID, 128), BF)
    h1b_ref[:, h1b_ref.shape[1] - 128 :] = jnp.zeros((MID, 128), BF)
    for start, stop in cut(*X_SPAN):
        value = placed(rim_ref[...], table, 3, start, stop) + flat_ref[:, start:stop].astype(F32)
        x.put(start, stop, value.astype(BF))
    enter(x, win_t1, h1a, cut(*X_SPAN), None)
    spread(h1a, hs1, cut(*HS1_SPAN))
    widen(wf1, hs1, wide, cut(*HS1_SPAN))
    leave(x, wide, wout_t1, h2a, y1, cut(*Y1_SPAN))
    mask = lambda start, stop: in_image(place, table, start, stop)
    enter(y1, win_t2, h1b, cut(*Y1_SPAN), mask)
    spread(h1b, hs2, cut(*Y1_SPAN))
    widen(wf2, hs2, wide, cut(*Y1_SPAN))
    leave(y1, wide, wout_t2, h2b, y2, cut(*Y2_SPAN))


def kernel(
    labels,
    place,
    flat_ref,
    rim_ref,
    even_ref,
    odd_ref,
    table,
    momentum_ref,
    win_t1,
    wf1,
    wb1,
    wout_t1,
    wout1,
    win_t2,
    wf2,
    wb2,
    wout_t2,
    wout2,
    win2,
    head_ref,
    x_mid,
    h1a_mid,
    hs1_mid,
    h2a_mid,
    y1_mid,
    h1b_mid,
    hs2_mid,
    h2b_mid,
    y2_mid,
    keep_ref,
    send_ref,
    packed,
    parts,
    x_ends,
    h1a_ends,
    hs1_ends,
    h2a_ends,
    y1_ends,
    h1b_ends,
    hs2_ends,
    h2b_ends,
    y2_ends,
    wide_ref,
    dg2_ref,
    ds,
    dz,
    tall,
):
    def joined(ends, mid, base):
        pad = (ends.shape[2] - CHUNK) // 2
        return Lanes(
            (-pad, INNER, ends.at[0], -pad),
            (INNER, OUTER, mid, base),
            (OUTER, LANES + pad, ends.at[1], OUTER - pad),
        )

    x = joined(x_ends, x_mid, X_SPAN[0])
    h1a = joined(h1a_ends, h1a_mid, X_SPAN[0])
    hs1 = joined(hs1_ends, hs1_mid, HS1_SPAN[0])
    h2a = joined(h2a_ends, h2a_mid, Y1_SPAN[0])
    y1 = joined(y1_ends, y1_mid, Y1_SPAN[0])
    h1b = joined(h1b_ends, h1b_mid, Y1_SPAN[0] - 128)
    hs2 = joined(hs2_ends, hs2_mid, Y1_SPAN[0])
    h2b = joined(h2b_ends, h2b_mid, Y2_SPAN[0])
    y2 = joined(y2_ends, y2_mid, Y2_SPAN[0])
    wide, dg2 = whole(wide_ref, -GUARD), whole(dg2_ref, -GUARD)
    for ref in (wide_ref, dg2_ref):
        ref[:, :GUARD] = jnp.zeros((ref.shape[0], GUARD), ref.dtype)
        ref[:, GUARD + LANES :] = jnp.zeros((ref.shape[0], GUARD), ref.dtype)
    for ref in (h1a_ends, h1b_ends):
        ref[0, :, 0:128] = jnp.zeros((MID, 128), BF)
        ref[1, :, CHUNK + 128 :] = jnp.zeros((MID, 128), BF)

    odd_row = lax.rem(place[0], 2) == 1
    above = jnp.where(odd_row, even_ref[...].astype(F32), odd_ref[...].astype(F32)).astype(BF)
    below = jnp.where(odd_row, odd_ref[...].astype(F32), even_ref[...].astype(F32)).astype(BF)
    for end, start, stop, k, rows in ((0, 0, INNER, 4, above), (1, OUTER, LANES, 5, below)):
        value = placed(rim_ref[...], table, 3, start, stop) + flat_ref[:, start:stop].astype(F32)
        value = value + placed(rows[:, 256:], table, k, start, stop)
        x_ends[end] = value.astype(BF)
        for r in range(HALO):
            lane = (r if end == 0 else ROWS - HALO + r) * COLS + HALO - start
            x_ends[end, :, lane : lane + 128] = rows[:, r * 128 : (r + 1) * 128]
    ends = [(0, INNER), (OUTER, LANES)]
    wider = [(0, INNER + 256), (OUTER - 256, LANES)]
    mask = lambda start, stop: in_image(place, table, start, stop)
    enter(x, win_t1, h1a, ends, None)
    spread(h1a, hs1, ends)
    widen(wf1, hs1, wide, wider)
    leave(x, wide, wout_t1, h2a, y1, ends)
    enter(y1, win_t2, h1b, ends, mask)
    spread(h1b, hs2, ends)
    widen(wf2, hs2, wide, wider)
    leave(y1, wide, wout_t2, h2b, y2, ends)

    everything = cut(0, LANES)
    assert (0, INNER) in everything and (OUTER, LANES) in everything
    pooled = sum(
        nt(y2.get(start, stop), table[:, start:stop].astype(BF)) for start, stop in everything
    ) * (1.0 / (TILE_ROWS * TILE_COLS))
    head = head_ref[...]
    classes = lax.broadcasted_iota(jnp.int32, (1, CLASSES), 1)
    loss = jnp.zeros((1, 1), F32)
    grad_head = jnp.zeros((C, CLASSES), F32)
    upstream = []
    for tile in range(2):
        column = pooled[:, tile : tile + 1]
        logits = jnp.sum(column * head, axis=0, keepdims=True)
        highest = jnp.max(logits, axis=1, keepdims=True)
        logsum = jnp.log(jnp.sum(jnp.exp(logits - highest), axis=1, keepdims=True)) + highest
        onehot = (classes == labels[tile]).astype(F32)
        loss = loss + logsum - jnp.sum(onehot * logits, axis=1, keepdims=True)
        dlogits = (jnp.exp(logits - logsum) - onehot) * (1.0 / NTILES)
        grad_head = grad_head + column * dlogits
        dpooled = jnp.sum(head * dlogits, axis=1, keepdims=True) / (TILE_ROWS * TILE_COLS)
        upstream.append(dpooled.astype(BF))

    for start, stop in everything:
        first, second = (table[t : t + 1, start:stop].astype(BF) for t in range(2))
        value = upstream[0] * first + upstream[1] * second
        dz[:, start:stop] = jnp.where(y2.get(start, stop) > ZERO, value, ZERO)

    def pack_tall(value, row):
        count = value.shape[0]
        tall[0:count, :] = value
        half = count // 2
        packed[row : row + half, 0:MID] = tall[pl.ds(0, half, stride=2), :]
        packed[row : row + half, MID:] = tall[pl.ds(1, half, stride=2), :]

    def backward(inputs, wb, wout, h1, hs, h2, row, then):
        grad_out = jnp.zeros((C, MID), F32)
        for start, stop in everything:
            value = dz[:, start:stop]
            grad_out = grad_out + nt(value, h2.get(start, stop))
            value = nn(wout[...], value).astype(BF)
            dg2.put(start, stop, jnp.where(h2.get(start, stop) > ZERO, value, ZERO))
        grad_out = grad_out.T
        packed[pl.ds(row + 416, MID, stride=2), :] = grad_out[:, :128]
        packed[pl.ds(row + 417, MID, stride=2), :] = grad_out[:, 128:]
        grad_mid = jnp.zeros((3 * MID, 3 * MID), F32)
        for start, stop in everything:
            for r in range(3):
                ds[r * MID : (r + 1) * MID, start:stop] = dg2.shifted(start, stop, (1 - r) * COLS)
            value = ds[:, start:stop]
            wide.put(start, stop, nn(wb[...], value))
            grad_mid = grad_mid + nt(hs.get(start, stop), value)
        for r in range(3):
            pack_tall(grad_mid[:, r * MID : (r + 1) * MID], row + 128 + r * 96)
        grad_in = jnp.zeros((C, MID), F32)
        for start, stop in everything:
            total = sum(
                wide.shifted(start, stop, 1 - s, slice(s * MID, (s + 1) * MID)) for s in range(3)
            )
            value = jnp.where(h1.get(start, stop) > ZERO, total.astype(BF), ZERO)
            grad_in = grad_in + nt(inputs.get(start, stop), value)
            if then is not None:
                then(start, stop, value)
        pack_tall(grad_in, row)

    def to_first(start, stop, value):
        total = nn(win2[...], value) + dz[:, start:stop].astype(F32)
        dz[:, start:stop] = jnp.where(y1.get(start, stop) > ZERO, total.astype(BF), ZERO)

    backward(y1, wb2, wout2, h1b, hs2, h2b, 544, to_first)
    backward(x, wb1, wout1, h1a, hs1, h2a, 0, None)
    tall[:, 0:CLASSES] = grad_head
    for j in range(16):
        packed[1088:1104, j * CLASSES : (j + 1) * CLASSES] = tall[
            pl.ds(j, 16, stride=16), 0:CLASSES
        ]

    row, col, core, far = place[0], place[1], place[2], place[3]
    lane = lax.broadcasted_iota(jnp.int32, (16, 128), 1)
    for m in range(16):
        m_col, m_far, m_core = m // 4, m // 2 % 2, m % 2
        first, offset = SHARE * m // 128, SHARE * m % 128
        lines = [
            pltpu.roll(packed[pl.ds(first + j, 16, stride=69), :], (128 - offset) % 128, 1)
            for j in range(6)
        ]
        block = parts.at[m_core ^ core, m_col ^ col]
        for j in range(5):
            value = jnp.where(lane < 128 - offset, lines[j], lines[j + 1])
            if j == 4:
                value = jnp.where(lane < 40, value, jnp.where(lane == 40, loss, 0.0))
            block[m_far * 16 : m_far * 16 + 16, j * 128 : (j + 1) * 128] = value
    mine = far * 16 + row
    parts[0, 0, pl.ds(mine, 1), :] = parts[0, 0, pl.ds(mine, 1), :] + 9.0 * momentum_ref[...]
    keep_ref[...] = parts[0]
    send_ref[...] = parts[1]


def total_kernel(place, own, got_a, got_b, got_c, row_ref, size_ref):
    total = (own[...] + got_a[...]) + (got_b[...] + got_c[...])
    lane = lax.broadcasted_iota(jnp.int32, (SHARES, PAD), 1)
    kept = jnp.where(lane < SHARE, jnp.abs(total), 0.0)
    size = jnp.sum(jnp.sum(kept, axis=0, keepdims=True), axis=1, keepdims=True)
    size_ref[...] = jnp.broadcast_to(size, (1, PAD))
    mine = place[3] * 16 + place[0]
    line = lax.broadcasted_iota(jnp.int32, (SHARES, PAD), 0)
    row_ref[...] = jnp.sum(jnp.where(line == mine, total, 0.0), axis=0, keepdims=True)


VMEM = pl.BlockSpec(memory_space=pltpu.VMEM)
SMEM = pl.BlockSpec(memory_space=pltpu.SMEM)
PARAMS = pltpu.CompilerParams(vmem_limit_bytes=36 * 1024 * 1024)


def shape(dims, kind):
    return jax.ShapeDtypeStruct(dims, kind)


def split(image):
    parts = 4
    return pl.pallas_call(
        split_kernel,
        out_shape=(shape((C, TILE_ROWS * 128), BF), shape((C, 128), BF)),
        in_specs=[pl.BlockSpec(memory_space=pltpu.HBM)],
        out_specs=(VMEM, VMEM),
        scratch_shapes=[
            pltpu.VMEM((parts, C // parts, TILE_ROWS, 128), BF),
            pltpu.VMEM((parts, C // parts * TILE_ROWS, 128), F32),
            pltpu.VMEM((TILE_ROWS * 128, 128), BF),
            pltpu.SemaphoreType.DMA((parts,)),
        ],
        compiler_params=PARAMS,
    )(image)


def prepare(own, weights):
    square = shape((3 * MID, 3 * MID), BF)
    down, up = shape((MID, C), BF), shape((C, MID), BF)
    block = [down, square, square, up, down]
    return pl.pallas_call(
        prepare_kernel,
        out_shape=[shape((C, LANES), BF)] + block + block + [up, shape((C, CLASSES), F32)],
        in_specs=[VMEM] * 2,
        out_specs=[VMEM] * 13,
        scratch_shapes=[pltpu.VMEM((C, MID), F32)],
        compiler_params=PARAMS,
        cost_estimate=pl.CostEstimate(flops=0, bytes_accessed=6_000_000, transcendentals=0),
    )(own, weights.reshape(PARAM // 128, 128))


def rim(place, own, even, odd, after):
    return pl.pallas_call(
        rim_kernel,
        out_shape=(shape((C, 128), BF), shape((C, 384), BF), shape((C, 384), BF)),
        in_specs=[SMEM] + [VMEM] * 4,
        out_specs=(VMEM,) * 3,
        compiler_params=PARAMS,
    )(place, own, even, odd, after)


def inner(place, flat, beyond, table, mats):
    win_t1, wf1, _, wout_t1, _, win_t2, wf2, _, wout_t2 = mats[:9]
    spans = [
        (C, X_SPAN),
        (MID, X_SPAN),
        (3 * MID, HS1_SPAN),
        (MID, Y1_SPAN),
        (C, Y1_SPAN),
        (MID, (Y1_SPAN[0] - 128, Y1_SPAN[1] + 128)),
        (3 * MID, Y1_SPAN),
        (MID, Y2_SPAN),
        (C, Y2_SPAN),
    ]
    return pl.pallas_call(
        inner_kernel,
        out_shape=[shape((rows, stop - start), BF) for rows, (start, stop) in spans],
        in_specs=[SMEM] + [VMEM] * 9,
        out_specs=[VMEM] * 9,
        scratch_shapes=[pltpu.VMEM((3 * MID, X_SPAN[1] - X_SPAN[0]), F32)],
        compiler_params=PARAMS,
        cost_estimate=pl.CostEstimate(
            flops=1_000_000_000, bytes_accessed=12_000_000, transcendentals=0
        ),
    )(place, flat, beyond, table, win_t1, wf1, wout_t1, win_t2, wf2, wout_t2)


def compute(labels, place, flat, beyond, even, odd, table, momentum, mats, mids):
    return pl.pallas_call(
        kernel,
        out_shape=(shape((4, SHARES, PAD), F32), shape((4, SHARES, PAD), F32)),
        in_specs=[SMEM, SMEM] + [VMEM] * 27,
        out_specs=(VMEM, VMEM),
        scratch_shapes=[
            pltpu.VMEM((PARAM // 128 + 8, 128), F32),
            pltpu.VMEM((2, 4, SHARES, PAD), F32),
            pltpu.VMEM((2, C, CHUNK), BF),
            pltpu.VMEM((2, MID, CHUNK + 256), BF),
            pltpu.VMEM((2, 3 * MID, CHUNK), BF),
            pltpu.VMEM((2, MID, CHUNK), BF),
            pltpu.VMEM((2, C, CHUNK), BF),
            pltpu.VMEM((2, MID, CHUNK + 256), BF),
            pltpu.VMEM((2, 3 * MID, CHUNK), BF),
            pltpu.VMEM((2, MID, CHUNK), BF),
            pltpu.VMEM((2, C, CHUNK), BF),
            pltpu.VMEM((3 * MID, WIDE), F32),
            pltpu.VMEM((MID, WIDE), BF),
            pltpu.VMEM((3 * MID, LANES), BF),
            pltpu.VMEM((C, LANES), BF),
            pltpu.VMEM((C, MID), F32),
        ],
        compiler_params=PARAMS,
    )(labels, place, flat, beyond, even, odd, table, momentum, *mats, *mids)


def make_table():
    pixel = np.arange(LANES)
    r, c = pixel // COLS - HALO, pixel % COLS - HALO
    real = pixel < PIX
    inside = real & (r >= 0) & (r < TILE_ROWS)
    tiles = [inside & (c >= t * TILE_COLS) & (c < (t + 1) * TILE_COLS) for t in range(2)]
    near = real & (r >= -1) & (r <= TILE_ROWS) & (c >= -1) & (c <= 2 * TILE_COLS)
    lane = np.where(c < 0, 2 * r + c + HALO, np.where(c >= 128, 64 + 2 * r + c - 128, -1000))
    sources = [
        np.where(inside, lane, -1000),
        np.where(real & (r < 0) & (lane > -500), lane + 2 * TILE_ROWS, -1000),
        np.where(real & (r >= TILE_ROWS) & (lane > -500), lane - 2 * TILE_ROWS, -1000),
    ]
    return jnp.asarray(np.stack([*tiles, near, *sources, r, c]).astype(np.float32))


def local(image, labels, weights, momentum):
    row, col, dp = lax.axis_index("row"), lax.axis_index("col"), lax.axis_index("dp")
    place = jnp.stack([row, col, dp % 2, dp // 2]).astype(jnp.int32)
    table = make_table()
    padded_momentum = jnp.pad(momentum, (0, PAD - SHARE)).reshape(1, PAD)

    own, edge = split(image)
    even = lax.ppermute(edge, "col", neighbours(4, False))
    odd = lax.ppermute(edge, "col", neighbours(4, True, True))
    flat, *mats = prepare(own, weights)
    beyond, up, down = rim(place, own, even, odd, mats[-1])
    even = lax.ppermute(up, "row", neighbours(16, False))
    odd = lax.ppermute(down, "row", neighbours(16, True))
    mids = inner(place, flat, beyond, table, mats)
    keep, send = compute(
        labels.reshape(2), place, flat, beyond, even, odd, table, padded_momentum, mats, mids
    )

    parts = keep + received([send], CORE)[0]
    parts = paired_sum(parts[0], received([parts[1], parts[3], parts[2]], X_RING))
    for stage in (Y_RING, Z_PAIR):
        parts = stage_sum(parts, stage)
    got = received([parts] * 3, Z_RING)
    share, magnitude = pl.pallas_call(
        total_kernel,
        out_shape=(shape((1, PAD), F32), shape((1, PAD), F32)),
        in_specs=[SMEM] + [VMEM] * 4,
        out_specs=(VMEM, VMEM),
        compiler_params=PARAMS,
    )(place, parts, *got)
    for stage in (CORE, X_RING):
        magnitude = stage_sum(magnitude, stage)
    scale_tau = 0.1 * magnitude[0, :SHARE] / PARAM + 1e-06
    loss = share[0, SHARE] / NTILES
    share = share[0, :SHARE]
    mixed = 0.1 * share
    update = mixed / (jnp.abs(mixed) + scale_tau)
    start = (row * 16 + col * 4 + dp) * SHARE
    weight_share = lax.dynamic_slice_in_dim(weights, start, SHARE, 0)
    new_weights = weight_share - 0.0001 * (update + 0.1 * weight_share)
    new_momentum = 0.9 * momentum + 0.01 * share
    return (new_weights, new_momentum, update, loss)


def solution(mesh):
    in_specs = (P("dp", None, "row", "col"), P("dp", "row", "col"), P(), P(("row", "col", "dp")))
    out_specs = (P(("row", "col", "dp")), P(("row", "col", "dp")), P(("row", "col", "dp")), P())
    return jax.shard_map(local, mesh=mesh, in_specs=in_specs, out_specs=out_specs, check_vma=False)
```

time: 83.9 us -> 81.9 us (0.976)
  local copies, waits for them, and re-layouts: 5.82 us -> 2.02 us
  Pallas kernels: 17.5 us -> 21 us
  waiting for transfers between devices: 21.2 us -> 19.9 us
    pallas_call x0 -> x2, Pallas kernels: none -> 5.34 us  [the longest x1 3.86 us: inner(): pl.pallas_call(inner_kernel, out_shape=[shape((rows, stop - start), BF) f...]
    pallas_call x1, Pallas kernels: 15.1 us -> 11.8 us  [compute(): pl.pallas_call(kernel, out_shape=(shape((4, SHARES, PAD), F32), shape((4,...]
    another operation x3 -> x0, local copies, waits for them, and re-layouts: 1.56 us -> none  [make_masks(): return jnp.stack(lines + [jnp.zeros((LANES,), F32)] * 2)]
    pallas_call x1, Pallas kernels: 1.19 us -> 2.57 us  [split(): pl.pallas_call(split_kernel, out_shape=(shape((C, TILE_ROWS * 128), BF),...]
    ppermute x1, waiting for transfers between devices: 1.35 us -> 0.07 us  [local(): odd = lax.ppermute(edge, 'col', neighbours(4, True, True))]
  transfers between devices with their start and end apart: 19 -> 19, of which waited for: 13 -> 13; matrix products, arithmetic and copies ran while one was open for 6% -> 2% of each run, Pallas kernels for 0% -> 7%
where the time goes in v3:
time: 81.9 us; the launch traced here: 81.7 us
  starting transfers between devices  34.7 us (42%)
  Pallas kernels  21 us (26%)
  waiting for transfers between devices  19.9 us (24%)
  between operations  2.59 us (3%)
  local copies, waits for them, and re-layouts  2.02 us (2%)
  other arithmetic  1.5 us (2%)
    ppermute x15, starting transfers between devices, received(): lax.ppermute(value, axis, pairs)  28.9 us
    ppermute x15, waiting for transfers between devices, received(): lax.ppermute(value, axis, pairs)  18.3 us
    pallas_call x1, Pallas kernels, compute(): pl.pallas_call(kernel, out_shape=(shape((4, SHARES, PAD), F32), shape((4,...  11.8 us
    pallas_call x1, Pallas kernels, inner(): pl.pallas_call(inner_kernel, out_shape=[shape((rows, stop - start), BF) f...  3.86 us
    ppermute x1, starting transfers between devices, local(): odd = lax.ppermute(edge, 'col', neighbours(4, True, True))  3.39 us
    pallas_call x1, Pallas kernels, split(): pl.pallas_call(split_kernel, out_shape=(shape((C, TILE_ROWS * 128), BF),...  2.57 us
  transfers between devices with their start and end apart: 19, of which 13 were waited for; matrix products, arithmetic and copies ran while one was open for 2% of the time, Pallas kernels for 7%

profile of v3, /device:TPU:1, one launch (start us, length us, event | category | flops | bytes accessed | tf_op | source)
XLA Modules:
  0.0 81.7 jit_solution(15598338547469656835)
XLA Ops:
  0.6 1.4 %copy-done = bf16[1,256,24,128]{3,2,1,0:T(8,128)(2,1)S(1)} copy-done((bf16[1,256,24,128]{3,2,1,0:T(8,128)(2,1)S(1)}, bf16[1,256,24,128]{3,2,1,0:T(8,128)(2,1)}, u32[]{:S(2)}) %copy-start) | copy-done | bytes 1572888
  2.0 2.6 %shard_map.84 = (bf16[256,3072]{1,0:T(8,128)(2,1)S(1)}, bf16[256,128]{1,0:T(8,128)(2,1)S(1)}) custom-call(bf16[1,256,24,128]{3,2,1,0:T(8,128)(2,1)S(1)} %copy-done), custom_call_target="tpu_custom_call" | custom-call | tf_op jit(solution)/shard_map/pallas_call | solution.py:552
  4.6 3.4 %collective-permute-start.1 = (bf16[256,128]{1,0:T(8,128)(2,1)S(1)}, bf16[256,128]{1,0:T(8,128)(2,1)S(1)}, u32[]{:S(2)}, u32[]{:S(2)}) collective-permute-start(bf16[256,128]{1,0:T(8,128)(2,1)S(1)} %get-tuple-element.37), channel_id=1, source_target_pairs={{4,8},{8,4},{0,12},{12,0},{5,9},{9,5},{1,13},{13,1},{6,10},{10,6},... | collective-permute-start | bytes 196616 | tf_op jit(solution)/shard_map/ppermute | solution.py:670
  8.0 0.0 collective-permute-start
  8.0 1.5 %shard_map.85 = (bf16[256,3840]{1,0:T(8,128)(2,1)S(1)}, bf16[64,256]{1,0:T(8,128)(2,1)S(1)}, bf16[192,192]{1,0:T(8,128)(2,1)S(1)}, bf16[192,192]{1,0:T(8,128)(2,...) custom-call(bf16[256,3072]{1,0:T(8,128)(2,1)S(1)} %get-tuple-element, ...), custom_call_target="tpu_custom_call" | custom-call | bytes 6000000 | tf_op jit(solution)/shard_map/pallas_call | solution.py:571
  9.5 0.1 pad_add_fusion.place
  9.6 0.1 collective-permute-done.1.odd_ref
  9.7 1.5 %collective-permute-done.even_ref = bf16[256,128]{1,0:T(8,128)(2,1)S(1)} collective-permute-done((bf16[256,128]{1,0:T(8,128)(2,1)S(1)}, bf16[256,128]{1,0:T(8,128)(2,1)S(1)}, u32[]{:S(2)}, u32[]{:S(2)}) %collective-permute-start) | collective-permute-done | bytes 65568 | tf_op jit(solution)/shard_map/ppermute | solution.py:669
  11.1 0.6 shard_map.86
  11.7 1.5 %collective-permute-start.2 = (bf16[256,384]{1,0:T(8,128)(2,1)S(1)}, bf16[256,384]{1,0:T(8,128)(2,1)S(1)}, u32[]{:S(2)}, u32[]{:S(2)}) collective-permute-start(bf16[256,384]{1,0:T(8,128)(2,1)S(1)} %get-tuple-element.40), channel_id=1, source_target_pairs={{0,16},{16,0},{32,48},{48,32},{64,80},{80,64},{96,112},{112,96},{1... | collective-permute-start | bytes 589832 | tf_op jit(solution)/shard_map/ppermute | solution.py:673
  13.3 0.8 %collective-permute-start.3 = (bf16[256,384]{1,0:T(8,128)(2,1)S(1)}, bf16[256,384]{1,0:T(8,128)(2,1)S(1)}, u32[]{:S(2)}, u32[]{:S(2)}) collective-permute-start(bf16[256,384]{1,0:T(8,128)(2,1)S(1)} %get-tuple-element.41), channel_id=1, source_target_pairs={{16,32},{32,16},{48,64},{64,48},{80,96},{96,80},{112,128},{128,112... | collective-permute-start | bytes 589832 | tf_op jit(solution)/shard_map/ppermute | solution.py:674
  14.2 0.0 copy-start.3
  14.2 3.9 %shard_map.87 = (bf16[256,3328]{1,0:T(8,128)(2,1)S(1)}, bf16[64,3328]{1,0:T(8,128)(2,1)S(1)}, bf16[192,3072]{1,0:T(8,128)(2,1)S(1)}, bf16[64,2816]{1,0:T(8,128)(...) custom-call(s32[4]{0:T(128)S(1)} %pad_add_fusion.place, ...), custom_call_target="tpu_custom_call" | custom-call | flops 1000000000 | bytes 12000000 | tf_op jit(solution)/shard_map/pallas_call | solution.py:605
  18.1 0.0 collective-permute-done.2.even_ref
  18.1 0.0 collective-permute-done.3.odd_ref
  18.1 11.8 %shard_map.88 = (f32[4,32,640]{2,1,0:T(8,128)S(1)}, f32[4,32,640]{2,1,0:T(8,128)S(1)}) custom-call(s32[2]{0:T(128)S(1)} %bitcast.20, s32[4]{0:T(128)S(1)} %pad_add_fusion.place, bf16[256,3840]{1,0:T(8,128)(2,1)S(1)} %get-tuple-element.36.flat_ref, bf16[256,128]{1,0:T(8,128)(2,1)S(1)} %get-tuple-element.39.rim_ref, ...), custom_call_target="tpu_custom_call" | custom-call | tf_op jit(solution)/shard_map/pallas_call | solution.py:619
  29.9 2.3 %collective-permute-start.4 = (f32[4,32,640]{2,1,0:T(8,128)S(1)}, f32[4,32,640]{2,1,0:T(8,128)S(1)}, u32[]{:S(2)}, u32[]{:S(2)}) collective-permute-start(f32[4,32,640]{2,1,0:T(8,128)S(1)} %get-tuple-element.63), channel_id=1, source_target_pairs={{0,1},{1,0},{2,3},{3,2},{4,5},{5,4},{6,7},{7,6},{8,9},{9,8},{10,11... | collective-permute-start | bytes 983048 | tf_op jit(solution)/shard_map/ppermute | solution.py:74
  32.2 1.3 %collective-permute-done.4 = f32[4,32,640]{2,1,0:T(8,128)S(1)} collective-permute-done((f32[4,32,640]{2,1,0:T(8,128)S(1)}, f32[4,32,640]{2,1,0:T(8,128)S(1)}, u32[]{:S(2)}, u32[]{:S(2)}) %collective-permute-start.4) | collective-permute-done | bytes 327712 | tf_op jit(solution)/shard_map/ppermute | solution.py:74
  33.6 0.7 collective-permute-start.7
  34.3 1.7 %collective-permute-start.6 = (f32[32,640]{1,0:T(8,128)S(1)}, f32[32,640]{1,0:T(8,128)S(1)}, u32[]{:S(2)}, u32[]{:S(2)}) collective-permute-start(f32[32,640]{1,0:T(8,128)S(1)} %get-tuple-element.71), channel_id=1, source_target_pairs={{0,12},{4,8},{8,4},{12,0},{1,13},{5,9},{9,5},{13,1},{2,14},{6,10},... | collective-permute-start | bytes 245768 | tf_op jit(solution)/shard_map/ppermute | solution.py:74
  36.0 0.3 collective-permute-start.5
  36.3 2.5 %collective-permute-done.7 = f32[32,640]{1,0:T(8,128)S(1)} collective-permute-done((f32[32,640]{1,0:T(8,128)S(1)}, f32[32,640]{1,0:T(8,128)S(1)}, u32[]{:S(2)}, u32[]{:S(2)}) %collective-permute-start.7) | collective-permute-done | bytes 81952 | tf_op jit(solution)/shard_map/ppermute | solution.py:74
  38.8 2.5 %collective-permute-done.6 = f32[32,640]{1,0:T(8,128)S(1)} collective-permute-done((f32[32,640]{1,0:T(8,128)S(1)}, f32[32,640]{1,0:T(8,128)S(1)}, u32[]{:S(2)}, u32[]{:S(2)}) %collective-permute-start.6) | collective-permute-done | bytes 81952 | tf_op jit(solution)/shard_map/ppermute | solution.py:74
  41.3 0.0 collective-permute-done.5
  41.3 5.4 %collective-permute-start.10 = (f32[32,640]{1,0:T(8,128)S(1)}, f32[32,640]{1,0:T(8,128)S(1)}, u32[]{:S(2)}, u32[]{:S(2)}) collective-permute-start(f32[32,640]{1,0:T(8,128)S(1)} %fusion.1), channel_id=1, source_target_pairs={{0,32},{16,48},{32,0},{48,16},{64,96},{80,112},{96,64},{112,80},{1... | collective-permute-start | bytes 245768 | tf_op jit(solution)/shard_map/ppermute | solution.py:74
  46.7 1.5 %collective-permute-start.9 = (f32[32,640]{1,0:T(8,128)S(1)}, f32[32,640]{1,0:T(8,128)S(1)}, u32[]{:S(2)}, u32[]{:S(2)}) collective-permute-start(f32[32,640]{1,0:T(8,128)S(1)} %fusion.1), channel_id=1, source_target_pairs={{0,48},{16,32},{32,16},{48,0},{64,112},{80,96},{96,80},{112,64},{1... | collective-permute-start | bytes 245768 | tf_op jit(solution)/shard_map/ppermute | solution.py:74
  48.2 0.5 collective-permute-start.8
  48.7 0.4 collective-permute-done.10
  49.1 2.7 %collective-permute-done.9 = f32[32,640]{1,0:T(8,128)S(1)} collective-permute-done((f32[32,640]{1,0:T(8,128)S(1)}, f32[32,640]{1,0:T(8,128)S(1)}, u32[]{:S(2)}, u32[]{:S(2)}) %collective-permute-start.9) | collective-permute-done | bytes 81952 | tf_op jit(solution)/shard_map/ppermute | solution.py:74
  51.8 0.9 %collective-permute-done.8 = f32[32,640]{1,0:T(8,128)S(1)} collective-permute-done((f32[32,640]{1,0:T(8,128)S(1)}, f32[32,640]{1,0:T(8,128)S(1)}, u32[]{:S(2)}, u32[]{:S(2)}) %collective-permute-start.8) | collective-permute-done | bytes 81952 | tf_op jit(solution)/shard_map/ppermute | solution.py:74
  52.7 2.8 %collective-permute-start.11 = (f32[32,640]{1,0:T(8,128)S(1)}, f32[32,640]{1,0:T(8,128)S(1)}, u32[]{:S(2)}, u32[]{:S(2)}) collective-permute-start(f32[32,640]{1,0:T(8,128)S(1)} %add_add_fusion), channel_id=1, source_target_pairs={{0,64},{1,65},{2,66},{3,67},{16,80},{17,81},{18,82},{19,83},{32,96... | collective-permute-start | bytes 245768 | tf_op jit(solution)/shard_map/ppermute | solution.py:74
  55.6 2.3 %collective-permute-done.11 = f32[32,640]{1,0:T(8,128)S(1)} collective-permute-done((f32[32,640]{1,0:T(8,128)S(1)}, f32[32,640]{1,0:T(8,128)S(1)}, u32[]{:S(2)}, u32[]{:S(2)}) %collective-permute-start.11) | collective-permute-done | bytes 81952 | tf_op jit(solution)/shard_map/ppermute | solution.py:74
  57.9 5.6 %collective-permute-start.14 = (f32[32,640]{1,0:T(8,128)S(1)}, f32[32,640]{1,0:T(8,128)S(1)}, u32[]{:S(2)}, u32[]{:S(2)}) collective-permute-start(f32[32,640]{1,0:T(8,128)S(1)} %add.81.own), channel_id=1, source_target_pairs={{0,2},{1,3},{2,0},{3,1},{16,18},{17,19},{18,16},{19,17},{32,34},{3... | collective-permute-start | bytes 245768 | tf_op jit(solution)/shard_map/ppermute | solution.py:74
  63.5 0.5 collective-permute-start.13
  64.1 1.8 %collective-permute-start.12 = (f32[32,640]{1,0:T(8,128)S(1)}, f32[32,640]{1,0:T(8,128)S(1)}, u32[]{:S(2)}, u32[]{:S(2)}) collective-permute-start(f32[32,640]{1,0:T(8,128)S(1)} %add.81.own), channel_id=1, source_target_pairs={{0,192},{1,193},{2,194},{3,195},{16,208},{17,209},{18,210},{19,211... | collective-permute-start | bytes 245768 | tf_op jit(solution)/shard_map/ppermute | solution.py:74
  65.9 0.0 collective-permute-done.14.got_c
  65.9 3.6 %collective-permute-done.13.got_b = f32[32,640]{1,0:T(8,128)S(1)} collective-permute-done((f32[32,640]{1,0:T(8,128)S(1)}, f32[32,640]{1,0:T(8,128)S(1)}, u32[]{:S(2)}, u32[]{:S(2)}) %collective-permute-start.13) | collective-permute-done | bytes 81952 | tf_op jit(solution)/shard_map/ppermute | solution.py:74
  69.5 0.8 collective-permute-done.12.got_a
  70.3 0.6 shard_map.89
  70.9 3.0 %collective-permute-start.15 = (f32[1,640]{1,0:T(1,128)S(1)}, f32[1,640]{1,0:T(1,128)S(1)}, u32[]{:S(2)}, u32[]{:S(2)}) collective-permute-start(f32[1,640]{1,0:T(1,128)S(1)} %get-tuple-element.65), channel_id=1, source_target_pairs={{0,1},{1,0},{2,3},{3,2},{4,5},{5,4},{6,7},{7,6},{8,9},{9,8},{10,11... | collective-permute-start | bytes 7688 | tf_op jit(solution)/shard_map/ppermute | solution.py:74
  74.0 0.8 collective-permute-done.15
  74.8 0.1 collective-permute-start.18
  74.9 2.3 %collective-permute-start.17 = (f32[1,640]{1,0:T(1,128)S(1)}, f32[1,640]{1,0:T(1,128)S(1)}, u32[]{:S(2)}, u32[]{:S(2)}) collective-permute-start(f32[1,640]{1,0:T(1,128)S(1)} %add.82), channel_id=1, source_target_pairs={{0,12},{4,8},{8,4},{12,0},{1,13},{5,9},{9,5},{13,1},{2,14},{6,10},... | collective-permute-start | bytes 7688 | tf_op jit(solution)/shard_map/ppermute | solution.py:74
  77.1 0.3 collective-permute-start.16
  77.4 0.6 multiply_add_fusion
  78.0 0.6 slice.27
  79.3 0.6 collective-permute-done.16
  79.9 0.7 multiply_subtract_fusion
  (20 shorter events, 0.2 us)
Async XLA Ops:
  0.6 1.4 %copy-start = (bf16[1,256,24,128]{3,2,1,0:T(8,128)(2,1)S(1)}, bf16[1,256,24,128]{3,2,1,0:T(8,128)(2,1)}, u32[]{:S(2)}) copy-start(bf16[1,256,24,128]{3,2,1,0:T(8,128)(2,1)} %image_ref.1) | copy-start | bytes 4718596
  2.0 6.0 %copy-start.1 = (f32[141312]{0:T(1024)S(1)}, f32[141312]{0:T(1024)}, u32[]{:S(2)}) copy-start(f32[141312]{0:T(1024)} %param.7) | copy-start | bytes 1695748
  4.6 5.1 %collective-permute-start.1 = (bf16[256,128]{1,0:T(8,128)(2,1)S(1)}, bf16[256,128]{1,0:T(8,128)(2,1)S(1)}, u32[]{:S(2)}, u32[]{:S(2)}) collective-permute-start(bf16[256,128]{1,0:T(8,128)(2,1)S(1)} %get-tuple-element.37), channel_id=1, source_target_pairs={{4,8},{8,4},{0,12},{12,0},{5,9},{9,5},{1,13},{13,1},{6,10},{10,6},... | collective-permute-start | bytes 196616 | tf_op jit(solution)/shard_map/ppermute | solution.py:670
  8.0 3.1 %collective-permute-start = (bf16[256,128]{1,0:T(8,128)(2,1)S(1)}, bf16[256,128]{1,0:T(8,128)(2,1)S(1)}, u32[]{:S(2)}, u32[]{:S(2)}) collective-permute-start(bf16[256,128]{1,0:T(8,128)(2,1)S(1)} %get-tuple-element.37), channel_id=1, source_target_pairs={{0,4},{4,0},{8,12},{12,8},{1,5},{5,1},{9,13},{13,9},{2,6},{6,2},{1... | collective-permute-start | bytes 196616 | tf_op jit(solution)/shard_map/ppermute | solution.py:669
  8.0 6.1 %copy-start.4 = (f32[552]{0:T(1024)S(1)}, f32[552]{0:T(1024)}, u32[]{:S(2)}) copy-start(f32[552]{0:T(1024)} %param.8) | copy-start | bytes 6628
  8.0 6.1 %copy-start.2 = (f32[8,3840]{1,0:T(8,128)S(1)}, f32[8,3840]{1,0:T(8,128)}, u32[]{:S(2)}) copy-start(f32[8,3840]{1,0:T(8,128)} %constant.67.clone.table) | copy-start | bytes 368644
  11.7 6.3 %collective-permute-start.2 = (bf16[256,384]{1,0:T(8,128)(2,1)S(1)}, bf16[256,384]{1,0:T(8,128)(2,1)S(1)}, u32[]{:S(2)}, u32[]{:S(2)}) collective-permute-start(bf16[256,384]{1,0:T(8,128)(2,1)S(1)} %get-tuple-element.40), channel_id=1, source_target_pairs={{0,16},{16,0},{32,48},{48,32},{64,80},{80,64},{96,112},{112,96},{1... | collective-permute-start | bytes 589832 | tf_op jit(solution)/shard_map/ppermute | solution.py:673
  13.3 4.8 %collective-permute-start.3 = (bf16[256,384]{1,0:T(8,128)(2,1)S(1)}, bf16[256,384]{1,0:T(8,128)(2,1)S(1)}, u32[]{:S(2)}, u32[]{:S(2)}) collective-permute-start(bf16[256,384]{1,0:T(8,128)(2,1)S(1)} %get-tuple-element.41), channel_id=1, source_target_pairs={{16,32},{32,16},{48,64},{64,48},{80,96},{96,80},{112,128},{128,112... | collective-permute-start | bytes 589832 | tf_op jit(solution)/shard_map/ppermute | solution.py:674
  14.2 3.9 %copy-start.3 = (s32[1,1,2]{2,1,0:T(1,128)S(1)}, s32[1,1,2]{2,1,0:T(1,128)}, u32[]{:S(2)}) copy-start(s32[1,1,2]{2,1,0:T(1,128)} %param.6) | copy-start | bytes 28
  29.9 3.6 %collective-permute-start.4 = (f32[4,32,640]{2,1,0:T(8,128)S(1)}, f32[4,32,640]{2,1,0:T(8,128)S(1)}, u32[]{:S(2)}, u32[]{:S(2)}) collective-permute-start(f32[4,32,640]{2,1,0:T(8,128)S(1)} %get-tuple-element.63), channel_id=1, source_target_pairs={{0,1},{1,0},{2,3},{3,2},{4,5},{5,4},{6,7},{7,6},{8,9},{9,8},{10,11... | collective-permute-start | bytes 983048 | tf_op jit(solution)/shard_map/ppermute | solution.py:74
  33.6 5.2 %collective-permute-start.7 = (f32[32,640]{1,0:T(8,128)S(1)}, f32[32,640]{1,0:T(8,128)S(1)}, u32[]{:S(2)}, u32[]{:S(2)}) collective-permute-start(f32[32,640]{1,0:T(8,128)S(1)} %get-tuple-element.70), channel_id=1, source_target_pairs={{0,8},{4,12},{8,0},{12,4},{1,9},{5,13},{9,1},{13,5},{2,10},{6,14},... | collective-permute-start | bytes 245768 | tf_op jit(solution)/shard_map/ppermute | solution.py:74
  34.3 7.0 %collective-permute-start.6 = (f32[32,640]{1,0:T(8,128)S(1)}, f32[32,640]{1,0:T(8,128)S(1)}, u32[]{:S(2)}, u32[]{:S(2)}) collective-permute-start(f32[32,640]{1,0:T(8,128)S(1)} %get-tuple-element.71), channel_id=1, source_target_pairs={{0,12},{4,8},{8,4},{12,0},{1,13},{5,9},{9,5},{13,1},{2,14},{6,10},... | collective-permute-start | bytes 245768 | tf_op jit(solution)/shard_map/ppermute | solution.py:74
  36.0 5.3 %collective-permute-start.5 = (f32[32,640]{1,0:T(8,128)S(1)}, f32[32,640]{1,0:T(8,128)S(1)}, u32[]{:S(2)}, u32[]{:S(2)}) collective-permute-start(f32[32,640]{1,0:T(8,128)S(1)} %get-tuple-element.72), channel_id=1, source_target_pairs={{0,4},{4,0},{8,12},{12,8},{1,5},{5,1},{9,13},{13,9},{2,6},{6,2},{1... | collective-permute-start | bytes 245768 | tf_op jit(solution)/shard_map/ppermute | solution.py:74
  41.3 7.8 %collective-permute-start.10 = (f32[32,640]{1,0:T(8,128)S(1)}, f32[32,640]{1,0:T(8,128)S(1)}, u32[]{:S(2)}, u32[]{:S(2)}) collective-permute-start(f32[32,640]{1,0:T(8,128)S(1)} %fusion.1), channel_id=1, source_target_pairs={{0,32},{16,48},{32,0},{48,16},{64,96},{80,112},{96,64},{112,80},{1... | collective-permute-start | bytes 245768 | tf_op jit(solution)/shard_map/ppermute | solution.py:74
  46.7 5.1 %collective-permute-start.9 = (f32[32,640]{1,0:T(8,128)S(1)}, f32[32,640]{1,0:T(8,128)S(1)}, u32[]{:S(2)}, u32[]{:S(2)}) collective-permute-start(f32[32,640]{1,0:T(8,128)S(1)} %fusion.1), channel_id=1, source_target_pairs={{0,48},{16,32},{32,16},{48,0},{64,112},{80,96},{96,80},{112,64},{1... | collective-permute-start | bytes 245768 | tf_op jit(solution)/shard_map/ppermute | solution.py:74
  48.2 4.5 %collective-permute-start.8 = (f32[32,640]{1,0:T(8,128)S(1)}, f32[32,640]{1,0:T(8,128)S(1)}, u32[]{:S(2)}, u32[]{:S(2)}) collective-permute-start(f32[32,640]{1,0:T(8,128)S(1)} %fusion.1), channel_id=1, source_target_pairs={{0,16},{16,0},{32,48},{48,32},{64,80},{80,64},{96,112},{112,96},{1... | collective-permute-start | bytes 245768 | tf_op jit(solution)/shard_map/ppermute | solution.py:74
  52.7 5.2 %collective-permute-start.11 = (f32[32,640]{1,0:T(8,128)S(1)}, f32[32,640]{1,0:T(8,128)S(1)}, u32[]{:S(2)}, u32[]{:S(2)}) collective-permute-start(f32[32,640]{1,0:T(8,128)S(1)} %add_add_fusion), channel_id=1, source_target_pairs={{0,64},{1,65},{2,66},{3,67},{16,80},{17,81},{18,82},{19,83},{32,96... | collective-permute-start | bytes 245768 | tf_op jit(solution)/shard_map/ppermute | solution.py:74
  57.9 8.0 %collective-permute-start.14 = (f32[32,640]{1,0:T(8,128)S(1)}, f32[32,640]{1,0:T(8,128)S(1)}, u32[]{:S(2)}, u32[]{:S(2)}) collective-permute-start(f32[32,640]{1,0:T(8,128)S(1)} %add.81.own), channel_id=1, source_target_pairs={{0,2},{1,3},{2,0},{3,1},{16,18},{17,19},{18,16},{19,17},{32,34},{3... | collective-permute-start | bytes 245768 | tf_op jit(solution)/shard_map/ppermute | solution.py:74
  63.5 6.0 %collective-permute-start.13 = (f32[32,640]{1,0:T(8,128)S(1)}, f32[32,640]{1,0:T(8,128)S(1)}, u32[]{:S(2)}, u32[]{:S(2)}) collective-permute-start(f32[32,640]{1,0:T(8,128)S(1)} %add.81.own), channel_id=1, source_target_pairs={{0,194},{1,195},{2,192},{3,193},{16,210},{17,211},{18,208},{19,209... | collective-permute-start | bytes 245768 | tf_op jit(solution)/shard_map/ppermute | solution.py:74
  64.1 6.2 %collective-permute-start.12 = (f32[32,640]{1,0:T(8,128)S(1)}, f32[32,640]{1,0:T(8,128)S(1)}, u32[]{:S(2)}, u32[]{:S(2)}) collective-permute-start(f32[32,640]{1,0:T(8,128)S(1)} %add.81.own), channel_id=1, source_target_pairs={{0,192},{1,193},{2,194},{3,195},{16,208},{17,209},{18,210},{19,211... | collective-permute-start | bytes 245768 | tf_op jit(solution)/shard_map/ppermute | solution.py:74
  70.9 3.8 %collective-permute-start.15 = (f32[1,640]{1,0:T(1,128)S(1)}, f32[1,640]{1,0:T(1,128)S(1)}, u32[]{:S(2)}, u32[]{:S(2)}) collective-permute-start(f32[1,640]{1,0:T(1,128)S(1)} %get-tuple-element.65), channel_id=1, source_target_pairs={{0,1},{1,0},{2,3},{3,2},{4,5},{5,4},{6,7},{7,6},{8,9},{9,8},{10,11... | collective-permute-start | bytes 7688 | tf_op jit(solution)/shard_map/ppermute | solution.py:74
  74.8 4.5 %collective-permute-start.18 = (f32[1,640]{1,0:T(1,128)S(1)}, f32[1,640]{1,0:T(1,128)S(1)}, u32[]{:S(2)}, u32[]{:S(2)}) collective-permute-start(f32[1,640]{1,0:T(1,128)S(1)} %add.82), channel_id=1, source_target_pairs={{0,8},{4,12},{8,0},{12,4},{1,9},{5,13},{9,1},{13,5},{2,10},{6,14},... | collective-permute-start | bytes 7688 | tf_op jit(solution)/shard_map/ppermute | solution.py:74
  74.9 4.4 %collective-permute-start.17 = (f32[1,640]{1,0:T(1,128)S(1)}, f32[1,640]{1,0:T(1,128)S(1)}, u32[]{:S(2)}, u32[]{:S(2)}) collective-permute-start(f32[1,640]{1,0:T(1,128)S(1)} %add.82), channel_id=1, source_target_pairs={{0,12},{4,8},{8,4},{12,0},{1,13},{5,9},{9,5},{13,1},{2,14},{6,10},... | collective-permute-start | bytes 7688 | tf_op jit(solution)/shard_map/ppermute | solution.py:74
  77.1 2.7 %collective-permute-start.16 = (f32[1,640]{1,0:T(1,128)S(1)}, f32[1,640]{1,0:T(1,128)S(1)}, u32[]{:S(2)}, u32[]{:S(2)}) collective-permute-start(f32[1,640]{1,0:T(1,128)S(1)} %add.82), channel_id=1, source_target_pairs={{0,4},{4,0},{8,12},{12,8},{1,5},{5,1},{9,13},{13,9},{2,6},{6,2},{1... | collective-permute-start | bytes 7688 | tf_op jit(solution)/shard_map/ppermute | solution.py:74

commit v4 on v3

--- a/solution.py
+++ b/solution.py
@@ -30,6 +30,8 @@
 ZERO = np.zeros((), BF)
 
 SHARES = 32
+CORNERS = 16
+MSG = (C + CORNERS, HALO * 128)
 PAD = 640
 
 
@@ -131,34 +133,19 @@
     return Lanes((base, base + ref.shape[1], ref, base))
 
 
-def split_kernel(image_ref, own_ref, edge_ref, landed, tall, select, arrived):
-    count = landed.shape[0]
-    part = C // count
-    copies = [
-        pltpu.make_async_copy(
-            image_ref.at[0, pl.ds(k * part, part)], landed.at[k], arrived.at[k]
-        )
-        for k in range(count)
-    ]
-    for copy in copies:
-        copy.start()
+def split_kernel(image_ref, own_ref, edge_ref, tall, select):
+    tall[...] = image_ref[0].astype(F32).reshape(C * TILE_ROWS, 128)
     lane = lax.broadcasted_iota(jnp.int32, (128, 128), 1)
     col = lax.broadcasted_iota(jnp.int32, (128, 128), 0)
     wanted = jnp.where(col < HALO, col + 64, jnp.where(col >= 126, col - 126, -1000))
     for r in range(TILE_ROWS):
+        own_ref[:, r * 128 : (r + 1) * 128] = tall[pl.ds(r, C, stride=TILE_ROWS), :].astype(BF)
         select[r * 128 : (r + 1) * 128, :] = (lane - 2 * r == wanted).astype(F32).astype(BF)
-    for k, copy in enumerate(copies):
-        copy.wait()
-        rows = slice(k * part, (k + 1) * part)
-        tall[k] = landed[k].astype(F32).reshape(part * TILE_ROWS, 128)
-        for r in range(TILE_ROWS):
-            own_ref[rows, r * 128 : (r + 1) * 128] = tall[
-                k, pl.ds(r, part, stride=TILE_ROWS), :
-            ].astype(BF)
-        edge_ref[rows, :] = nn(own_ref[rows, :], select[...]).astype(BF)
+    edge_ref[...] = nn(own_ref[...], select[...]).astype(BF)
 
 
 def prepare_kernel(
+    labels,
     own_ref,
     weights_ref,
     flat_ref,
@@ -174,6 +161,7 @@
     wout2,
     win2,
     head_ref,
+    target_ref,
     tall,
 ):
     for r in range(TILE_ROWS):
@@ -213,6 +201,9 @@
             1088:1104, j * CLASSES : (j + 1) * CLASSES
         ]
     head_ref[...] = tall[:, 0:CLASSES]
+    line = lax.broadcasted_iota(jnp.int32, (8, CLASSES), 0)
+    label = jnp.where(line == 0, labels[0], labels[1])
+    target_ref[...] = (lax.broadcasted_iota(jnp.int32, (8, CLASSES), 1) == label).astype(F32)
 
 
 def rim_kernel(place, own_ref, even_ref, odd_ref, _, rim_ref, up_ref, down_ref):
@@ -226,17 +217,18 @@
     rim = jnp.where(outside, 0.0, jnp.where(by_even, from_even, from_odd)).astype(BF)
     rim_ref[...] = rim
     odd_row = lax.rem(row, 2)
-    high = (TILE_ROWS - HALO) * 128
-    first = pl.multiple_of((1 - odd_row) * high, 128)
-    second = pl.multiple_of(odd_row * high, 128)
-    up_ref[:, 0:256] = own_ref[:, pl.ds(first, 256)]
-    up_ref[:, 256:384] = rim
-    down_ref[:, 0:256] = own_ref[:, pl.ds(second, 256)]
-    down_ref[:, 256:384] = rim
+    corner = lax.broadcasted_iota(jnp.int32, (CORNERS, 128), 0)
+    source = lax.broadcasted_iota(jnp.int32, (CORNERS, 128), 1)
+    for ref, low in ((up_ref, odd_row), (down_ref, 1 - odd_row)):
+        first = (1 - low) * (TILE_ROWS - HALO)
+        ref[0:C, :] = own_ref[:, pl.ds(pl.multiple_of(first * 128, 128), HALO * 128)]
+        wanted = 2 * first + jnp.where(corner < 4, corner, 64 + corner - 4)
+        pick = ((source == wanted) & (corner < 8)).astype(F32).astype(BF)
+        ref[C:, :] = nt(pick, rim).astype(BF)
 
 
 def placed(rim, table, k, start, stop):
-    source = lax.broadcasted_iota(jnp.int32, (128, stop - start), 0).astype(F32)
+    source = lax.broadcasted_iota(jnp.int32, (rim.shape[1], stop - start), 0).astype(F32)
     return nn(rim, (source == table[k : k + 1, start:stop]).astype(F32).astype(BF))
 
 
@@ -335,12 +327,11 @@
 
 
 def kernel(
-    labels,
     place,
     flat_ref,
     rim_ref,
+    odd_ref,
     even_ref,
-    odd_ref,
     table,
     momentum_ref,
     win_t1,
@@ -355,6 +346,7 @@
     wout2,
     win2,
     head_ref,
+    target_ref,
     x_mid,
     h1a_mid,
     hs1_mid,
@@ -413,11 +405,12 @@
     below = jnp.where(odd_row, odd_ref[...].astype(F32), even_ref[...].astype(F32)).astype(BF)
     for end, start, stop, k, rows in ((0, 0, INNER, 4, above), (1, OUTER, LANES, 5, below)):
         value = placed(rim_ref[...], table, 3, start, stop) + flat_ref[:, start:stop].astype(F32)
-        value = value + placed(rows[:, 256:], table, k, start, stop)
+        corners = rows[C:, :].astype(F32).T.astype(BF)
+        value = value + placed(corners, table, k, start, stop)
         x_ends[end] = value.astype(BF)
         for r in range(HALO):
             lane = (r if end == 0 else ROWS - HALO + r) * COLS + HALO - start
-            x_ends[end, :, lane : lane + 128] = rows[:, r * 128 : (r + 1) * 128]
+            x_ends[end, :, lane : lane + 128] = rows[0:C, r * 128 : (r + 1) * 128]
     ends = [(0, INNER), (OUTER, LANES)]
     wider = [(0, INNER + 256), (OUTER - 256, LANES)]
     mask = lambda start, stop: in_image(place, table, start, stop)
@@ -436,7 +429,6 @@
         nt(y2.get(start, stop), table[:, start:stop].astype(BF)) for start, stop in everything
     ) * (1.0 / (TILE_ROWS * TILE_COLS))
     head = head_ref[...]
-    classes = lax.broadcasted_iota(jnp.int32, (1, CLASSES), 1)
     loss = jnp.zeros((1, 1), F32)
     grad_head = jnp.zeros((C, CLASSES), F32)
     upstream = []
@@ -445,14 +437,19 @@
         logits = jnp.sum(column * head, axis=0, keepdims=True)
         highest = jnp.max(logits, axis=1, keepdims=True)
         logsum = jnp.log(jnp.sum(jnp.exp(logits - highest), axis=1, keepdims=True)) + highest
-        onehot = (classes == labels[tile]).astype(F32)
+        onehot = target_ref[tile : tile + 1, :]
         loss = loss + logsum - jnp.sum(onehot * logits, axis=1, keepdims=True)
         dlogits = (jnp.exp(logits - logsum) - onehot) * (1.0 / NTILES)
         grad_head = grad_head + column * dlogits
         dpooled = jnp.sum(head * dlogits, axis=1, keepdims=True) / (TILE_ROWS * TILE_COLS)
         upstream.append(dpooled.astype(BF))
 
-    for start, stop in everything:
+    own = [(256, 1024), (1024, 1792), (1792, 2560), (2560, 3584)]
+    one = [(0, 768), (768, 1536), (1536, 2304), (2304, 3072), (3072, 3584)]
+    dz[:, 0:256] = jnp.zeros((C, 256), BF)
+    dg2_ref[:, GUARD : GUARD + 256] = jnp.zeros((MID, 256), BF)
+    dg2_ref[:, GUARD + 3584 :] = jnp.zeros((MID, LANES - 3584 + GUARD), BF)
+    for start, stop in own:
         first, second = (table[t : t + 1, start:stop].astype(BF) for t in range(2))
         value = upstream[0] * first + upstream[1] * second
         dz[:, start:stop] = jnp.where(y2.get(start, stop) > ZERO, value, ZERO)
@@ -464,9 +461,9 @@
         packed[row : row + half, 0:MID] = tall[pl.ds(0, half, stride=2), :]
         packed[row : row + half, MID:] = tall[pl.ds(1, half, stride=2), :]
 
-    def backward(inputs, wb, wout, h1, hs, h2, row, then):
+    def backward(inputs, wb, wout, h1, hs, h2, row, then, near, far):
         grad_out = jnp.zeros((C, MID), F32)
-        for start, stop in everything:
+        for start, stop in near:
             value = dz[:, start:stop]
             grad_out = grad_out + nt(value, h2.get(start, stop))
             value = nn(wout[...], value).astype(BF)
@@ -475,7 +472,7 @@
         packed[pl.ds(row + 416, MID, stride=2), :] = grad_out[:, :128]
         packed[pl.ds(row + 417, MID, stride=2), :] = grad_out[:, 128:]
         grad_mid = jnp.zeros((3 * MID, 3 * MID), F32)
-        for start, stop in everything:
+        for start, stop in far:
             for r in range(3):
                 ds[r * MID : (r + 1) * MID, start:stop] = dg2.shifted(start, stop, (1 - r) * COLS)
             value = ds[:, start:stop]
@@ -484,7 +481,7 @@
         for r in range(3):
             pack_tall(grad_mid[:, r * MID : (r + 1) * MID], row + 128 + r * 96)
         grad_in = jnp.zeros((C, MID), F32)
-        for start, stop in everything:
+        for start, stop in far:
             total = sum(
                 wide.shifted(start, stop, 1 - s, slice(s * MID, (s + 1) * MID)) for s in range(3)
             )
@@ -498,8 +495,7 @@
         total = nn(win2[...], value) + dz[:, start:stop].astype(F32)
         dz[:, start:stop] = jnp.where(y1.get(start, stop) > ZERO, total.astype(BF), ZERO)
 
-    backward(y1, wb2, wout2, h1b, hs2, h2b, 544, to_first)
-    backward(x, wb1, wout1, h1a, hs1, h2a, 0, None)
+    backward(y1, wb2, wout2, h1b, hs2, h2b, 544, to_first, own, one)
     tall[:, 0:CLASSES] = grad_head
     for j in range(16):
         packed[1088:1104, j * CLASSES : (j + 1) * CLASSES] = tall[
@@ -507,20 +503,28 @@
         ]
 
     row, col, core, far = place[0], place[1], place[2], place[3]
-    lane = lax.broadcasted_iota(jnp.int32, (16, 128), 1)
-    for m in range(16):
-        m_col, m_far, m_core = m // 4, m // 2 % 2, m % 2
-        first, offset = SHARE * m // 128, SHARE * m % 128
-        lines = [
-            pltpu.roll(packed[pl.ds(first + j, 16, stride=69), :], (128 - offset) % 128, 1)
-            for j in range(6)
-        ]
-        block = parts.at[m_core ^ core, m_col ^ col]
-        for j in range(5):
-            value = jnp.where(lane < 128 - offset, lines[j], lines[j + 1])
-            if j == 4:
-                value = jnp.where(lane < 40, value, jnp.where(lane == 40, loss, 0.0))
-            block[m_far * 16 : m_far * 16 + 16, j * 128 : (j + 1) * 128] = value
+    lane = lax.broadcasted_iota(jnp.int32, (8, 128), 1)
+
+    def pack_shares(low):
+        for m in range(16):
+            m_col, m_far, m_core = m // 4, m // 2 % 2, m % 2
+            first, offset = 69 * low + SHARE * m // 128, SHARE * m % 128
+            lines = [
+                pltpu.roll(packed[pl.ds(first + j, 8, stride=69), :], (128 - offset) % 128, 1)
+                for j in range(6)
+            ]
+            block = parts.at[m_core ^ core, m_col ^ col]
+            for j in range(5):
+                value = jnp.where(lane < 128 - offset, lines[j], lines[j + 1])
+                if j == 4:
+                    value = jnp.where(lane < 40, value, jnp.where(lane == 40, loss, 0.0))
+                begin = m_far * 16 + low
+                block[begin : begin + 8, j * 128 : (j + 1) * 128] = value
+
+    pack_shares(8)
+    backward(x, wb1, wout1, h1a, hs1, h2a, 0, None, one, everything)
+
+    pack_shares(0)
     mine = far * 16 + row
     parts[0, 0, pl.ds(mine, 1), :] = parts[0, 0, pl.ds(mine, 1), :] + 9.0 * momentum_ref[...]
     keep_ref[...] = parts[0]
@@ -548,41 +552,38 @@
 
 
 def split(image):
-    parts = 4
     return pl.pallas_call(
         split_kernel,
         out_shape=(shape((C, TILE_ROWS * 128), BF), shape((C, 128), BF)),
-        in_specs=[pl.BlockSpec(memory_space=pltpu.HBM)],
+        in_specs=[VMEM],
         out_specs=(VMEM, VMEM),
         scratch_shapes=[
-            pltpu.VMEM((parts, C // parts, TILE_ROWS, 128), BF),
-            pltpu.VMEM((parts, C // parts * TILE_ROWS, 128), F32),
+            pltpu.VMEM((C * TILE_ROWS, 128), F32),
             pltpu.VMEM((TILE_ROWS * 128, 128), BF),
-            pltpu.SemaphoreType.DMA((parts,)),
         ],
         compiler_params=PARAMS,
     )(image)
 
 
-def prepare(own, weights):
+def prepare(labels, own, weights):
     square = shape((3 * MID, 3 * MID), BF)
     down, up = shape((MID, C), BF), shape((C, MID), BF)
     block = [down, square, square, up, down]
     return pl.pallas_call(
         prepare_kernel,
-        out_shape=[shape((C, LANES), BF)] + block + block + [up, shape((C, CLASSES), F32)],
-        in_specs=[VMEM] * 2,
-        out_specs=[VMEM] * 13,
+        out_shape=[shape((C, LANES), BF)] + block + block + [up, shape((C, CLASSES), F32), shape((8, CLASSES), F32)],
+        in_specs=[SMEM] + [VMEM] * 2,
+        out_specs=[VMEM] * 14,
         scratch_shapes=[pltpu.VMEM((C, MID), F32)],
         compiler_params=PARAMS,
         cost_estimate=pl.CostEstimate(flops=0, bytes_accessed=6_000_000, transcendentals=0),
-    )(own, weights.reshape(PARAM // 128, 128))
+    )(labels, own, weights.reshape(PARAM // 128, 128))
 
 
 def rim(place, own, even, odd, after):
     return pl.pallas_call(
         rim_kernel,
-        out_shape=(shape((C, 128), BF), shape((C, 384), BF), shape((C, 384), BF)),
+        out_shape=(shape((C, 128), BF), shape(MSG, BF), shape(MSG, BF)),
         in_specs=[SMEM] + [VMEM] * 4,
         out_specs=(VMEM,) * 3,
         compiler_params=PARAMS,
@@ -615,11 +616,11 @@
     )(place, flat, beyond, table, win_t1, wf1, wout_t1, win_t2, wf2, wout_t2)
 
 
-def compute(labels, place, flat, beyond, even, odd, table, momentum, mats, mids):
+def compute(place, flat, beyond, odd, even, table, momentum, mats, mids):
     return pl.pallas_call(
         kernel,
         out_shape=(shape((4, SHARES, PAD), F32), shape((4, SHARES, PAD), F32)),
-        in_specs=[SMEM, SMEM] + [VMEM] * 27,
+        in_specs=[SMEM] + [VMEM] * 28,
         out_specs=(VMEM, VMEM),
         scratch_shapes=[
             pltpu.VMEM((PARAM // 128 + 8, 128), F32),
@@ -640,7 +641,7 @@
             pltpu.VMEM((C, MID), F32),
         ],
         compiler_params=PARAMS,
-    )(labels, place, flat, beyond, even, odd, table, momentum, *mats, *mids)
+    )(place, flat, beyond, odd, even, table, momentum, *mats, *mids)
 
 
 def make_table():
@@ -651,10 +652,11 @@
     tiles = [inside & (c >= t * TILE_COLS) & (c < (t + 1) * TILE_COLS) for t in range(2)]
     near = real & (r >= -1) & (r <= TILE_ROWS) & (c >= -1) & (c <= 2 * TILE_COLS)
     lane = np.where(c < 0, 2 * r + c + HALO, np.where(c >= 128, 64 + 2 * r + c - 128, -1000))
+    corner = lambda k: np.where(c < 0, 2 * k + c + HALO, np.where(c >= 128, 4 + 2 * k + c - 128, -1000))
     sources = [
         np.where(inside, lane, -1000),
-        np.where(real & (r < 0) & (lane > -500), lane + 2 * TILE_ROWS, -1000),
-        np.where(real & (r >= TILE_ROWS) & (lane > -500), lane - 2 * TILE_ROWS, -1000),
+        np.where(real & (r < 0), corner(r + HALO), -1000),
+        np.where(real & (r >= TILE_ROWS), corner(r - TILE_ROWS), -1000),
     ]
     return jnp.asarray(np.stack([*tiles, near, *sources, r, c]).astype(np.float32))
 
@@ -668,13 +670,13 @@
     own, edge = split(image)
     even = lax.ppermute(edge, "col", neighbours(4, False))
     odd = lax.ppermute(edge, "col", neighbours(4, True, True))
-    flat, *mats = prepare(own, weights)
+    flat, *mats = prepare(labels.reshape(2), own, weights)
     beyond, up, down = rim(place, own, even, odd, mats[-1])
+    odd = lax.ppermute(down, "row", neighbours(16, True))
     even = lax.ppermute(up, "row", neighbours(16, False))
-    odd = lax.ppermute(down, "row", neighbours(16, True))
     mids = inner(place, flat, beyond, table, mats)
     keep, send = compute(
-        labels.reshape(2), place, flat, beyond, even, odd, table, padded_momentum, mats, mids
+        place, flat, beyond, odd, even, table, padded_momentum, mats, mids
     )
 
     parts = keep + received([send], CORE)[0]

time: 81.9 us -> 80 us (0.977)
  waiting for transfers between devices: 19.9 us -> 18.2 us
  Pallas kernels: 21 us -> 19.7 us
    ppermute x1, starting transfers between devices: 1.55 us -> 4.26 us  [local(): even = lax.ppermute(up, 'row', neighbours(16, False))]
    ppermute x15, starting transfers between devices: 28.9 us -> 26.9 us  [received(): lax.ppermute(value, axis, pairs)]
    pallas_call x1, Pallas kernels: 2.57 us -> 1.19 us  [split(): pl.pallas_call(split_kernel, out_shape=(shape((C, TILE_ROWS * 128), BF),...]
    ppermute x15, waiting for transfers between devices: 18.3 us -> 17.2 us  [received(): lax.ppermute(value, axis, pairs)]
  transfers between devices with their start and end apart: 19 -> 19, of which waited for: 13 -> 12; matrix products, arithmetic and copies ran while one was open for 2% -> 2% of each run, Pallas kernels for 7% -> 7%
where the time goes in v4:
time: 80 us; the launch traced here: 79.1 us
  starting transfers between devices  35.2 us (44%)
  Pallas kernels  19.7 us (25%)
  waiting for transfers between devices  18.2 us (23%)
  between operations  2.55 us (3%)
  local copies, waits for them, and re-layouts  2.03 us (3%)
  other arithmetic  1.49 us (2%)
    ppermute x15, starting transfers between devices, received(): lax.ppermute(value, axis, pairs)  26.9 us
    ppermute x15, waiting for transfers between devices, received(): lax.ppermute(value, axis, pairs)  17.2 us
    pallas_call x1, Pallas kernels, compute(): pl.pallas_call(kernel, out_shape=(shape((4, SHARES, PAD), F32), shape((4,...  11.2 us
    ppermute x1, starting transfers between devices, local(): even = lax.ppermute(up, 'row', neighbours(16, False))  4.26 us
    pallas_call x1, Pallas kernels, inner(): pl.pallas_call(inner_kernel, out_shape=[shape((rows, stop - start), BF) f...  3.86 us
    ppermute x1, starting transfers between devices, local(): odd = lax.ppermute(edge, 'col', neighbours(4, True, True))  3.39 us
    pallas_call x1, Pallas kernels, prepare(): pl.pallas_call(prepare_kernel, out_shape=[shape((C, LANES), BF)] + block...  2.03 us
  transfers between devices with their start and end apart: 19, of which 12 were waited for; matrix products, arithmetic and copies ran while one was open for 2% of the time, Pallas kernels for 7%

profile of v4, /device:TPU:1, one launch (start us, length us, event | category | flops | bytes accessed | tf_op | source)
XLA Modules:
  0.0 79.1 jit_solution(11889695136411064144)
XLA Ops:
  0.6 1.4 %copy-done = bf16[1,256,24,128]{3,2,1,0:T(8,128)(2,1)S(1)} copy-done((bf16[1,256,24,128]{3,2,1,0:T(8,128)(2,1)S(1)}, bf16[1,256,24,128]{3,2,1,0:T(8,128)(2,1)}, u32[]{:S(2)}) %copy-start) | copy-done | bytes 1572888
  2.0 1.2 %shard_map.84 = (bf16[256,3072]{1,0:T(8,128)(2,1)S(1)}, bf16[256,128]{1,0:T(8,128)(2,1)S(1)}) custom-call(bf16[1,256,24,128]{3,2,1,0:T(8,128)(2,1)S(1)} %copy-done), custom_call_target="tpu_custom_call" | custom-call | tf_op jit(solution)/shard_map/pallas_call | solution.py:555
  3.2 3.4 %collective-permute-start.1 = (bf16[256,128]{1,0:T(8,128)(2,1)S(1)}, bf16[256,128]{1,0:T(8,128)(2,1)S(1)}, u32[]{:S(2)}, u32[]{:S(2)}) collective-permute-start(bf16[256,128]{1,0:T(8,128)(2,1)S(1)} %get-tuple-element.38), channel_id=1, source_target_pairs={{4,8},{8,4},{0,12},{12,0},{5,9},{9,5},{1,13},{13,1},{6,10},{10,6},... | collective-permute-start | bytes 196616 | tf_op jit(solution)/shard_map/ppermute | solution.py:672
  6.6 0.0 collective-permute-start
  6.6 0.0 copy-start.4
  6.7 0.0 copy-start.2
  6.7 2.0 %shard_map.85 = (bf16[256,3840]{1,0:T(8,128)(2,1)S(1)}, bf16[64,256]{1,0:T(8,128)(2,1)S(1)}, bf16[192,192]{1,0:T(8,128)(2,1)S(1)}, bf16[192,192]{1,0:T(8,128)(2,...) custom-call(s32[2]{0:T(128)S(1)} %bitcast.20, ...), custom_call_target="tpu_custom_call" | custom-call | bytes 6000000 | tf_op jit(solution)/shard_map/pallas_call | solution.py:572
  8.7 0.1 pad_add_fusion.place
  8.8 0.0 collective-permute-done.1.odd_ref
  8.8 1.0 %collective-permute-done.even_ref = bf16[256,128]{1,0:T(8,128)(2,1)S(1)} collective-permute-done((bf16[256,128]{1,0:T(8,128)(2,1)S(1)}, bf16[256,128]{1,0:T(8,128)(2,1)S(1)}, u32[]{:S(2)}, u32[]{:S(2)}) %collective-permute-start) | collective-permute-done | bytes 65568 | tf_op jit(solution)/shard_map/ppermute | solution.py:671
  9.7 0.7 shard_map.86
  10.4 0.7 collective-permute-start.2
  11.1 4.3 %collective-permute-start.3 = (bf16[272,256]{1,0:T(8,128)(2,1)S(1)}, bf16[272,256]{1,0:T(8,128)(2,1)S(1)}, u32[]{:S(2)}, u32[]{:S(2)}) collective-permute-start(bf16[272,256]{1,0:T(8,128)(2,1)S(1)} %get-tuple-element.42), channel_id=1, source_target_pairs={{0,16},{16,0},{32,48},{48,32},{64,80},{80,64},{96,112},{112,96},{1... | collective-permute-start | bytes 417800 | tf_op jit(solution)/shard_map/ppermute | solution.py:676
  15.4 3.9 %shard_map.87 = (bf16[256,3328]{1,0:T(8,128)(2,1)S(1)}, bf16[64,3328]{1,0:T(8,128)(2,1)S(1)}, bf16[192,3072]{1,0:T(8,128)(2,1)S(1)}, bf16[64,2816]{1,0:T(8,128)(...) custom-call(s32[4]{0:T(128)S(1)} %pad_add_fusion.place, ...), custom_call_target="tpu_custom_call" | custom-call | flops 1000000000 | bytes 12000000 | tf_op jit(solution)/shard_map/pallas_call | solution.py:606
  19.3 0.0 collective-permute-done.3.even_ref
  19.3 11.2 %shard_map.88 = (f32[4,32,640]{2,1,0:T(8,128)S(1)}, f32[4,32,640]{2,1,0:T(8,128)S(1)}) custom-call(s32[4]{0:T(128)S(1)} %pad_add_fusion.place, bf16[256,3840]{1,0:T(8,128)(2,1)S(1)} %get-tuple-element.37.flat_ref, bf16[256,128]{1,0:T(8,128)(2,1)S(1)} %get-tuple-element.40.rim_ref, bf16[272,256]{1,0:T(8,128)(2,1)S(1)} %collective-permute-done.2.odd_ref, ...), custom_call_target="tpu_custom_call" | custom-call | tf_op jit(solution)/shard_map/pallas_call | solution.py:620
  30.5 2.8 %collective-permute-start.4 = (f32[4,32,640]{2,1,0:T(8,128)S(1)}, f32[4,32,640]{2,1,0:T(8,128)S(1)}, u32[]{:S(2)}, u32[]{:S(2)}) collective-permute-start(f32[4,32,640]{2,1,0:T(8,128)S(1)} %get-tuple-element.65), channel_id=1, source_target_pairs={{0,1},{1,0},{2,3},{3,2},{4,5},{5,4},{6,7},{7,6},{8,9},{9,8},{10,11... | collective-permute-start | bytes 983048 | tf_op jit(solution)/shard_map/ppermute | solution.py:76
  33.4 1.3 %collective-permute-done.4 = f32[4,32,640]{2,1,0:T(8,128)S(1)} collective-permute-done((f32[4,32,640]{2,1,0:T(8,128)S(1)}, f32[4,32,640]{2,1,0:T(8,128)S(1)}, u32[]{:S(2)}, u32[]{:S(2)}) %collective-permute-start.4) | collective-permute-done | bytes 327712 | tf_op jit(solution)/shard_map/ppermute | solution.py:76
  34.7 0.6 collective-permute-start.7
  35.3 1.8 %collective-permute-start.6 = (f32[32,640]{1,0:T(8,128)S(1)}, f32[32,640]{1,0:T(8,128)S(1)}, u32[]{:S(2)}, u32[]{:S(2)}) collective-permute-start(f32[32,640]{1,0:T(8,128)S(1)} %get-tuple-element.73), channel_id=1, source_target_pairs={{0,12},{4,8},{8,4},{12,0},{1,13},{5,9},{9,5},{13,1},{2,14},{6,10},... | collective-permute-start | bytes 245768 | tf_op jit(solution)/shard_map/ppermute | solution.py:76
  37.1 0.3 collective-permute-start.5
  37.4 2.5 %collective-permute-done.7 = f32[32,640]{1,0:T(8,128)S(1)} collective-permute-done((f32[32,640]{1,0:T(8,128)S(1)}, f32[32,640]{1,0:T(8,128)S(1)}, u32[]{:S(2)}, u32[]{:S(2)}) %collective-permute-start.7) | collective-permute-done | bytes 81952 | tf_op jit(solution)/shard_map/ppermute | solution.py:76
  39.9 2.5 %collective-permute-done.6 = f32[32,640]{1,0:T(8,128)S(1)} collective-permute-done((f32[32,640]{1,0:T(8,128)S(1)}, f32[32,640]{1,0:T(8,128)S(1)}, u32[]{:S(2)}, u32[]{:S(2)}) %collective-permute-start.6) | collective-permute-done | bytes 81952 | tf_op jit(solution)/shard_map/ppermute | solution.py:76
  42.4 2.7 %collective-permute-start.10 = (f32[32,640]{1,0:T(8,128)S(1)}, f32[32,640]{1,0:T(8,128)S(1)}, u32[]{:S(2)}, u32[]{:S(2)}) collective-permute-start(f32[32,640]{1,0:T(8,128)S(1)} %fusion.1), channel_id=1, source_target_pairs={{0,32},{16,48},{32,0},{48,16},{64,96},{80,112},{96,64},{112,80},{1... | collective-permute-start | bytes 245768 | tf_op jit(solution)/shard_map/ppermute | solution.py:76
  45.1 0.6 collective-permute-start.9
  45.7 1.6 %collective-permute-done.10 = f32[32,640]{1,0:T(8,128)S(1)} collective-permute-done((f32[32,640]{1,0:T(8,128)S(1)}, f32[32,640]{1,0:T(8,128)S(1)}, u32[]{:S(2)}, u32[]{:S(2)}) %collective-permute-start.10) | collective-permute-done | bytes 81952 | tf_op jit(solution)/shard_map/ppermute | solution.py:76
  47.3 2.3 %collective-permute-done.9 = f32[32,640]{1,0:T(8,128)S(1)} collective-permute-done((f32[32,640]{1,0:T(8,128)S(1)}, f32[32,640]{1,0:T(8,128)S(1)}, u32[]{:S(2)}, u32[]{:S(2)}) %collective-permute-start.9) | collective-permute-done | bytes 81952 | tf_op jit(solution)/shard_map/ppermute | solution.py:76
  49.6 0.0 collective-permute-done.8
  49.7 1.7 %collective-permute-start.11 = (f32[32,640]{1,0:T(8,128)S(1)}, f32[32,640]{1,0:T(8,128)S(1)}, u32[]{:S(2)}, u32[]{:S(2)}) collective-permute-start(f32[32,640]{1,0:T(8,128)S(1)} %add_add_fusion), channel_id=1, source_target_pairs={{0,64},{1,65},{2,66},{3,67},{16,80},{17,81},{18,82},{19,83},{32,96... | collective-permute-start | bytes 245768 | tf_op jit(solution)/shard_map/ppermute | solution.py:76
  51.4 1.8 %collective-permute-done.11 = f32[32,640]{1,0:T(8,128)S(1)} collective-permute-done((f32[32,640]{1,0:T(8,128)S(1)}, f32[32,640]{1,0:T(8,128)S(1)}, u32[]{:S(2)}, u32[]{:S(2)}) %collective-permute-start.11) | collective-permute-done | bytes 81952 | tf_op jit(solution)/shard_map/ppermute | solution.py:76
  53.2 8.0 %collective-permute-start.14 = (f32[32,640]{1,0:T(8,128)S(1)}, f32[32,640]{1,0:T(8,128)S(1)}, u32[]{:S(2)}, u32[]{:S(2)}) collective-permute-start(f32[32,640]{1,0:T(8,128)S(1)} %add.81.own), channel_id=1, source_target_pairs={{0,2},{1,3},{2,0},{3,1},{16,18},{17,19},{18,16},{19,17},{32,34},{3... | collective-permute-start | bytes 245768 | tf_op jit(solution)/shard_map/ppermute | solution.py:76
  61.2 0.0 collective-permute-start.13
  61.2 2.4 %collective-permute-start.12 = (f32[32,640]{1,0:T(8,128)S(1)}, f32[32,640]{1,0:T(8,128)S(1)}, u32[]{:S(2)}, u32[]{:S(2)}) collective-permute-start(f32[32,640]{1,0:T(8,128)S(1)} %add.81.own), channel_id=1, source_target_pairs={{0,192},{1,193},{2,194},{3,195},{16,208},{17,209},{18,210},{19,211... | collective-permute-start | bytes 245768 | tf_op jit(solution)/shard_map/ppermute | solution.py:76
  63.6 0.0 collective-permute-done.14.got_c
  63.6 3.2 %collective-permute-done.13.got_b = f32[32,640]{1,0:T(8,128)S(1)} collective-permute-done((f32[32,640]{1,0:T(8,128)S(1)}, f32[32,640]{1,0:T(8,128)S(1)}, u32[]{:S(2)}, u32[]{:S(2)}) %collective-permute-start.13) | collective-permute-done | bytes 81952 | tf_op jit(solution)/shard_map/ppermute | solution.py:76
  66.8 0.7 collective-permute-done.12.got_a
  67.5 0.6 shard_map.89
  68.1 3.3 %collective-permute-start.15 = (f32[1,640]{1,0:T(1,128)S(1)}, f32[1,640]{1,0:T(1,128)S(1)}, u32[]{:S(2)}, u32[]{:S(2)}) collective-permute-start(f32[1,640]{1,0:T(1,128)S(1)} %get-tuple-element.67), channel_id=1, source_target_pairs={{0,1},{1,0},{2,3},{3,2},{4,5},{5,4},{6,7},{7,6},{8,9},{9,8},{10,11... | collective-permute-start | bytes 7688 | tf_op jit(solution)/shard_map/ppermute | solution.py:76
  71.4 0.8 %collective-permute-done.15 = f32[1,640]{1,0:T(1,128)S(1)} collective-permute-done((f32[1,640]{1,0:T(1,128)S(1)}, f32[1,640]{1,0:T(1,128)S(1)}, u32[]{:S(2)}, u32[]{:S(2)}) %collective-permute-start.15) | collective-permute-done | bytes 2592 | tf_op jit(solution)/shard_map/ppermute | solution.py:76
  72.2 1.0 %collective-permute-start.18 = (f32[1,640]{1,0:T(1,128)S(1)}, f32[1,640]{1,0:T(1,128)S(1)}, u32[]{:S(2)}, u32[]{:S(2)}) collective-permute-start(f32[1,640]{1,0:T(1,128)S(1)} %add.82), channel_id=1, source_target_pairs={{0,8},{4,12},{8,0},{12,4},{1,9},{5,13},{9,1},{13,5},{2,10},{6,14},... | collective-permute-start | bytes 7688 | tf_op jit(solution)/shard_map/ppermute | solution.py:76
  73.2 1.4 %collective-permute-start.17 = (f32[1,640]{1,0:T(1,128)S(1)}, f32[1,640]{1,0:T(1,128)S(1)}, u32[]{:S(2)}, u32[]{:S(2)}) collective-permute-start(f32[1,640]{1,0:T(1,128)S(1)} %add.82), channel_id=1, source_target_pairs={{0,12},{4,8},{8,4},{12,0},{1,13},{5,9},{9,5},{13,1},{2,14},{6,10},... | collective-permute-start | bytes 7688 | tf_op jit(solution)/shard_map/ppermute | solution.py:76
  74.6 0.3 collective-permute-start.16
  74.9 0.6 multiply_add_fusion
  75.5 0.6 slice.27
  76.7 0.0 collective-permute-done.18
  76.7 0.4 collective-permute-done.17
  77.1 0.1 collective-permute-done.16
  77.3 0.7 multiply_subtract_fusion
  (20 shorter events, 0.2 us)
Async XLA Ops:
  0.6 1.4 %copy-start = (bf16[1,256,24,128]{3,2,1,0:T(8,128)(2,1)S(1)}, bf16[1,256,24,128]{3,2,1,0:T(8,128)(2,1)}, u32[]{:S(2)}) copy-start(bf16[1,256,24,128]{3,2,1,0:T(8,128)(2,1)} %image_ref.1) | copy-start | bytes 4718596
  2.0 4.6 %copy-start.1 = (f32[141312]{0:T(1024)S(1)}, f32[141312]{0:T(1024)}, u32[]{:S(2)}) copy-start(f32[141312]{0:T(1024)} %param.7) | copy-start | bytes 1695748
  2.0 4.6 %copy-start.3 = (s32[1,1,2]{2,1,0:T(1,128)S(1)}, s32[1,1,2]{2,1,0:T(1,128)}, u32[]{:S(2)}) copy-start(s32[1,1,2]{2,1,0:T(1,128)} %param.6) | copy-start | bytes 28
  3.2 5.5 %collective-permute-start.1 = (bf16[256,128]{1,0:T(8,128)(2,1)S(1)}, bf16[256,128]{1,0:T(8,128)(2,1)S(1)}, u32[]{:S(2)}, u32[]{:S(2)}) collective-permute-start(bf16[256,128]{1,0:T(8,128)(2,1)S(1)} %get-tuple-element.38), channel_id=1, source_target_pairs={{4,8},{8,4},{0,12},{12,0},{5,9},{9,5},{1,13},{13,1},{6,10},{10,6},... | collective-permute-start | bytes 196616 | tf_op jit(solution)/shard_map/ppermute | solution.py:672
  6.6 3.1 %collective-permute-start = (bf16[256,128]{1,0:T(8,128)(2,1)S(1)}, bf16[256,128]{1,0:T(8,128)(2,1)S(1)}, u32[]{:S(2)}, u32[]{:S(2)}) collective-permute-start(bf16[256,128]{1,0:T(8,128)(2,1)S(1)} %get-tuple-element.38), channel_id=1, source_target_pairs={{0,4},{4,0},{8,12},{12,8},{1,5},{5,1},{9,13},{13,9},{2,6},{6,2},{1... | collective-permute-start | bytes 196616 | tf_op jit(solution)/shard_map/ppermute | solution.py:671
  6.6 8.7 %copy-start.4 = (f32[552]{0:T(1024)S(1)}, f32[552]{0:T(1024)}, u32[]{:S(2)}) copy-start(f32[552]{0:T(1024)} %param.8) | copy-start | bytes 6628
  6.7 8.7 %copy-start.2 = (f32[8,3840]{1,0:T(8,128)S(1)}, f32[8,3840]{1,0:T(8,128)}, u32[]{:S(2)}) copy-start(f32[8,3840]{1,0:T(8,128)} %constant.67.clone.table) | copy-start | bytes 368644
  10.4 8.8 %collective-permute-start.2 = (bf16[272,256]{1,0:T(8,128)(2,1)S(1)}, bf16[272,256]{1,0:T(8,128)(2,1)S(1)}, u32[]{:S(2)}, u32[]{:S(2)}) collective-permute-start(bf16[272,256]{1,0:T(8,128)(2,1)S(1)} %get-tuple-element.41), channel_id=1, source_target_pairs={{16,32},{32,16},{48,64},{64,48},{80,96},{96,80},{112,128},{128,112... | collective-permute-start | bytes 417800 | tf_op jit(solution)/shard_map/ppermute | solution.py:675
  11.1 8.2 %collective-permute-start.3 = (bf16[272,256]{1,0:T(8,128)(2,1)S(1)}, bf16[272,256]{1,0:T(8,128)(2,1)S(1)}, u32[]{:S(2)}, u32[]{:S(2)}) collective-permute-start(bf16[272,256]{1,0:T(8,128)(2,1)S(1)} %get-tuple-element.42), channel_id=1, source_target_pairs={{0,16},{16,0},{32,48},{48,32},{64,80},{80,64},{96,112},{112,96},{1... | collective-permute-start | bytes 417800 | tf_op jit(solution)/shard_map/ppermute | solution.py:676
  30.5 4.1 %collective-permute-start.4 = (f32[4,32,640]{2,1,0:T(8,128)S(1)}, f32[4,32,640]{2,1,0:T(8,128)S(1)}, u32[]{:S(2)}, u32[]{:S(2)}) collective-permute-start(f32[4,32,640]{2,1,0:T(8,128)S(1)} %get-tuple-element.65), channel_id=1, source_target_pairs={{0,1},{1,0},{2,3},{3,2},{4,5},{5,4},{6,7},{7,6},{8,9},{9,8},{10,11... | collective-permute-start | bytes 983048 | tf_op jit(solution)/shard_map/ppermute | solution.py:76
  34.7 5.2 %collective-permute-start.7 = (f32[32,640]{1,0:T(8,128)S(1)}, f32[32,640]{1,0:T(8,128)S(1)}, u32[]{:S(2)}, u32[]{:S(2)}) collective-permute-start(f32[32,640]{1,0:T(8,128)S(1)} %get-tuple-element.72), channel_id=1, source_target_pairs={{0,8},{4,12},{8,0},{12,4},{1,9},{5,13},{9,1},{13,5},{2,10},{6,14},... | collective-permute-start | bytes 245768 | tf_op jit(solution)/shard_map/ppermute | solution.py:76
  35.3 7.1 %collective-permute-start.6 = (f32[32,640]{1,0:T(8,128)S(1)}, f32[32,640]{1,0:T(8,128)S(1)}, u32[]{:S(2)}, u32[]{:S(2)}) collective-permute-start(f32[32,640]{1,0:T(8,128)S(1)} %get-tuple-element.73), channel_id=1, source_target_pairs={{0,12},{4,8},{8,4},{12,0},{1,13},{5,9},{9,5},{13,1},{2,14},{6,10},... | collective-permute-start | bytes 245768 | tf_op jit(solution)/shard_map/ppermute | solution.py:76
  37.1 5.3 %collective-permute-start.5 = (f32[32,640]{1,0:T(8,128)S(1)}, f32[32,640]{1,0:T(8,128)S(1)}, u32[]{:S(2)}, u32[]{:S(2)}) collective-permute-start(f32[32,640]{1,0:T(8,128)S(1)} %get-tuple-element.74), channel_id=1, source_target_pairs={{0,4},{4,0},{8,12},{12,8},{1,5},{5,1},{9,13},{13,9},{2,6},{6,2},{1... | collective-permute-start | bytes 245768 | tf_op jit(solution)/shard_map/ppermute | solution.py:76
  42.4 4.9 %collective-permute-start.10 = (f32[32,640]{1,0:T(8,128)S(1)}, f32[32,640]{1,0:T(8,128)S(1)}, u32[]{:S(2)}, u32[]{:S(2)}) collective-permute-start(f32[32,640]{1,0:T(8,128)S(1)} %fusion.1), channel_id=1, source_target_pairs={{0,32},{16,48},{32,0},{48,16},{64,96},{80,112},{96,64},{112,80},{1... | collective-permute-start | bytes 245768 | tf_op jit(solution)/shard_map/ppermute | solution.py:76
  45.1 4.5 %collective-permute-start.9 = (f32[32,640]{1,0:T(8,128)S(1)}, f32[32,640]{1,0:T(8,128)S(1)}, u32[]{:S(2)}, u32[]{:S(2)}) collective-permute-start(f32[32,640]{1,0:T(8,128)S(1)} %fusion.1), channel_id=1, source_target_pairs={{0,48},{16,32},{32,16},{48,0},{64,112},{80,96},{96,80},{112,64},{1... | collective-permute-start | bytes 245768 | tf_op jit(solution)/shard_map/ppermute | solution.py:76
  45.7 3.9 %collective-permute-start.8 = (f32[32,640]{1,0:T(8,128)S(1)}, f32[32,640]{1,0:T(8,128)S(1)}, u32[]{:S(2)}, u32[]{:S(2)}) collective-permute-start(f32[32,640]{1,0:T(8,128)S(1)} %fusion.1), channel_id=1, source_target_pairs={{0,16},{16,0},{32,48},{48,32},{64,80},{80,64},{96,112},{112,96},{1... | collective-permute-start | bytes 245768 | tf_op jit(solution)/shard_map/ppermute | solution.py:76
  49.7 3.6 %collective-permute-start.11 = (f32[32,640]{1,0:T(8,128)S(1)}, f32[32,640]{1,0:T(8,128)S(1)}, u32[]{:S(2)}, u32[]{:S(2)}) collective-permute-start(f32[32,640]{1,0:T(8,128)S(1)} %add_add_fusion), channel_id=1, source_target_pairs={{0,64},{1,65},{2,66},{3,67},{16,80},{17,81},{18,82},{19,83},{32,96... | collective-permute-start | bytes 245768 | tf_op jit(solution)/shard_map/ppermute | solution.py:76
  53.2 10.4 %collective-permute-start.14 = (f32[32,640]{1,0:T(8,128)S(1)}, f32[32,640]{1,0:T(8,128)S(1)}, u32[]{:S(2)}, u32[]{:S(2)}) collective-permute-start(f32[32,640]{1,0:T(8,128)S(1)} %add.81.own), channel_id=1, source_target_pairs={{0,2},{1,3},{2,0},{3,1},{16,18},{17,19},{18,16},{19,17},{32,34},{3... | collective-permute-start | bytes 245768 | tf_op jit(solution)/shard_map/ppermute | solution.py:76
  61.2 5.5 %collective-permute-start.13 = (f32[32,640]{1,0:T(8,128)S(1)}, f32[32,640]{1,0:T(8,128)S(1)}, u32[]{:S(2)}, u32[]{:S(2)}) collective-permute-start(f32[32,640]{1,0:T(8,128)S(1)} %add.81.own), channel_id=1, source_target_pairs={{0,194},{1,195},{2,192},{3,193},{16,210},{17,211},{18,208},{19,209... | collective-permute-start | bytes 245768 | tf_op jit(solution)/shard_map/ppermute | solution.py:76
  61.2 6.2 %collective-permute-start.12 = (f32[32,640]{1,0:T(8,128)S(1)}, f32[32,640]{1,0:T(8,128)S(1)}, u32[]{:S(2)}, u32[]{:S(2)}) collective-permute-start(f32[32,640]{1,0:T(8,128)S(1)} %add.81.own), channel_id=1, source_target_pairs={{0,192},{1,193},{2,194},{3,195},{16,208},{17,209},{18,210},{19,211... | collective-permute-start | bytes 245768 | tf_op jit(solution)/shard_map/ppermute | solution.py:76
  68.1 4.1 %collective-permute-start.15 = (f32[1,640]{1,0:T(1,128)S(1)}, f32[1,640]{1,0:T(1,128)S(1)}, u32[]{:S(2)}, u32[]{:S(2)}) collective-permute-start(f32[1,640]{1,0:T(1,128)S(1)} %get-tuple-element.67), channel_id=1, source_target_pairs={{0,1},{1,0},{2,3},{3,2},{4,5},{5,4},{6,7},{7,6},{8,9},{9,8},{10,11... | collective-permute-start | bytes 7688 | tf_op jit(solution)/shard_map/ppermute | solution.py:76
  72.2 4.5 %collective-permute-start.18 = (f32[1,640]{1,0:T(1,128)S(1)}, f32[1,640]{1,0:T(1,128)S(1)}, u32[]{:S(2)}, u32[]{:S(2)}) collective-permute-start(f32[1,640]{1,0:T(1,128)S(1)} %add.82), channel_id=1, source_target_pairs={{0,8},{4,12},{8,0},{12,4},{1,9},{5,13},{9,1},{13,5},{2,10},{6,14},... | collective-permute-start | bytes 7688 | tf_op jit(solution)/shard_map/ppermute | solution.py:76
  73.2 3.9 %collective-permute-start.17 = (f32[1,640]{1,0:T(1,128)S(1)}, f32[1,640]{1,0:T(1,128)S(1)}, u32[]{:S(2)}, u32[]{:S(2)}) collective-permute-start(f32[1,640]{1,0:T(1,128)S(1)} %add.82), channel_id=1, source_target_pairs={{0,12},{4,8},{8,4},{12,0},{1,13},{5,9},{9,5},{13,1},{2,14},{6,10},... | collective-permute-start | bytes 7688 | tf_op jit(solution)/shard_map/ppermute | solution.py:76
  74.6 2.7 %collective-permute-start.16 = (f32[1,640]{1,0:T(1,128)S(1)}, f32[1,640]{1,0:T(1,128)S(1)}, u32[]{:S(2)}, u32[]{:S(2)}) collective-permute-start(f32[1,640]{1,0:T(1,128)S(1)} %add.82), channel_id=1, source_target_pairs={{0,4},{4,0},{8,12},{12,8},{1,5},{5,1},{9,13},{13,9},{2,6},{6,2},{1... | collective-permute-start | bytes 7688 | tf_op jit(solution)/shard_map/ppermute | solution.py:76

commit v5 on v4

--- a/solution.py
+++ b/solution.py
@@ -23,6 +23,7 @@
 GUARD = 256
 WIDE = LANES + 2 * GUARD
 CHUNK = 768
+PIECE = 1024
 INNER, OUTER = CHUNK, LANES - CHUNK
 
 BF = jnp.bfloat16
@@ -67,7 +68,7 @@
 Z_PAIR = (("row", "dp"), [along_z(lambda z: z ^ 1)])
 Z_RING = (
     ("row", "dp"),
-    [along_z(z_near), along_z(lambda z: 7 - z), along_z(lambda z: z_near(7 - z))],
+    [along_z(z_near), along_z(lambda z: 7 - z), along_z(lambda z: z ^ 5)],
 )
 
 
@@ -97,11 +98,11 @@
 ALL_ROWS = slice(None)
 
 
-def cut(start, stop, most=CHUNK):
-    tiles = (stop - start) // 128
-    count = -(-tiles // (most // 128))
-    edges = [start + tiles * k // count * 128 for k in range(count + 1)]
-    return list(zip(edges[:-1], edges[1:]))
+def cut(start, stop):
+    edges = list(range(start, stop, PIECE))
+    if len(edges) > 1 and stop - edges[-1] <= 256:
+        edges.pop()
+    return list(zip(edges, edges[1:] + [stop]))
 
 
 class Lanes:
@@ -144,11 +145,18 @@
     edge_ref[...] = nn(own_ref[...], select[...]).astype(BF)
 
 
+def spots(count, table, k, start, stop):
+    source = lax.broadcasted_iota(jnp.int32, (count, stop - start), 0).astype(F32)
+    return (source == table[k : k + 1, start:stop]).astype(F32).astype(BF)
+
+
 def prepare_kernel(
     labels,
     own_ref,
     weights_ref,
+    table,
     flat_ref,
+    spot_ref,
     win_t1,
     wf1,
     wb1,
@@ -201,6 +209,8 @@
             1088:1104, j * CLASSES : (j + 1) * CLASSES
         ]
     head_ref[...] = tall[:, 0:CLASSES]
+    for start, stop in cut(0, LANES):
+        spot_ref[:, start:stop] = spots(128, table, 3, start, stop)
     line = lax.broadcasted_iota(jnp.int32, (8, CLASSES), 0)
     label = jnp.where(line == 0, labels[0], labels[1])
     target_ref[...] = (lax.broadcasted_iota(jnp.int32, (8, CLASSES), 1) == label).astype(F32)
@@ -227,11 +237,6 @@
         ref[C:, :] = nt(pick, rim).astype(BF)
 
 
-def placed(rim, table, k, start, stop):
-    source = lax.broadcasted_iota(jnp.int32, (rim.shape[1], stop - start), 0).astype(F32)
-    return nn(rim, (source == table[k : k + 1, start:stop]).astype(F32).astype(BF))
-
-
 def in_image(place, table, start, stop):
     row, col = place[0], place[1]
     r, c = table[6:7, start:stop], table[7:8, start:stop]
@@ -243,27 +248,39 @@
     return jnp.where(inside, table[2:3, start:stop], 0.0)
 
 
+def emit(phases):
+    for pieces, work in phases:
+        for start, stop in pieces:
+            work(start, stop)
+
+
 def enter(inputs, win_t, h1, ranges, mask):
-    for start, stop in ranges:
+    def work(start, stop):
         value = jnp.maximum(nn(win_t[...], inputs.get(start, stop)).astype(BF), ZERO)
         if mask is not None:
             value = value * mask(start, stop).astype(BF)
         h1.put(start, stop, value)
 
+    return ranges, work
+
 
 def spread(h1, hs, ranges):
-    for start, stop in ranges:
+    def work(start, stop):
         for s in range(3):
             hs.put(start, stop, h1.shifted(start, stop, s - 1), slice(s * MID, (s + 1) * MID))
 
+    return ranges, work
+
 
 def widen(wf, hs, wide, ranges):
-    for start, stop in ranges:
+    def work(start, stop):
         wide.put(start, stop, nn(wf[...], hs.get(start, stop)))
 
+    return ranges, work
+
 
 def leave(inputs, wide, wout_t, h2, output, ranges):
-    for start, stop in ranges:
+    def work(start, stop):
         total = sum(
             wide.shifted(start, stop, (r - 1) * COLS, slice(r * MID, (r + 1) * MID))
             for r in range(3)
@@ -273,6 +290,8 @@
         total = nn(wout_t[...], value) + inputs.get(start, stop).astype(F32)
         output.put(start, stop, jnp.maximum(total.astype(BF), ZERO))
 
+    return ranges, work
+
 
 X_SPAN = (INNER - 512, OUTER + 512)
 HS1_SPAN = (INNER - 384, OUTER + 384)
@@ -283,6 +302,7 @@
 def inner_kernel(
     place,
     flat_ref,
+    spot_ref,
     rim_ref,
     table,
     win_t1,
@@ -312,23 +332,33 @@
     wide_ref[:, wide_ref.shape[1] - 128 :] = jnp.zeros((3 * MID, 128), F32)
     h1b_ref[:, 0:128] = jnp.zeros((MID, 128), BF)
     h1b_ref[:, h1b_ref.shape[1] - 128 :] = jnp.zeros((MID, 128), BF)
-    for start, stop in cut(*X_SPAN):
-        value = placed(rim_ref[...], table, 3, start, stop) + flat_ref[:, start:stop].astype(F32)
+
+    def lay_out(start, stop):
+        value = nn(rim_ref[...], spot_ref[:, start:stop]) + flat_ref[:, start:stop].astype(F32)
         x.put(start, stop, value.astype(BF))
-    enter(x, win_t1, h1a, cut(*X_SPAN), None)
-    spread(h1a, hs1, cut(*HS1_SPAN))
-    widen(wf1, hs1, wide, cut(*HS1_SPAN))
-    leave(x, wide, wout_t1, h2a, y1, cut(*Y1_SPAN))
+
     mask = lambda start, stop: in_image(place, table, start, stop)
-    enter(y1, win_t2, h1b, cut(*Y1_SPAN), mask)
-    spread(h1b, hs2, cut(*Y1_SPAN))
-    widen(wf2, hs2, wide, cut(*Y1_SPAN))
-    leave(y1, wide, wout_t2, h2b, y2, cut(*Y2_SPAN))
+    x_pieces, hs1_pieces = cut(*X_SPAN), cut(*HS1_SPAN)
+    y1_pieces, y2_pieces = cut(*Y1_SPAN), cut(*Y2_SPAN)
+    emit(
+        [
+            (x_pieces, lay_out),
+            enter(x, win_t1, h1a, x_pieces, None),
+            spread(h1a, hs1, hs1_pieces),
+            widen(wf1, hs1, wide, hs1_pieces),
+            leave(x, wide, wout_t1, h2a, y1, y1_pieces),
+            enter(y1, win_t2, h1b, y1_pieces, mask),
+            spread(h1b, hs2, y1_pieces),
+            widen(wf2, hs2, wide, y1_pieces),
+            leave(y1, wide, wout_t2, h2b, y2, y2_pieces),
+        ]
+    )
 
 
 def kernel(
     place,
     flat_ref,
+    spot_ref,
     rim_ref,
     odd_ref,
     even_ref,
@@ -404,9 +434,9 @@
     above = jnp.where(odd_row, even_ref[...].astype(F32), odd_ref[...].astype(F32)).astype(BF)
     below = jnp.where(odd_row, odd_ref[...].astype(F32), even_ref[...].astype(F32)).astype(BF)
     for end, start, stop, k, rows in ((0, 0, INNER, 4, above), (1, OUTER, LANES, 5, below)):
-        value = placed(rim_ref[...], table, 3, start, stop) + flat_ref[:, start:stop].astype(F32)
+        value = nn(rim_ref[...], spot_ref[:, start:stop]) + flat_ref[:, start:stop].astype(F32)
         corners = rows[C:, :].astype(F32).T.astype(BF)
-        value = value + placed(corners, table, k, start, stop)
+        value = value + nn(corners, spots(CORNERS, table, k, start, stop))
         x_ends[end] = value.astype(BF)
         for r in range(HALO):
             lane = (r if end == 0 else ROWS - HALO + r) * COLS + HALO - start
@@ -414,20 +444,28 @@
     ends = [(0, INNER), (OUTER, LANES)]
     wider = [(0, INNER + 256), (OUTER - 256, LANES)]
     mask = lambda start, stop: in_image(place, table, start, stop)
-    enter(x, win_t1, h1a, ends, None)
-    spread(h1a, hs1, ends)
-    widen(wf1, hs1, wide, wider)
-    leave(x, wide, wout_t1, h2a, y1, ends)
-    enter(y1, win_t2, h1b, ends, mask)
-    spread(h1b, hs2, ends)
-    widen(wf2, hs2, wide, wider)
-    leave(y1, wide, wout_t2, h2b, y2, ends)
-
     everything = cut(0, LANES)
-    assert (0, INNER) in everything and (OUTER, LANES) in everything
-    pooled = sum(
-        nt(y2.get(start, stop), table[:, start:stop].astype(BF)) for start, stop in everything
-    ) * (1.0 / (TILE_ROWS * TILE_COLS))
+    sums = {"pooled": jnp.zeros((C, 8), F32)}
+
+    def pool(start, stop):
+        sums["pooled"] += nt(y2.get(start, stop), table[:, start:stop].astype(BF))
+
+    for start, stop in cut(INNER, OUTER):
+        pool(start, stop)
+    emit(
+        [
+            enter(x, win_t1, h1a, ends, None),
+            spread(h1a, hs1, ends),
+            widen(wf1, hs1, wide, wider),
+            leave(x, wide, wout_t1, h2a, y1, ends),
+            enter(y1, win_t2, h1b, ends, mask),
+            spread(h1b, hs2, ends),
+            widen(wf2, hs2, wide, wider),
+            leave(y1, wide, wout_t2, h2b, y2, ends),
+            (ends, pool),
+        ]
+    )
+    pooled = sums["pooled"] * (1.0 / (TILE_ROWS * TILE_COLS))
     head = head_ref[...]
     loss = jnp.zeros((1, 1), F32)
     grad_head = jnp.zeros((C, CLASSES), F32)
@@ -444,12 +482,12 @@
         dpooled = jnp.sum(head * dlogits, axis=1, keepdims=True) / (TILE_ROWS * TILE_COLS)
         upstream.append(dpooled.astype(BF))
 
-    own = [(256, 1024), (1024, 1792), (1792, 2560), (2560, 3584)]
-    one = [(0, 768), (768, 1536), (1536, 2304), (2304, 3072), (3072, 3584)]
+    own, one = cut(256, 3584), cut(0, 3584)
     dz[:, 0:256] = jnp.zeros((C, 256), BF)
     dg2_ref[:, GUARD : GUARD + 256] = jnp.zeros((MID, 256), BF)
     dg2_ref[:, GUARD + 3584 :] = jnp.zeros((MID, LANES - 3584 + GUARD), BF)
-    for start, stop in own:
+
+    def seed(start, stop):
         first, second = (table[t : t + 1, start:stop].astype(BF) for t in range(2))
         value = upstream[0] * first + upstream[1] * second
         dz[:, start:stop] = jnp.where(y2.get(start, stop) > ZERO, value, ZERO)
@@ -462,40 +500,51 @@
         packed[row : row + half, MID:] = tall[pl.ds(1, half, stride=2), :]
 
     def backward(inputs, wb, wout, h1, hs, h2, row, then, near, far):
-        grad_out = jnp.zeros((C, MID), F32)
-        for start, stop in near:
+        grads = {
+            "out": jnp.zeros((C, MID), F32),
+            "mid": jnp.zeros((3 * MID, 3 * MID), F32),
+            "in": jnp.zeros((C, MID), F32),
+        }
+
+        def to_mid(start, stop):
             value = dz[:, start:stop]
-            grad_out = grad_out + nt(value, h2.get(start, stop))
+            grads["out"] += nt(value, h2.get(start, stop))
             value = nn(wout[...], value).astype(BF)
             dg2.put(start, stop, jnp.where(h2.get(start, stop) > ZERO, value, ZERO))
-        grad_out = grad_out.T
-        packed[pl.ds(row + 416, MID, stride=2), :] = grad_out[:, :128]
-        packed[pl.ds(row + 417, MID, stride=2), :] = grad_out[:, 128:]
-        grad_mid = jnp.zeros((3 * MID, 3 * MID), F32)
-        for start, stop in far:
+            if (start, stop) == near[-1]:
+                total = grads["out"].T
+                packed[pl.ds(row + 416, MID, stride=2), :] = total[:, :128]
+                packed[pl.ds(row + 417, MID, stride=2), :] = total[:, 128:]
+
+        def through_taps(start, stop):
             for r in range(3):
                 ds[r * MID : (r + 1) * MID, start:stop] = dg2.shifted(start, stop, (1 - r) * COLS)
             value = ds[:, start:stop]
             wide.put(start, stop, nn(wb[...], value))
-            grad_mid = grad_mid + nt(hs.get(start, stop), value)
-        for r in range(3):
-            pack_tall(grad_mid[:, r * MID : (r + 1) * MID], row + 128 + r * 96)
-        grad_in = jnp.zeros((C, MID), F32)
-        for start, stop in far:
+            grads["mid"] += nt(hs.get(start, stop), value)
+            if (start, stop) == far[-1]:
+                for r in range(3):
+                    pack_tall(grads["mid"][:, r * MID : (r + 1) * MID], row + 128 + r * 96)
+
+        def to_inputs(start, stop):
             total = sum(
                 wide.shifted(start, stop, 1 - s, slice(s * MID, (s + 1) * MID)) for s in range(3)
             )
             value = jnp.where(h1.get(start, stop) > ZERO, total.astype(BF), ZERO)
-            grad_in = grad_in + nt(inputs.get(start, stop), value)
+            grads["in"] += nt(inputs.get(start, stop), value)
             if then is not None:
                 then(start, stop, value)
-        pack_tall(grad_in, row)
+            if (start, stop) == far[-1]:
+                pack_tall(grads["in"], row)
+                if then is not None:
+                    pack_shares(8)
+
+        return [(near, to_mid), (far, through_taps), (far, to_inputs)]
 
     def to_first(start, stop, value):
         total = nn(win2[...], value) + dz[:, start:stop].astype(F32)
         dz[:, start:stop] = jnp.where(y1.get(start, stop) > ZERO, total.astype(BF), ZERO)
 
-    backward(y1, wb2, wout2, h1b, hs2, h2b, 544, to_first, own, one)
     tall[:, 0:CLASSES] = grad_head
     for j in range(16):
         packed[1088:1104, j * CLASSES : (j + 1) * CLASSES] = tall[
@@ -521,8 +570,11 @@
                 begin = m_far * 16 + low
                 block[begin : begin + 8, j * 128 : (j + 1) * 128] = value
 
-    pack_shares(8)
-    backward(x, wb1, wout1, h1a, hs1, h2a, 0, None, one, everything)
+    emit(
+        [(own, seed)]
+        + backward(y1, wb2, wout2, h1b, hs2, h2b, 544, to_first, own, one)
+        + backward(x, wb1, wout1, h1a, hs1, h2a, 0, None, one, everything)
+    )
 
     pack_shares(0)
     mine = far * 16 + row
@@ -565,19 +617,19 @@
     )(image)
 
 
-def prepare(labels, own, weights):
+def prepare(labels, own, weights, table):
     square = shape((3 * MID, 3 * MID), BF)
     down, up = shape((MID, C), BF), shape((C, MID), BF)
     block = [down, square, square, up, down]
     return pl.pallas_call(
         prepare_kernel,
-        out_shape=[shape((C, LANES), BF)] + block + block + [up, shape((C, CLASSES), F32), shape((8, CLASSES), F32)],
-        in_specs=[SMEM] + [VMEM] * 2,
-        out_specs=[VMEM] * 14,
+        out_shape=[shape((C, LANES), BF), shape((128, LANES), BF)] + block + block + [up, shape((C, CLASSES), F32), shape((8, CLASSES), F32)],
+        in_specs=[SMEM] + [VMEM] * 3,
+        out_specs=[VMEM] * 15,
         scratch_shapes=[pltpu.VMEM((C, MID), F32)],
         compiler_params=PARAMS,
         cost_estimate=pl.CostEstimate(flops=0, bytes_accessed=6_000_000, transcendentals=0),
-    )(labels, own, weights.reshape(PARAM // 128, 128))
+    )(labels, own, weights.reshape(PARAM // 128, 128), table)
 
 
 def rim(place, own, even, odd, after):
@@ -590,7 +642,7 @@
     )(place, own, even, odd, after)
 
 
-def inner(place, flat, beyond, table, mats):
+def inner(place, flat, spot, beyond, table, mats):
     win_t1, wf1, _, wout_t1, _, win_t2, wf2, _, wout_t2 = mats[:9]
     spans = [
         (C, X_SPAN),
@@ -606,21 +658,21 @@
     return pl.pallas_call(
         inner_kernel,
         out_shape=[shape((rows, stop - start), BF) for rows, (start, stop) in spans],
-        in_specs=[SMEM] + [VMEM] * 9,
+        in_specs=[SMEM] + [VMEM] * 10,
         out_specs=[VMEM] * 9,
         scratch_shapes=[pltpu.VMEM((3 * MID, X_SPAN[1] - X_SPAN[0]), F32)],
         compiler_params=PARAMS,
         cost_estimate=pl.CostEstimate(
             flops=1_000_000_000, bytes_accessed=12_000_000, transcendentals=0
         ),
-    )(place, flat, beyond, table, win_t1, wf1, wout_t1, win_t2, wf2, wout_t2)
-
-
-def compute(place, flat, beyond, odd, even, table, momentum, mats, mids):
+    )(place, flat, spot, beyond, table, win_t1, wf1, wout_t1, win_t2, wf2, wout_t2)
+
+
+def compute(place, flat, spot, beyond, odd, even, table, momentum, mats, mids):
     return pl.pallas_call(
         kernel,
         out_shape=(shape((4, SHARES, PAD), F32), shape((4, SHARES, PAD), F32)),
-        in_specs=[SMEM] + [VMEM] * 28,
+        in_specs=[SMEM] + [VMEM] * 29,
         out_specs=(VMEM, VMEM),
         scratch_shapes=[
             pltpu.VMEM((PARAM // 128 + 8, 128), F32),
@@ -641,7 +693,7 @@
             pltpu.VMEM((C, MID), F32),
         ],
         compiler_params=PARAMS,
-    )(place, flat, beyond, odd, even, table, momentum, *mats, *mids)
+    )(place, flat, spot, beyond, odd, even, table, momentum, *mats, *mids)
 
 
 def make_table():
@@ -670,13 +722,13 @@
     own, edge = split(image)
     even = lax.ppermute(edge, "col", neighbours(4, False))
     odd = lax.ppermute(edge, "col", neighbours(4, True, True))
-    flat, *mats = prepare(labels.reshape(2), own, weights)
+    flat, spot, *mats = prepare(labels.reshape(2), own, weights, table)
     beyond, up, down = rim(place, own, even, odd, mats[-1])
     odd = lax.ppermute(down, "row", neighbours(16, True))
     even = lax.ppermute(up, "row", neighbours(16, False))
-    mids = inner(place, flat, beyond, table, mats)
+    mids = inner(place, flat, spot, beyond, table, mats)
     keep, send = compute(
-        place, flat, beyond, odd, even, table, padded_momentum, mats, mids
+        place, flat, spot, beyond, odd, even, table, padded_momentum, mats, mids
     )
 
     parts = keep + received([send], CORE)[0]

time: 80 us -> 78.1 us (0.976)
  starting transfers between devices: 35.2 us -> 33.9 us
  waiting for transfers between devices: 18.2 us -> 19.1 us
    ppermute x15, starting transfers between devices: 26.9 us -> 25.5 us  [received(): lax.ppermute(value, axis, pairs)]
    ppermute x15, waiting for transfers between devices: 17.2 us -> 18.3 us  [received(): lax.ppermute(value, axis, pairs)]
    pallas_call x1, Pallas kernels: 11.2 us -> 10.4 us  [compute(): pl.pallas_call(kernel, out_shape=(shape((4, SHARES, PAD), F32), shape((4,...]
  transfers between devices with their start and end apart: 19 -> 19, of which waited for: 12 -> 11; matrix products, arithmetic and copies ran while one was open for 2% -> 2% of each run, Pallas kernels for 7% -> 8%
where the time goes in v5:
time: 78.1 us; the launch traced here: 78 us
  starting transfers between devices  33.9 us (43%)
  waiting for transfers between devices  19.1 us (24%)
  Pallas kernels  19 us (24%)
  between operations  2.56 us (3%)
  local copies, waits for them, and re-layouts  2.03 us (3%)
  other arithmetic  1.49 us (2%)
    ppermute x15, starting transfers between devices, received(): lax.ppermute(value, axis, pairs)  25.5 us
    ppermute x15, waiting for transfers between devices, received(): lax.ppermute(value, axis, pairs)  18.3 us
    pallas_call x1, Pallas kernels, compute(): pl.pallas_call(kernel, out_shape=(shape((4, SHARES, PAD), F32), shape((4,...  10.4 us
    ppermute x1, starting transfers between devices, local(): even = lax.ppermute(up, 'row', neighbours(16, False))  4.26 us
    pallas_call x1, Pallas kernels, inner(): pl.pallas_call(inner_kernel, out_shape=[shape((rows, stop - start), BF) f...  3.83 us
    ppermute x1, starting transfers between devices, local(): odd = lax.ppermute(edge, 'col', neighbours(4, True, True))  3.39 us
    pallas_call x1, Pallas kernels, prepare(): pl.pallas_call(prepare_kernel, out_shape=[shape((C, LANES), BF), shape((1...  2.19 us
  transfers between devices with their start and end apart: 19, of which 11 were waited for; matrix products, arithmetic and copies ran while one was open for 2% of the time, Pallas kernels for 8%

profile of v5, /device:TPU:1, one launch (start us, length us, event | category | flops | bytes accessed | tf_op | source)
XLA Modules:
  0.0 78.0 jit_solution(12745728506928952135)
XLA Ops:
  0.6 1.4 %copy-done = bf16[1,256,24,128]{3,2,1,0:T(8,128)(2,1)S(1)} copy-done((bf16[1,256,24,128]{3,2,1,0:T(8,128)(2,1)S(1)}, bf16[1,256,24,128]{3,2,1,0:T(8,128)(2,1)}, u32[]{:S(2)}) %copy-start) | copy-done | bytes 1572888
  2.0 1.2 %shard_map.84 = (bf16[256,3072]{1,0:T(8,128)(2,1)S(1)}, bf16[256,128]{1,0:T(8,128)(2,1)S(1)}) custom-call(bf16[1,256,24,128]{3,2,1,0:T(8,128)(2,1)S(1)} %copy-done), custom_call_target="tpu_custom_call" | custom-call | tf_op jit(solution)/shard_map/pallas_call | solution.py:607
  3.2 3.4 %collective-permute-start.1 = (bf16[256,128]{1,0:T(8,128)(2,1)S(1)}, bf16[256,128]{1,0:T(8,128)(2,1)S(1)}, u32[]{:S(2)}, u32[]{:S(2)}) collective-permute-start(bf16[256,128]{1,0:T(8,128)(2,1)S(1)} %get-tuple-element.40), channel_id=1, source_target_pairs={{4,8},{8,4},{0,12},{12,0},{5,9},{9,5},{1,13},{13,1},{6,10},{10,6},... | collective-permute-start | bytes 196616 | tf_op jit(solution)/shard_map/ppermute | solution.py:724
  6.6 0.0 collective-permute-start
  6.7 0.0 copy-start.4
  6.7 2.2 %shard_map.85 = (bf16[256,3840]{1,0:T(8,128)(2,1)S(1)}, bf16[128,3840]{1,0:T(8,128)(2,1)S(1)}, bf16[64,256]{1,0:T(8,128)(2,1)S(1)}, bf16[192,192]{1,0:T(8,128)(2...) custom-call(s32[2]{0:T(128)S(1)} %bitcast.20, ...), custom_call_target="tpu_custom_call" | custom-call | bytes 6000000 | tf_op jit(solution)/shard_map/pallas_call | solution.py:624
  8.9 0.1 pad_add_fusion.place
  8.9 0.0 collective-permute-done.1.odd_ref
  8.9 0.8 %collective-permute-done.even_ref = bf16[256,128]{1,0:T(8,128)(2,1)S(1)} collective-permute-done((bf16[256,128]{1,0:T(8,128)(2,1)S(1)}, bf16[256,128]{1,0:T(8,128)(2,1)S(1)}, u32[]{:S(2)}, u32[]{:S(2)}) %collective-permute-start) | collective-permute-done | bytes 65568 | tf_op jit(solution)/shard_map/ppermute | solution.py:723
  9.7 0.7 shard_map.86
  10.5 0.7 collective-permute-start.2
  11.1 4.3 %collective-permute-start.3 = (bf16[272,256]{1,0:T(8,128)(2,1)S(1)}, bf16[272,256]{1,0:T(8,128)(2,1)S(1)}, u32[]{:S(2)}, u32[]{:S(2)}) collective-permute-start(bf16[272,256]{1,0:T(8,128)(2,1)S(1)} %get-tuple-element.44), channel_id=1, source_target_pairs={{0,16},{16,0},{32,48},{48,32},{64,80},{80,64},{96,112},{112,96},{1... | collective-permute-start | bytes 417800 | tf_op jit(solution)/shard_map/ppermute | solution.py:728
  15.4 3.8 %shard_map.87 = (bf16[256,3328]{1,0:T(8,128)(2,1)S(1)}, bf16[64,3328]{1,0:T(8,128)(2,1)S(1)}, bf16[192,3072]{1,0:T(8,128)(2,1)S(1)}, bf16[64,2816]{1,0:T(8,128)(...) custom-call(s32[4]{0:T(128)S(1)} %pad_add_fusion.place, ...), custom_call_target="tpu_custom_call" | custom-call | flops 1000000000 | bytes 12000000 | tf_op jit(solution)/shard_map/pallas_call | solution.py:658
  19.2 0.0 collective-permute-done.2.odd_ref
  19.2 0.0 collective-permute-done.3.even_ref
  19.3 10.4 %shard_map.88 = (f32[4,32,640]{2,1,0:T(8,128)S(1)}, f32[4,32,640]{2,1,0:T(8,128)S(1)}) custom-call(s32[4]{0:T(128)S(1)} %pad_add_fusion.place, bf16[256,3840]{1,0:T(8,128)(2,1)S(1)} %get-tuple-element.38.flat_ref, bf16[128,3840]{1,0:T(8,128)(2,1)S(1)} %get-tuple-element.39.spot_ref, bf16[256,128]{1,0:T(8,128)(2,1)S(1)} %get-tuple-element.42.rim_ref, ...), custom_call_target="tpu_custom_call" | custom-call | tf_op jit(solution)/shard_map/pallas_call | solution.py:672
  29.7 2.6 %collective-permute-start.4 = (f32[4,32,640]{2,1,0:T(8,128)S(1)}, f32[4,32,640]{2,1,0:T(8,128)S(1)}, u32[]{:S(2)}, u32[]{:S(2)}) collective-permute-start(f32[4,32,640]{2,1,0:T(8,128)S(1)} %get-tuple-element.67), channel_id=1, source_target_pairs={{0,1},{1,0},{2,3},{3,2},{4,5},{5,4},{6,7},{7,6},{8,9},{9,8},{10,11... | collective-permute-start | bytes 983048 | tf_op jit(solution)/shard_map/ppermute | solution.py:77
  32.3 1.3 %collective-permute-done.4 = f32[4,32,640]{2,1,0:T(8,128)S(1)} collective-permute-done((f32[4,32,640]{2,1,0:T(8,128)S(1)}, f32[4,32,640]{2,1,0:T(8,128)S(1)}, u32[]{:S(2)}, u32[]{:S(2)}) %collective-permute-start.4) | collective-permute-done | bytes 327712 | tf_op jit(solution)/shard_map/ppermute | solution.py:77
  33.6 0.8 %collective-permute-start.7 = (f32[32,640]{1,0:T(8,128)S(1)}, f32[32,640]{1,0:T(8,128)S(1)}, u32[]{:S(2)}, u32[]{:S(2)}) collective-permute-start(f32[32,640]{1,0:T(8,128)S(1)} %get-tuple-element.74), channel_id=1, source_target_pairs={{0,8},{4,12},{8,0},{12,4},{1,9},{5,13},{9,1},{13,5},{2,10},{6,14},... | collective-permute-start | bytes 245768 | tf_op jit(solution)/shard_map/ppermute | solution.py:77
  34.4 1.8 %collective-permute-start.6 = (f32[32,640]{1,0:T(8,128)S(1)}, f32[32,640]{1,0:T(8,128)S(1)}, u32[]{:S(2)}, u32[]{:S(2)}) collective-permute-start(f32[32,640]{1,0:T(8,128)S(1)} %get-tuple-element.75), channel_id=1, source_target_pairs={{0,12},{4,8},{8,4},{12,0},{1,13},{5,9},{9,5},{13,1},{2,14},{6,10},... | collective-permute-start | bytes 245768 | tf_op jit(solution)/shard_map/ppermute | solution.py:77
  36.2 0.3 collective-permute-start.5
  36.5 2.5 %collective-permute-done.7 = f32[32,640]{1,0:T(8,128)S(1)} collective-permute-done((f32[32,640]{1,0:T(8,128)S(1)}, f32[32,640]{1,0:T(8,128)S(1)}, u32[]{:S(2)}, u32[]{:S(2)}) %collective-permute-start.7) | collective-permute-done | bytes 81952 | tf_op jit(solution)/shard_map/ppermute | solution.py:77
  39.1 2.5 %collective-permute-done.6 = f32[32,640]{1,0:T(8,128)S(1)} collective-permute-done((f32[32,640]{1,0:T(8,128)S(1)}, f32[32,640]{1,0:T(8,128)S(1)}, u32[]{:S(2)}, u32[]{:S(2)}) %collective-permute-start.6) | collective-permute-done | bytes 81952 | tf_op jit(solution)/shard_map/ppermute | solution.py:77
  41.5 0.0 collective-permute-done.5
  41.6 2.7 %collective-permute-start.10 = (f32[32,640]{1,0:T(8,128)S(1)}, f32[32,640]{1,0:T(8,128)S(1)}, u32[]{:S(2)}, u32[]{:S(2)}) collective-permute-start(f32[32,640]{1,0:T(8,128)S(1)} %fusion.1), channel_id=1, source_target_pairs={{0,32},{16,48},{32,0},{48,16},{64,96},{80,112},{96,64},{112,80},{1... | collective-permute-start | bytes 245768 | tf_op jit(solution)/shard_map/ppermute | solution.py:77
  44.3 0.6 collective-permute-start.9
  44.9 0.0 collective-permute-start.8
  44.9 1.5 %collective-permute-done.10 = f32[32,640]{1,0:T(8,128)S(1)} collective-permute-done((f32[32,640]{1,0:T(8,128)S(1)}, f32[32,640]{1,0:T(8,128)S(1)}, u32[]{:S(2)}, u32[]{:S(2)}) %collective-permute-start.10) | collective-permute-done | bytes 81952 | tf_op jit(solution)/shard_map/ppermute | solution.py:77
  46.4 2.3 %collective-permute-done.9 = f32[32,640]{1,0:T(8,128)S(1)} collective-permute-done((f32[32,640]{1,0:T(8,128)S(1)}, f32[32,640]{1,0:T(8,128)S(1)}, u32[]{:S(2)}, u32[]{:S(2)}) %collective-permute-start.9) | collective-permute-done | bytes 81952 | tf_op jit(solution)/shard_map/ppermute | solution.py:77
  48.8 0.0 collective-permute-done.8
  48.8 1.8 %collective-permute-start.11 = (f32[32,640]{1,0:T(8,128)S(1)}, f32[32,640]{1,0:T(8,128)S(1)}, u32[]{:S(2)}, u32[]{:S(2)}) collective-permute-start(f32[32,640]{1,0:T(8,128)S(1)} %add_add_fusion), channel_id=1, source_target_pairs={{0,64},{1,65},{2,66},{3,67},{16,80},{17,81},{18,82},{19,83},{32,96... | collective-permute-start | bytes 245768 | tf_op jit(solution)/shard_map/ppermute | solution.py:77
  50.6 1.8 %collective-permute-done.11 = f32[32,640]{1,0:T(8,128)S(1)} collective-permute-done((f32[32,640]{1,0:T(8,128)S(1)}, f32[32,640]{1,0:T(8,128)S(1)}, u32[]{:S(2)}, u32[]{:S(2)}) %collective-permute-start.11) | collective-permute-done | bytes 81952 | tf_op jit(solution)/shard_map/ppermute | solution.py:77
  52.4 8.3 %collective-permute-start.14 = (f32[32,640]{1,0:T(8,128)S(1)}, f32[32,640]{1,0:T(8,128)S(1)}, u32[]{:S(2)}, u32[]{:S(2)}) collective-permute-start(f32[32,640]{1,0:T(8,128)S(1)} %add.81.own), channel_id=1, source_target_pairs={{0,66},{1,67},{2,64},{3,65},{16,82},{17,83},{18,80},{19,81},{32,98... | collective-permute-start | bytes 245768 | tf_op jit(solution)/shard_map/ppermute | solution.py:77
  60.7 1.6 %collective-permute-start.12 = (f32[32,640]{1,0:T(8,128)S(1)}, f32[32,640]{1,0:T(8,128)S(1)}, u32[]{:S(2)}, u32[]{:S(2)}) collective-permute-start(f32[32,640]{1,0:T(8,128)S(1)} %add.81.own), channel_id=1, source_target_pairs={{0,192},{1,193},{2,194},{3,195},{16,208},{17,209},{18,210},{19,211... | collective-permute-start | bytes 245768 | tf_op jit(solution)/shard_map/ppermute | solution.py:77
  62.3 1.5 %collective-permute-done.14.got_c = f32[32,640]{1,0:T(8,128)S(1)} collective-permute-done((f32[32,640]{1,0:T(8,128)S(1)}, f32[32,640]{1,0:T(8,128)S(1)}, u32[]{:S(2)}, u32[]{:S(2)}) %collective-permute-start.14) | collective-permute-done | bytes 81952 | tf_op jit(solution)/shard_map/ppermute | solution.py:77
  63.8 3.5 %collective-permute-done.13.got_b = f32[32,640]{1,0:T(8,128)S(1)} collective-permute-done((f32[32,640]{1,0:T(8,128)S(1)}, f32[32,640]{1,0:T(8,128)S(1)}, u32[]{:S(2)}, u32[]{:S(2)}) %collective-permute-start.13) | collective-permute-done | bytes 81952 | tf_op jit(solution)/shard_map/ppermute | solution.py:77
  67.3 0.0 collective-permute-done.12.got_a
  67.3 0.6 shard_map.89
  67.9 2.3 %collective-permute-start.15 = (f32[1,640]{1,0:T(1,128)S(1)}, f32[1,640]{1,0:T(1,128)S(1)}, u32[]{:S(2)}, u32[]{:S(2)}) collective-permute-start(f32[1,640]{1,0:T(1,128)S(1)} %get-tuple-element.69), channel_id=1, source_target_pairs={{0,1},{1,0},{2,3},{3,2},{4,5},{5,4},{6,7},{7,6},{8,9},{9,8},{10,11... | collective-permute-start | bytes 7688 | tf_op jit(solution)/shard_map/ppermute | solution.py:77
  70.3 0.8 %collective-permute-done.15 = f32[1,640]{1,0:T(1,128)S(1)} collective-permute-done((f32[1,640]{1,0:T(1,128)S(1)}, f32[1,640]{1,0:T(1,128)S(1)}, u32[]{:S(2)}, u32[]{:S(2)}) %collective-permute-start.15) | collective-permute-done | bytes 2592 | tf_op jit(solution)/shard_map/ppermute | solution.py:77
  71.1 0.2 collective-permute-start.18
  71.3 2.1 %collective-permute-start.17 = (f32[1,640]{1,0:T(1,128)S(1)}, f32[1,640]{1,0:T(1,128)S(1)}, u32[]{:S(2)}, u32[]{:S(2)}) collective-permute-start(f32[1,640]{1,0:T(1,128)S(1)} %add.82), channel_id=1, source_target_pairs={{0,12},{4,8},{8,4},{12,0},{1,13},{5,9},{9,5},{13,1},{2,14},{6,10},... | collective-permute-start | bytes 7688 | tf_op jit(solution)/shard_map/ppermute | solution.py:77
  73.4 0.3 collective-permute-start.16
  73.7 0.6 multiply_add_fusion
  74.3 0.6 slice.27
  75.6 0.0 collective-permute-done.17
  75.6 0.6 collective-permute-done.16
  76.2 0.7 multiply_subtract_fusion
  (20 shorter events, 0.2 us)
Async XLA Ops:
  0.6 1.4 %copy-start = (bf16[1,256,24,128]{3,2,1,0:T(8,128)(2,1)S(1)}, bf16[1,256,24,128]{3,2,1,0:T(8,128)(2,1)}, u32[]{:S(2)}) copy-start(bf16[1,256,24,128]{3,2,1,0:T(8,128)(2,1)} %image_ref.1) | copy-start | bytes 4718596
  2.0 4.6 %copy-start.1 = (f32[141312]{0:T(1024)S(1)}, f32[141312]{0:T(1024)}, u32[]{:S(2)}) copy-start(f32[141312]{0:T(1024)} %param.7) | copy-start | bytes 1695748
  2.0 4.6 %copy-start.2 = (f32[8,3840]{1,0:T(8,128)S(1)}, f32[8,3840]{1,0:T(8,128)}, u32[]{:S(2)}) copy-start(f32[8,3840]{1,0:T(8,128)} %constant.67.clone.table) | copy-start | bytes 368644
  2.0 4.6 %copy-start.3 = (s32[1,1,2]{2,1,0:T(1,128)S(1)}, s32[1,1,2]{2,1,0:T(1,128)}, u32[]{:S(2)}) copy-start(s32[1,1,2]{2,1,0:T(1,128)} %param.6) | copy-start | bytes 28
  3.2 5.7 %collective-permute-start.1 = (bf16[256,128]{1,0:T(8,128)(2,1)S(1)}, bf16[256,128]{1,0:T(8,128)(2,1)S(1)}, u32[]{:S(2)}, u32[]{:S(2)}) collective-permute-start(bf16[256,128]{1,0:T(8,128)(2,1)S(1)} %get-tuple-element.40), channel_id=1, source_target_pairs={{4,8},{8,4},{0,12},{12,0},{5,9},{9,5},{1,13},{13,1},{6,10},{10,6},... | collective-permute-start | bytes 196616 | tf_op jit(solution)/shard_map/ppermute | solution.py:724
  6.6 3.1 %collective-permute-start = (bf16[256,128]{1,0:T(8,128)(2,1)S(1)}, bf16[256,128]{1,0:T(8,128)(2,1)S(1)}, u32[]{:S(2)}, u32[]{:S(2)}) collective-permute-start(bf16[256,128]{1,0:T(8,128)(2,1)S(1)} %get-tuple-element.40), channel_id=1, source_target_pairs={{0,4},{4,0},{8,12},{12,8},{1,5},{5,1},{9,13},{13,9},{2,6},{6,2},{1... | collective-permute-start | bytes 196616 | tf_op jit(solution)/shard_map/ppermute | solution.py:723
  6.7 8.7 %copy-start.4 = (f32[552]{0:T(1024)S(1)}, f32[552]{0:T(1024)}, u32[]{:S(2)}) copy-start(f32[552]{0:T(1024)} %param.8) | copy-start | bytes 6628
  10.5 8.8 %collective-permute-start.2 = (bf16[272,256]{1,0:T(8,128)(2,1)S(1)}, bf16[272,256]{1,0:T(8,128)(2,1)S(1)}, u32[]{:S(2)}, u32[]{:S(2)}) collective-permute-start(bf16[272,256]{1,0:T(8,128)(2,1)S(1)} %get-tuple-element.43), channel_id=1, source_target_pairs={{16,32},{32,16},{48,64},{64,48},{80,96},{96,80},{112,128},{128,112... | collective-permute-start | bytes 417800 | tf_op jit(solution)/shard_map/ppermute | solution.py:727
  11.1 8.1 %collective-permute-start.3 = (bf16[272,256]{1,0:T(8,128)(2,1)S(1)}, bf16[272,256]{1,0:T(8,128)(2,1)S(1)}, u32[]{:S(2)}, u32[]{:S(2)}) collective-permute-start(bf16[272,256]{1,0:T(8,128)(2,1)S(1)} %get-tuple-element.44), channel_id=1, source_target_pairs={{0,16},{16,0},{32,48},{48,32},{64,80},{80,64},{96,112},{112,96},{1... | collective-permute-start | bytes 417800 | tf_op jit(solution)/shard_map/ppermute | solution.py:728
  29.7 3.8 %collective-permute-start.4 = (f32[4,32,640]{2,1,0:T(8,128)S(1)}, f32[4,32,640]{2,1,0:T(8,128)S(1)}, u32[]{:S(2)}, u32[]{:S(2)}) collective-permute-start(f32[4,32,640]{2,1,0:T(8,128)S(1)} %get-tuple-element.67), channel_id=1, source_target_pairs={{0,1},{1,0},{2,3},{3,2},{4,5},{5,4},{6,7},{7,6},{8,9},{9,8},{10,11... | collective-permute-start | bytes 983048 | tf_op jit(solution)/shard_map/ppermute | solution.py:77
  33.6 5.5 %collective-permute-start.7 = (f32[32,640]{1,0:T(8,128)S(1)}, f32[32,640]{1,0:T(8,128)S(1)}, u32[]{:S(2)}, u32[]{:S(2)}) collective-permute-start(f32[32,640]{1,0:T(8,128)S(1)} %get-tuple-element.74), channel_id=1, source_target_pairs={{0,8},{4,12},{8,0},{12,4},{1,9},{5,13},{9,1},{13,5},{2,10},{6,14},... | collective-permute-start | bytes 245768 | tf_op jit(solution)/shard_map/ppermute | solution.py:77
  34.4 7.1 %collective-permute-start.6 = (f32[32,640]{1,0:T(8,128)S(1)}, f32[32,640]{1,0:T(8,128)S(1)}, u32[]{:S(2)}, u32[]{:S(2)}) collective-permute-start(f32[32,640]{1,0:T(8,128)S(1)} %get-tuple-element.75), channel_id=1, source_target_pairs={{0,12},{4,8},{8,4},{12,0},{1,13},{5,9},{9,5},{13,1},{2,14},{6,10},... | collective-permute-start | bytes 245768 | tf_op jit(solution)/shard_map/ppermute | solution.py:77
  36.2 5.3 %collective-permute-start.5 = (f32[32,640]{1,0:T(8,128)S(1)}, f32[32,640]{1,0:T(8,128)S(1)}, u32[]{:S(2)}, u32[]{:S(2)}) collective-permute-start(f32[32,640]{1,0:T(8,128)S(1)} %get-tuple-element.76), channel_id=1, source_target_pairs={{0,4},{4,0},{8,12},{12,8},{1,5},{5,1},{9,13},{13,9},{2,6},{6,2},{1... | collective-permute-start | bytes 245768 | tf_op jit(solution)/shard_map/ppermute | solution.py:77
  41.6 4.9 %collective-permute-start.10 = (f32[32,640]{1,0:T(8,128)S(1)}, f32[32,640]{1,0:T(8,128)S(1)}, u32[]{:S(2)}, u32[]{:S(2)}) collective-permute-start(f32[32,640]{1,0:T(8,128)S(1)} %fusion.1), channel_id=1, source_target_pairs={{0,32},{16,48},{32,0},{48,16},{64,96},{80,112},{96,64},{112,80},{1... | collective-permute-start | bytes 245768 | tf_op jit(solution)/shard_map/ppermute | solution.py:77
  44.3 4.5 %collective-permute-start.9 = (f32[32,640]{1,0:T(8,128)S(1)}, f32[32,640]{1,0:T(8,128)S(1)}, u32[]{:S(2)}, u32[]{:S(2)}) collective-permute-start(f32[32,640]{1,0:T(8,128)S(1)} %fusion.1), channel_id=1, source_target_pairs={{0,48},{16,32},{32,16},{48,0},{64,112},{80,96},{96,80},{112,64},{1... | collective-permute-start | bytes 245768 | tf_op jit(solution)/shard_map/ppermute | solution.py:77
  44.9 3.9 %collective-permute-start.8 = (f32[32,640]{1,0:T(8,128)S(1)}, f32[32,640]{1,0:T(8,128)S(1)}, u32[]{:S(2)}, u32[]{:S(2)}) collective-permute-start(f32[32,640]{1,0:T(8,128)S(1)} %fusion.1), channel_id=1, source_target_pairs={{0,16},{16,0},{32,48},{48,32},{64,80},{80,64},{96,112},{112,96},{1... | collective-permute-start | bytes 245768 | tf_op jit(solution)/shard_map/ppermute | solution.py:77
  48.8 3.6 %collective-permute-start.11 = (f32[32,640]{1,0:T(8,128)S(1)}, f32[32,640]{1,0:T(8,128)S(1)}, u32[]{:S(2)}, u32[]{:S(2)}) collective-permute-start(f32[32,640]{1,0:T(8,128)S(1)} %add_add_fusion), channel_id=1, source_target_pairs={{0,64},{1,65},{2,66},{3,67},{16,80},{17,81},{18,82},{19,83},{32,96... | collective-permute-start | bytes 245768 | tf_op jit(solution)/shard_map/ppermute | solution.py:77
  52.4 11.4 %collective-permute-start.14 = (f32[32,640]{1,0:T(8,128)S(1)}, f32[32,640]{1,0:T(8,128)S(1)}, u32[]{:S(2)}, u32[]{:S(2)}) collective-permute-start(f32[32,640]{1,0:T(8,128)S(1)} %add.81.own), channel_id=1, source_target_pairs={{0,66},{1,67},{2,64},{3,65},{16,82},{17,83},{18,80},{19,81},{32,98... | collective-permute-start | bytes 245768 | tf_op jit(solution)/shard_map/ppermute | solution.py:77
  60.7 6.6 %collective-permute-start.13 = (f32[32,640]{1,0:T(8,128)S(1)}, f32[32,640]{1,0:T(8,128)S(1)}, u32[]{:S(2)}, u32[]{:S(2)}) collective-permute-start(f32[32,640]{1,0:T(8,128)S(1)} %add.81.own), channel_id=1, source_target_pairs={{0,194},{1,195},{2,192},{3,193},{16,210},{17,211},{18,208},{19,209... | collective-permute-start | bytes 245768 | tf_op jit(solution)/shard_map/ppermute | solution.py:77
  60.7 6.6 %collective-permute-start.12 = (f32[32,640]{1,0:T(8,128)S(1)}, f32[32,640]{1,0:T(8,128)S(1)}, u32[]{:S(2)}, u32[]{:S(2)}) collective-permute-start(f32[32,640]{1,0:T(8,128)S(1)} %add.81.own), channel_id=1, source_target_pairs={{0,192},{1,193},{2,194},{3,195},{16,208},{17,209},{18,210},{19,211... | collective-permute-start | bytes 245768 | tf_op jit(solution)/shard_map/ppermute | solution.py:77
  67.9 3.2 %collective-permute-start.15 = (f32[1,640]{1,0:T(1,128)S(1)}, f32[1,640]{1,0:T(1,128)S(1)}, u32[]{:S(2)}, u32[]{:S(2)}) collective-permute-start(f32[1,640]{1,0:T(1,128)S(1)} %get-tuple-element.69), channel_id=1, source_target_pairs={{0,1},{1,0},{2,3},{3,2},{4,5},{5,4},{6,7},{7,6},{8,9},{9,8},{10,11... | collective-permute-start | bytes 7688 | tf_op jit(solution)/shard_map/ppermute | solution.py:77
  71.1 4.5 %collective-permute-start.18 = (f32[1,640]{1,0:T(1,128)S(1)}, f32[1,640]{1,0:T(1,128)S(1)}, u32[]{:S(2)}, u32[]{:S(2)}) collective-permute-start(f32[1,640]{1,0:T(1,128)S(1)} %add.82), channel_id=1, source_target_pairs={{0,8},{4,12},{8,0},{12,4},{1,9},{5,13},{9,1},{13,5},{2,10},{6,14},... | collective-permute-start | bytes 7688 | tf_op jit(solution)/shard_map/ppermute | solution.py:77
  71.3 4.3 %collective-permute-start.17 = (f32[1,640]{1,0:T(1,128)S(1)}, f32[1,640]{1,0:T(1,128)S(1)}, u32[]{:S(2)}, u32[]{:S(2)}) collective-permute-start(f32[1,640]{1,0:T(1,128)S(1)} %add.82), channel_id=1, source_target_pairs={{0,12},{4,8},{8,4},{12,0},{1,13},{5,9},{9,5},{13,1},{2,14},{6,10},... | collective-permute-start | bytes 7688 | tf_op jit(solution)/shard_map/ppermute | solution.py:77
  73.4 2.7 %collective-permute-start.16 = (f32[1,640]{1,0:T(1,128)S(1)}, f32[1,640]{1,0:T(1,128)S(1)}, u32[]{:S(2)}, u32[]{:S(2)}) collective-permute-start(f32[1,640]{1,0:T(1,128)S(1)} %add.82), channel_id=1, source_target_pairs={{0,4},{4,0},{8,12},{12,8},{1,5},{5,1},{9,13},{13,9},{2,6},{6,2},{1... | collective-permute-start | bytes 7688 | tf_op jit(solution)/shard_map/ppermute | solution.py:77

commit v6 on v5

--- a/solution.py
+++ b/solution.py
@@ -63,12 +63,12 @@
 
 
 CORE = ("dp", [exchange(4, lambda i: i ^ 1)])
-X_RING = ("col", [exchange(4, lambda i, k=k: i ^ k) for k in (1, 3, 2)])
-Y_RING = ("row", [exchange(16, lambda i, k=k: i ^ k) for k in (1, 3, 2)])
+X_RING = ("col", [exchange(4, lambda i, k=k: i ^ k) for k in (2, 3, 1)])
+Y_RING = ("row", [exchange(16, lambda i, k=k: i ^ k) for k in (3, 1, 2)])
 Z_PAIR = (("row", "dp"), [along_z(lambda z: z ^ 1)])
 Z_RING = (
     ("row", "dp"),
-    [along_z(z_near), along_z(lambda z: 7 - z), along_z(lambda z: z ^ 5)],
+    [along_z(lambda z: z ^ 5), along_z(lambda z: 7 - z), along_z(z_near)],
 )
 
 
@@ -138,20 +138,14 @@
     tall[...] = image_ref[0].astype(F32).reshape(C * TILE_ROWS, 128)
     lane = lax.broadcasted_iota(jnp.int32, (128, 128), 1)
     col = lax.broadcasted_iota(jnp.int32, (128, 128), 0)
-    wanted = jnp.where(col < HALO, col + 64, jnp.where(col >= 126, col - 126, -1000))
+    wanted = jnp.where(col < HALO, col + 4, jnp.where(col >= 126, col - 124, -1000))
     for r in range(TILE_ROWS):
         own_ref[:, r * 128 : (r + 1) * 128] = tall[pl.ds(r, C, stride=TILE_ROWS), :].astype(BF)
-        select[r * 128 : (r + 1) * 128, :] = (lane - 2 * r == wanted).astype(F32).astype(BF)
+        select[r * 128 : (r + 1) * 128, :] = (lane - 4 * r == wanted).astype(F32).astype(BF)
     edge_ref[...] = nn(own_ref[...], select[...]).astype(BF)
 
 
-def spots(count, table, k, start, stop):
-    source = lax.broadcasted_iota(jnp.int32, (count, stop - start), 0).astype(F32)
-    return (source == table[k : k + 1, start:stop]).astype(F32).astype(BF)
-
-
 def prepare_kernel(
-    labels,
     own_ref,
     weights_ref,
     table,
@@ -169,9 +163,11 @@
     wout2,
     win2,
     head_ref,
-    target_ref,
     tall,
 ):
+    for start, stop in cut(*X_SPAN):
+        source = lax.broadcasted_iota(jnp.int32, (128, stop - start), 0).astype(F32)
+        spot_ref[:, start:stop] = (source == table[5:6, start:stop]).astype(F32).astype(BF)
     for r in range(TILE_ROWS):
         lane = (r + HALO) * COLS + HALO
         flat_ref[:, lane : lane + 128] = own_ref[:, r * 128 : (r + 1) * 128]
@@ -209,21 +205,16 @@
             1088:1104, j * CLASSES : (j + 1) * CLASSES
         ]
     head_ref[...] = tall[:, 0:CLASSES]
-    for start, stop in cut(0, LANES):
-        spot_ref[:, start:stop] = spots(128, table, 3, start, stop)
-    line = lax.broadcasted_iota(jnp.int32, (8, CLASSES), 0)
-    label = jnp.where(line == 0, labels[0], labels[1])
-    target_ref[...] = (lax.broadcasted_iota(jnp.int32, (8, CLASSES), 1) == label).astype(F32)
-
-
-def rim_kernel(place, own_ref, even_ref, odd_ref, _, rim_ref, up_ref, down_ref):
+
+
+def rim_kernel(place, own_ref, odd_ref, even_ref, _, rim_ref, up_ref, down_ref):
     row, col = place[0], place[1]
-    lane = lax.broadcasted_iota(jnp.int32, (C, 128), 1)
+    on_left = lax.rem(lax.broadcasted_iota(jnp.int32, (C, 128), 1), 4) >= 2
     odd_col = lax.rem(col, 2)
     from_even = even_ref[...].astype(F32)
     from_odd = odd_ref[...].astype(F32)
-    by_even = (lane < 64).astype(jnp.int32) == odd_col
-    outside = ((lane < 64) & (col == 0)) | ((lane >= 64) & (col == 3))
+    by_even = on_left.astype(jnp.int32) == odd_col
+    outside = (on_left & (col == 0)) | (~on_left & (col == 3))
     rim = jnp.where(outside, 0.0, jnp.where(by_even, from_even, from_odd)).astype(BF)
     rim_ref[...] = rim
     odd_row = lax.rem(row, 2)
@@ -232,14 +223,15 @@
     for ref, low in ((up_ref, odd_row), (down_ref, 1 - odd_row)):
         first = (1 - low) * (TILE_ROWS - HALO)
         ref[0:C, :] = own_ref[:, pl.ds(pl.multiple_of(first * 128, 128), HALO * 128)]
-        wanted = 2 * first + jnp.where(corner < 4, corner, 64 + corner - 4)
+        row_of, pixel = lax.rem(corner, 4) // 2, lax.rem(corner, 2)
+        wanted = 4 * (first + row_of) + pixel + jnp.where(corner < 4, 2, 4)
         pick = ((source == wanted) & (corner < 8)).astype(F32).astype(BF)
         ref[C:, :] = nt(pick, rim).astype(BF)
 
 
 def in_image(place, table, start, stop):
     row, col = place[0], place[1]
-    r, c = table[6:7, start:stop], table[7:8, start:stop]
+    r, c = table[3:4, start:stop], table[4:5, start:stop]
     r_low = jnp.where(row > 0, -HALO, 0).astype(F32)
     r_high = jnp.where(row < 15, TILE_ROWS + HALO, TILE_ROWS).astype(F32)
     c_low = jnp.where(col > 0, -HALO, 0).astype(F32)
@@ -252,6 +244,13 @@
     for pieces, work in phases:
         for start, stop in pieces:
             work(start, stop)
+
+
+def put_rim(ref, rim, start, stop):
+    for b in range(TILE_ROWS + 1):
+        lane = (b + HALO) * COLS - HALO
+        if start <= lane and lane + 2 * HALO <= stop:
+            ref[:, lane - start : lane - start + 2 * HALO] = rim[:, 4 * b : 4 * b + 4]
 
 
 def enter(inputs, win_t, h1, ranges, mask):
@@ -358,7 +357,6 @@
 def kernel(
     place,
     flat_ref,
-    spot_ref,
     rim_ref,
     odd_ref,
     even_ref,
@@ -433,14 +431,16 @@
     odd_row = lax.rem(place[0], 2) == 1
     above = jnp.where(odd_row, even_ref[...].astype(F32), odd_ref[...].astype(F32)).astype(BF)
     below = jnp.where(odd_row, odd_ref[...].astype(F32), even_ref[...].astype(F32)).astype(BF)
-    for end, start, stop, k, rows in ((0, 0, INNER, 4, above), (1, OUTER, LANES, 5, below)):
-        value = nn(rim_ref[...], spot_ref[:, start:stop]) + flat_ref[:, start:stop].astype(F32)
+    for end, start, stop, rows in ((0, 0, INNER, above), (1, OUTER, LANES, below)):
+        ref = x_ends.at[end]
+        ref[...] = flat_ref[:, start:stop]
+        put_rim(ref, rim_ref, start, stop)
         corners = rows[C:, :].astype(F32).T.astype(BF)
-        value = value + nn(corners, spots(CORNERS, table, k, start, stop))
-        x_ends[end] = value.astype(BF)
-        for r in range(HALO):
-            lane = (r if end == 0 else ROWS - HALO + r) * COLS + HALO - start
-            x_ends[end, :, lane : lane + 128] = rows[0:C, r * 128 : (r + 1) * 128]
+        for k in range(HALO):
+            lane = (k if end == 0 else ROWS - HALO + k) * COLS - start
+            ref[:, lane : lane + HALO] = corners[:, 2 * k : 2 * k + 2]
+            ref[:, lane + HALO : lane + HALO + 128] = rows[0:C, k * 128 : (k + 1) * 128]
+            ref[:, lane + HALO + 128 : lane + COLS] = corners[:, 4 + 2 * k : 6 + 2 * k]
     ends = [(0, INNER), (OUTER, LANES)]
     wider = [(0, INNER + 256), (OUTER - 256, LANES)]
     mask = lambda start, stop: in_image(place, table, start, stop)
@@ -617,29 +617,29 @@
     )(image)
 
 
-def prepare(labels, own, weights, table):
+def prepare(own, weights, table):
     square = shape((3 * MID, 3 * MID), BF)
     down, up = shape((MID, C), BF), shape((C, MID), BF)
     block = [down, square, square, up, down]
     return pl.pallas_call(
         prepare_kernel,
-        out_shape=[shape((C, LANES), BF), shape((128, LANES), BF)] + block + block + [up, shape((C, CLASSES), F32), shape((8, CLASSES), F32)],
-        in_specs=[SMEM] + [VMEM] * 3,
-        out_specs=[VMEM] * 15,
+        out_shape=[shape((C, LANES), BF), shape((128, LANES), BF)] + block + block + [up, shape((C, CLASSES), F32)],
+        in_specs=[VMEM] * 3,
+        out_specs=[VMEM] * 14,
         scratch_shapes=[pltpu.VMEM((C, MID), F32)],
         compiler_params=PARAMS,
         cost_estimate=pl.CostEstimate(flops=0, bytes_accessed=6_000_000, transcendentals=0),
-    )(labels, own, weights.reshape(PARAM // 128, 128), table)
-
-
-def rim(place, own, even, odd, after):
+    )(own, weights.reshape(PARAM // 128, 128), table)
+
+
+def rim(place, own, odd, even, after):
     return pl.pallas_call(
         rim_kernel,
         out_shape=(shape((C, 128), BF), shape(MSG, BF), shape(MSG, BF)),
         in_specs=[SMEM] + [VMEM] * 4,
         out_specs=(VMEM,) * 3,
         compiler_params=PARAMS,
-    )(place, own, even, odd, after)
+    )(place, own, odd, even, after)
 
 
 def inner(place, flat, spot, beyond, table, mats):
@@ -668,11 +668,11 @@
     )(place, flat, spot, beyond, table, win_t1, wf1, wout_t1, win_t2, wf2, wout_t2)
 
 
-def compute(place, flat, spot, beyond, odd, even, table, momentum, mats, mids):
+def compute(place, flat, beyond, odd, even, table, momentum, mats, mids):
     return pl.pallas_call(
         kernel,
         out_shape=(shape((4, SHARES, PAD), F32), shape((4, SHARES, PAD), F32)),
-        in_specs=[SMEM] + [VMEM] * 29,
+        in_specs=[SMEM] + [VMEM] * 28,
         out_specs=(VMEM, VMEM),
         scratch_shapes=[
             pltpu.VMEM((PARAM // 128 + 8, 128), F32),
@@ -693,7 +693,7 @@
             pltpu.VMEM((C, MID), F32),
         ],
         compiler_params=PARAMS,
-    )(place, flat, spot, beyond, odd, even, table, momentum, *mats, *mids)
+    )(place, flat, beyond, odd, even, table, momentum, *mats, *mids)
 
 
 def make_table():
@@ -703,36 +703,32 @@
     inside = real & (r >= 0) & (r < TILE_ROWS)
     tiles = [inside & (c >= t * TILE_COLS) & (c < (t + 1) * TILE_COLS) for t in range(2)]
     near = real & (r >= -1) & (r <= TILE_ROWS) & (c >= -1) & (c <= 2 * TILE_COLS)
-    lane = np.where(c < 0, 2 * r + c + HALO, np.where(c >= 128, 64 + 2 * r + c - 128, -1000))
-    corner = lambda k: np.where(c < 0, 2 * k + c + HALO, np.where(c >= 128, 4 + 2 * k + c - 128, -1000))
-    sources = [
-        np.where(inside, lane, -1000),
-        np.where(real & (r < 0), corner(r + HALO), -1000),
-        np.where(real & (r >= TILE_ROWS), corner(r - TILE_ROWS), -1000),
-    ]
-    return jnp.asarray(np.stack([*tiles, near, *sources, r, c]).astype(np.float32))
+    lane = np.where(c < 0, 4 * r + c + 4, np.where(c >= 128, 4 * r + c - 124, -1000))
+    lane = np.where(real & (r >= 0) & (r < TILE_ROWS), lane, -1000)
+    return jnp.asarray(np.stack([*tiles, near, r, c, lane, 0 * r, 0 * r]).astype(np.float32))
 
 
 def local(image, labels, weights, momentum):
     row, col, dp = lax.axis_index("row"), lax.axis_index("col"), lax.axis_index("dp")
     place = jnp.stack([row, col, dp % 2, dp // 2]).astype(jnp.int32)
     table = make_table()
+    targets = (labels.reshape(2, 1) == jnp.arange(CLASSES, dtype=jnp.int32)).astype(F32)
     padded_momentum = jnp.pad(momentum, (0, PAD - SHARE)).reshape(1, PAD)
 
     own, edge = split(image)
+    odd = lax.ppermute(edge, "col", neighbours(4, True, True))
     even = lax.ppermute(edge, "col", neighbours(4, False))
-    odd = lax.ppermute(edge, "col", neighbours(4, True, True))
-    flat, spot, *mats = prepare(labels.reshape(2), own, weights, table)
-    beyond, up, down = rim(place, own, even, odd, mats[-1])
+    flat, spot, *mats = prepare(own, weights, table)
+    beyond, up, down = rim(place, own, odd, even, mats[-1])
     odd = lax.ppermute(down, "row", neighbours(16, True))
     even = lax.ppermute(up, "row", neighbours(16, False))
     mids = inner(place, flat, spot, beyond, table, mats)
     keep, send = compute(
-        place, flat, spot, beyond, odd, even, table, padded_momentum, mats, mids
+        place, flat, beyond, odd, even, table, padded_momentum, [*mats, targets], mids
     )
 
     parts = keep + received([send], CORE)[0]
-    parts = paired_sum(parts[0], received([parts[1], parts[3], parts[2]], X_RING))
+    parts = paired_sum(parts[0], received([parts[2], parts[3], parts[1]], X_RING))
     for stage in (Y_RING, Z_PAIR):
         parts = stage_sum(parts, stage)
     got = received([parts] * 3, Z_RING)

time: 78.1 us -> 78 us (level)
  Pallas kernels: 19 us -> 18.2 us
  transfers between devices with their start and end apart: 19 -> 19, of which waited for: 11 -> 11; matrix products, arithmetic and copies ran while one was open for 2% -> 2% of each run, Pallas kernels for 8% -> 7%
where the time goes in v6:
time: 78 us; the launch traced here: 77.9 us
  starting transfers between devices  33.8 us (43%)
  waiting for transfers between devices  19.6 us (25%)
  Pallas kernels  18.2 us (23%)
  between operations  2.56 us (3%)
  local copies, waits for them, and re-layouts  2.03 us (3%)
  other arithmetic  1.56 us (2%)
    ppermute x15, starting transfers between devices, received(): lax.ppermute(value, axis, pairs)  25.5 us
    ppermute x15, waiting for transfers between devices, received(): lax.ppermute(value, axis, pairs)  18.2 us
    pallas_call x1, Pallas kernels, compute(): pl.pallas_call(kernel, out_shape=(shape((4, SHARES, PAD), F32), shape((4,...  10.2 us
    ppermute x1, starting transfers between devices, local(): even = lax.ppermute(up, 'row', neighbours(16, False))  4.26 us
    pallas_call x1, Pallas kernels, inner(): pl.pallas_call(inner_kernel, out_shape=[shape((rows, stop - start), BF) f...  3.84 us
    ppermute x1, starting transfers between devices, local(): odd = lax.ppermute(edge, 'col', neighbours(4, True, True))  3.39 us
    pallas_call x1, Pallas kernels, prepare(): pl.pallas_call(prepare_kernel, out_shape=[shape((C, LANES), BF), shape((1...  1.62 us
  transfers between devices with their start and end apart: 19, of which 11 were waited for; matrix products, arithmetic and copies ran while one was open for 2% of the time, Pallas kernels for 7%

profile of v6, /device:TPU:1, one launch (start us, length us, event | category | flops | bytes accessed | tf_op | source)
XLA Modules:
  0.0 77.9 jit_solution(17275903285620614108)
XLA Ops:
  0.6 1.4 %copy-done = bf16[1,256,24,128]{3,2,1,0:T(8,128)(2,1)S(1)} copy-done((bf16[1,256,24,128]{3,2,1,0:T(8,128)(2,1)S(1)}, bf16[1,256,24,128]{3,2,1,0:T(8,128)(2,1)}, u32[]{:S(2)}) %copy-start) | copy-done | bytes 1572888
  2.0 1.2 %shard_map.84 = (bf16[256,3072]{1,0:T(8,128)(2,1)S(1)}, bf16[256,128]{1,0:T(8,128)(2,1)S(1)}) custom-call(bf16[1,256,24,128]{3,2,1,0:T(8,128)(2,1)S(1)} %copy-done), custom_call_target="tpu_custom_call" | custom-call | tf_op jit(solution)/shard_map/pallas_call | solution.py:607
  3.2 3.4 %collective-permute-start = (bf16[256,128]{1,0:T(8,128)(2,1)S(1)}, bf16[256,128]{1,0:T(8,128)(2,1)S(1)}, u32[]{:S(2)}, u32[]{:S(2)}) collective-permute-start(bf16[256,128]{1,0:T(8,128)(2,1)S(1)} %get-tuple-element.38), channel_id=1, source_target_pairs={{4,8},{8,4},{0,12},{12,0},{5,9},{9,5},{1,13},{13,1},{6,10},{10,6},... | collective-permute-start | bytes 196616 | tf_op jit(solution)/shard_map/ppermute | solution.py:719
  6.6 0.0 collective-permute-start.1
  6.6 0.0 copy-start.4
  6.7 0.0 copy-start.3
  6.7 1.6 %shard_map.85 = (bf16[256,3840]{1,0:T(8,128)(2,1)S(1)}, bf16[128,3840]{1,0:T(8,128)(2,1)S(1)}, bf16[64,256]{1,0:T(8,128)(2,1)S(1)}, bf16[192,192]{1,0:T(8,128)(2...) custom-call(bf16[256,3072]{1,0:T(8,128)(2,1)S(1)} %get-tuple-element, ...), custom_call_target="tpu_custom_call" | custom-call | bytes 6000000 | tf_op jit(solution)/shard_map/pallas_call | solution.py:624
  8.3 0.1 pad_add_fusion.place
  8.4 0.0 collective-permute-done.odd_ref
  8.4 1.4 %collective-permute-done.1.even_ref = bf16[256,128]{1,0:T(8,128)(2,1)S(1)} collective-permute-done((bf16[256,128]{1,0:T(8,128)(2,1)S(1)}, bf16[256,128]{1,0:T(8,128)(2,1)S(1)}, u32[]{:S(2)}, u32[]{:S(2)}) %collective-permute-start.1) | collective-permute-done | bytes 65568 | tf_op jit(solution)/shard_map/ppermute | solution.py:720
  9.7 0.7 shard_map.86
  10.5 0.7 collective-permute-start.2
  11.1 4.3 %collective-permute-start.3 = (bf16[272,256]{1,0:T(8,128)(2,1)S(1)}, bf16[272,256]{1,0:T(8,128)(2,1)S(1)}, u32[]{:S(2)}, u32[]{:S(2)}) collective-permute-start(bf16[272,256]{1,0:T(8,128)(2,1)S(1)} %get-tuple-element.42), channel_id=1, source_target_pairs={{0,16},{16,0},{32,48},{48,32},{64,80},{80,64},{96,112},{112,96},{1... | collective-permute-start | bytes 417800 | tf_op jit(solution)/shard_map/ppermute | solution.py:724
  15.4 0.1 compare_convert_fusion.target_ref
  15.5 3.8 %shard_map.87 = (bf16[256,3328]{1,0:T(8,128)(2,1)S(1)}, bf16[64,3328]{1,0:T(8,128)(2,1)S(1)}, bf16[192,3072]{1,0:T(8,128)(2,1)S(1)}, bf16[64,2816]{1,0:T(8,128)(...) custom-call(s32[4]{0:T(128)S(1)} %pad_add_fusion.place, ...), custom_call_target="tpu_custom_call" | custom-call | flops 1000000000 | bytes 12000000 | tf_op jit(solution)/shard_map/pallas_call | solution.py:658
  19.3 0.0 collective-permute-done.2.odd_ref
  19.3 0.0 collective-permute-done.3.even_ref
  19.3 10.2 %shard_map.88 = (f32[4,32,640]{2,1,0:T(8,128)S(1)}, f32[4,32,640]{2,1,0:T(8,128)S(1)}) custom-call(s32[4]{0:T(128)S(1)} %pad_add_fusion.place, bf16[256,3840]{1,0:T(8,128)(2,1)S(1)} %get-tuple-element.37.flat_ref, bf16[256,128]{1,0:T(8,128)(2,1)S(1)} %get-tuple-element.40.rim_ref, bf16[272,256]{1,0:T(8,128)(2,1)S(1)} %collective-permute-done.2.odd_ref, ...), custom_call_target="tpu_custom_call" | custom-call | tf_op jit(solution)/shard_map/pallas_call | solution.py:672
  29.6 2.6 %collective-permute-start.4 = (f32[4,32,640]{2,1,0:T(8,128)S(1)}, f32[4,32,640]{2,1,0:T(8,128)S(1)}, u32[]{:S(2)}, u32[]{:S(2)}) collective-permute-start(f32[4,32,640]{2,1,0:T(8,128)S(1)} %get-tuple-element.65), channel_id=1, source_target_pairs={{0,1},{1,0},{2,3},{3,2},{4,5},{5,4},{6,7},{7,6},{8,9},{9,8},{10,11... | collective-permute-start | bytes 983048 | tf_op jit(solution)/shard_map/ppermute | solution.py:77
  32.2 1.3 %collective-permute-done.4 = f32[4,32,640]{2,1,0:T(8,128)S(1)} collective-permute-done((f32[4,32,640]{2,1,0:T(8,128)S(1)}, f32[4,32,640]{2,1,0:T(8,128)S(1)}, u32[]{:S(2)}, u32[]{:S(2)}) %collective-permute-start.4) | collective-permute-done | bytes 327712 | tf_op jit(solution)/shard_map/ppermute | solution.py:77
  33.5 0.8 %collective-permute-start.5 = (f32[32,640]{1,0:T(8,128)S(1)}, f32[32,640]{1,0:T(8,128)S(1)}, u32[]{:S(2)}, u32[]{:S(2)}) collective-permute-start(f32[32,640]{1,0:T(8,128)S(1)} %get-tuple-element.74), channel_id=1, source_target_pairs={{0,8},{4,12},{8,0},{12,4},{1,9},{5,13},{9,1},{13,5},{2,10},{6,14},... | collective-permute-start | bytes 245768 | tf_op jit(solution)/shard_map/ppermute | solution.py:77
  34.3 1.8 %collective-permute-start.6 = (f32[32,640]{1,0:T(8,128)S(1)}, f32[32,640]{1,0:T(8,128)S(1)}, u32[]{:S(2)}, u32[]{:S(2)}) collective-permute-start(f32[32,640]{1,0:T(8,128)S(1)} %get-tuple-element.73), channel_id=1, source_target_pairs={{0,12},{4,8},{8,4},{12,0},{1,13},{5,9},{9,5},{13,1},{2,14},{6,10},... | collective-permute-start | bytes 245768 | tf_op jit(solution)/shard_map/ppermute | solution.py:77
  36.1 0.3 collective-permute-start.7
  36.4 2.5 %collective-permute-done.5 = f32[32,640]{1,0:T(8,128)S(1)} collective-permute-done((f32[32,640]{1,0:T(8,128)S(1)}, f32[32,640]{1,0:T(8,128)S(1)}, u32[]{:S(2)}, u32[]{:S(2)}) %collective-permute-start.5) | collective-permute-done | bytes 81952 | tf_op jit(solution)/shard_map/ppermute | solution.py:77
  39.0 2.5 %collective-permute-done.6 = f32[32,640]{1,0:T(8,128)S(1)} collective-permute-done((f32[32,640]{1,0:T(8,128)S(1)}, f32[32,640]{1,0:T(8,128)S(1)}, u32[]{:S(2)}, u32[]{:S(2)}) %collective-permute-start.6) | collective-permute-done | bytes 81952 | tf_op jit(solution)/shard_map/ppermute | solution.py:77
  41.4 0.0 collective-permute-done.7
  41.5 2.7 %collective-permute-start.10 = (f32[32,640]{1,0:T(8,128)S(1)}, f32[32,640]{1,0:T(8,128)S(1)}, u32[]{:S(2)}, u32[]{:S(2)}) collective-permute-start(f32[32,640]{1,0:T(8,128)S(1)} %fusion.1), channel_id=1, source_target_pairs={{0,32},{16,48},{32,0},{48,16},{64,96},{80,112},{96,64},{112,80},{1... | collective-permute-start | bytes 245768 | tf_op jit(solution)/shard_map/ppermute | solution.py:77
  44.2 0.6 collective-permute-start.8
  44.7 0.0 collective-permute-start.9
  44.7 1.6 %collective-permute-done.10 = f32[32,640]{1,0:T(8,128)S(1)} collective-permute-done((f32[32,640]{1,0:T(8,128)S(1)}, f32[32,640]{1,0:T(8,128)S(1)}, u32[]{:S(2)}, u32[]{:S(2)}) %collective-permute-start.10) | collective-permute-done | bytes 81952 | tf_op jit(solution)/shard_map/ppermute | solution.py:77
  46.3 2.3 %collective-permute-done.8 = f32[32,640]{1,0:T(8,128)S(1)} collective-permute-done((f32[32,640]{1,0:T(8,128)S(1)}, f32[32,640]{1,0:T(8,128)S(1)}, u32[]{:S(2)}, u32[]{:S(2)}) %collective-permute-start.8) | collective-permute-done | bytes 81952 | tf_op jit(solution)/shard_map/ppermute | solution.py:77
  48.7 1.7 %collective-permute-start.11 = (f32[32,640]{1,0:T(8,128)S(1)}, f32[32,640]{1,0:T(8,128)S(1)}, u32[]{:S(2)}, u32[]{:S(2)}) collective-permute-start(f32[32,640]{1,0:T(8,128)S(1)} %add_add_fusion), channel_id=1, source_target_pairs={{0,64},{1,65},{2,66},{3,67},{16,80},{17,81},{18,82},{19,83},{32,96... | collective-permute-start | bytes 245768 | tf_op jit(solution)/shard_map/ppermute | solution.py:77
  50.4 1.8 %collective-permute-done.11 = f32[32,640]{1,0:T(8,128)S(1)} collective-permute-done((f32[32,640]{1,0:T(8,128)S(1)}, f32[32,640]{1,0:T(8,128)S(1)}, u32[]{:S(2)}, u32[]{:S(2)}) %collective-permute-start.11) | collective-permute-done | bytes 81952 | tf_op jit(solution)/shard_map/ppermute | solution.py:77
  52.3 8.2 %collective-permute-start.12 = (f32[32,640]{1,0:T(8,128)S(1)}, f32[32,640]{1,0:T(8,128)S(1)}, u32[]{:S(2)}, u32[]{:S(2)}) collective-permute-start(f32[32,640]{1,0:T(8,128)S(1)} %add.81.own), channel_id=1, source_target_pairs={{0,66},{1,67},{2,64},{3,65},{16,82},{17,83},{18,80},{19,81},{32,98... | collective-permute-start | bytes 245768 | tf_op jit(solution)/shard_map/ppermute | solution.py:77
  60.5 0.0 collective-permute-start.13
  60.5 1.6 %collective-permute-start.14 = (f32[32,640]{1,0:T(8,128)S(1)}, f32[32,640]{1,0:T(8,128)S(1)}, u32[]{:S(2)}, u32[]{:S(2)}) collective-permute-start(f32[32,640]{1,0:T(8,128)S(1)} %add.81.own), channel_id=1, source_target_pairs={{0,192},{1,193},{2,194},{3,195},{16,208},{17,209},{18,210},{19,211... | collective-permute-start | bytes 245768 | tf_op jit(solution)/shard_map/ppermute | solution.py:77
  62.1 1.5 %collective-permute-done.12.got_a = f32[32,640]{1,0:T(8,128)S(1)} collective-permute-done((f32[32,640]{1,0:T(8,128)S(1)}, f32[32,640]{1,0:T(8,128)S(1)}, u32[]{:S(2)}, u32[]{:S(2)}) %collective-permute-start.12) | collective-permute-done | bytes 81952 | tf_op jit(solution)/shard_map/ppermute | solution.py:77
  63.6 3.4 %collective-permute-done.13.got_b = f32[32,640]{1,0:T(8,128)S(1)} collective-permute-done((f32[32,640]{1,0:T(8,128)S(1)}, f32[32,640]{1,0:T(8,128)S(1)}, u32[]{:S(2)}, u32[]{:S(2)}) %collective-permute-start.13) | collective-permute-done | bytes 81952 | tf_op jit(solution)/shard_map/ppermute | solution.py:77
  67.0 0.6 shard_map.89
  67.7 2.5 %collective-permute-start.15 = (f32[1,640]{1,0:T(1,128)S(1)}, f32[1,640]{1,0:T(1,128)S(1)}, u32[]{:S(2)}, u32[]{:S(2)}) collective-permute-start(f32[1,640]{1,0:T(1,128)S(1)} %get-tuple-element.67), channel_id=1, source_target_pairs={{0,1},{1,0},{2,3},{3,2},{4,5},{5,4},{6,7},{7,6},{8,9},{9,8},{10,11... | collective-permute-start | bytes 7688 | tf_op jit(solution)/shard_map/ppermute | solution.py:77
  70.2 0.8 %collective-permute-done.15 = f32[1,640]{1,0:T(1,128)S(1)} collective-permute-done((f32[1,640]{1,0:T(1,128)S(1)}, f32[1,640]{1,0:T(1,128)S(1)}, u32[]{:S(2)}, u32[]{:S(2)}) %collective-permute-start.15) | collective-permute-done | bytes 2592 | tf_op jit(solution)/shard_map/ppermute | solution.py:77
  71.0 0.2 collective-permute-start.16
  71.2 2.1 %collective-permute-start.17 = (f32[1,640]{1,0:T(1,128)S(1)}, f32[1,640]{1,0:T(1,128)S(1)}, u32[]{:S(2)}, u32[]{:S(2)}) collective-permute-start(f32[1,640]{1,0:T(1,128)S(1)} %add.82), channel_id=1, source_target_pairs={{0,12},{4,8},{8,4},{12,0},{1,13},{5,9},{9,5},{13,1},{2,14},{6,10},... | collective-permute-start | bytes 7688 | tf_op jit(solution)/shard_map/ppermute | solution.py:77
  73.3 0.3 collective-permute-start.18
  73.6 0.6 multiply_add_fusion
  74.2 0.6 slice.27
  75.5 0.6 collective-permute-done.18
  76.0 0.7 multiply_subtract_fusion
  (21 shorter events, 0.2 us)
Async XLA Ops:
  0.6 1.4 %copy-start = (bf16[1,256,24,128]{3,2,1,0:T(8,128)(2,1)S(1)}, bf16[1,256,24,128]{3,2,1,0:T(8,128)(2,1)}, u32[]{:S(2)}) copy-start(bf16[1,256,24,128]{3,2,1,0:T(8,128)(2,1)} %image_ref.1) | copy-start | bytes 4718596
  2.0 4.6 %copy-start.1 = (f32[141312]{0:T(1024)S(1)}, f32[141312]{0:T(1024)}, u32[]{:S(2)}) copy-start(f32[141312]{0:T(1024)} %param.7) | copy-start | bytes 1695748
  2.0 4.6 %copy-start.2 = (f32[8,3840]{1,0:T(8,128)S(1)}, f32[8,3840]{1,0:T(8,128)}, u32[]{:S(2)}) copy-start(f32[8,3840]{1,0:T(8,128)} %constant.67.clone.table) | copy-start | bytes 368644
  3.2 5.1 %collective-permute-start = (bf16[256,128]{1,0:T(8,128)(2,1)S(1)}, bf16[256,128]{1,0:T(8,128)(2,1)S(1)}, u32[]{:S(2)}, u32[]{:S(2)}) collective-permute-start(bf16[256,128]{1,0:T(8,128)(2,1)S(1)} %get-tuple-element.38), channel_id=1, source_target_pairs={{4,8},{8,4},{0,12},{12,0},{5,9},{9,5},{1,13},{13,1},{6,10},{10,6},... | collective-permute-start | bytes 196616 | tf_op jit(solution)/shard_map/ppermute | solution.py:719
  6.6 3.1 %collective-permute-start.1 = (bf16[256,128]{1,0:T(8,128)(2,1)S(1)}, bf16[256,128]{1,0:T(8,128)(2,1)S(1)}, u32[]{:S(2)}, u32[]{:S(2)}) collective-permute-start(bf16[256,128]{1,0:T(8,128)(2,1)S(1)} %get-tuple-element.38), channel_id=1, source_target_pairs={{0,4},{4,0},{8,12},{12,8},{1,5},{5,1},{9,13},{13,9},{2,6},{6,2},{1... | collective-permute-start | bytes 196616 | tf_op jit(solution)/shard_map/ppermute | solution.py:720
  6.6 8.7 %copy-start.4 = (s32[1,1,2]{2,1,0:T(1,128)S(1)}, s32[1,1,2]{2,1,0:T(1,128)}, u32[]{:S(2)}) copy-start(s32[1,1,2]{2,1,0:T(1,128)} %param.6) | copy-start | bytes 28
  6.7 8.8 %copy-start.3 = (f32[552]{0:T(1024)S(1)}, f32[552]{0:T(1024)}, u32[]{:S(2)}) copy-start(f32[552]{0:T(1024)} %param.8) | copy-start | bytes 6628
  10.5 8.9 %collective-permute-start.2 = (bf16[272,256]{1,0:T(8,128)(2,1)S(1)}, bf16[272,256]{1,0:T(8,128)(2,1)S(1)}, u32[]{:S(2)}, u32[]{:S(2)}) collective-permute-start(bf16[272,256]{1,0:T(8,128)(2,1)S(1)} %get-tuple-element.41), channel_id=1, source_target_pairs={{16,32},{32,16},{48,64},{64,48},{80,96},{96,80},{112,128},{128,112... | collective-permute-start | bytes 417800 | tf_op jit(solution)/shard_map/ppermute | solution.py:723
  11.1 8.2 %collective-permute-start.3 = (bf16[272,256]{1,0:T(8,128)(2,1)S(1)}, bf16[272,256]{1,0:T(8,128)(2,1)S(1)}, u32[]{:S(2)}, u32[]{:S(2)}) collective-permute-start(bf16[272,256]{1,0:T(8,128)(2,1)S(1)} %get-tuple-element.42), channel_id=1, source_target_pairs={{0,16},{16,0},{32,48},{48,32},{64,80},{80,64},{96,112},{112,96},{1... | collective-permute-start | bytes 417800 | tf_op jit(solution)/shard_map/ppermute | solution.py:724
  29.6 3.8 %collective-permute-start.4 = (f32[4,32,640]{2,1,0:T(8,128)S(1)}, f32[4,32,640]{2,1,0:T(8,128)S(1)}, u32[]{:S(2)}, u32[]{:S(2)}) collective-permute-start(f32[4,32,640]{2,1,0:T(8,128)S(1)} %get-tuple-element.65), channel_id=1, source_target_pairs={{0,1},{1,0},{2,3},{3,2},{4,5},{5,4},{6,7},{7,6},{8,9},{9,8},{10,11... | collective-permute-start | bytes 983048 | tf_op jit(solution)/shard_map/ppermute | solution.py:77
  33.5 5.5 %collective-permute-start.5 = (f32[32,640]{1,0:T(8,128)S(1)}, f32[32,640]{1,0:T(8,128)S(1)}, u32[]{:S(2)}, u32[]{:S(2)}) collective-permute-start(f32[32,640]{1,0:T(8,128)S(1)} %get-tuple-element.74), channel_id=1, source_target_pairs={{0,8},{4,12},{8,0},{12,4},{1,9},{5,13},{9,1},{13,5},{2,10},{6,14},... | collective-permute-start | bytes 245768 | tf_op jit(solution)/shard_map/ppermute | solution.py:77
  34.3 7.1 %collective-permute-start.6 = (f32[32,640]{1,0:T(8,128)S(1)}, f32[32,640]{1,0:T(8,128)S(1)}, u32[]{:S(2)}, u32[]{:S(2)}) collective-permute-start(f32[32,640]{1,0:T(8,128)S(1)} %get-tuple-element.73), channel_id=1, source_target_pairs={{0,12},{4,8},{8,4},{12,0},{1,13},{5,9},{9,5},{13,1},{2,14},{6,10},... | collective-permute-start | bytes 245768 | tf_op jit(solution)/shard_map/ppermute | solution.py:77
  36.1 5.3 %collective-permute-start.7 = (f32[32,640]{1,0:T(8,128)S(1)}, f32[32,640]{1,0:T(8,128)S(1)}, u32[]{:S(2)}, u32[]{:S(2)}) collective-permute-start(f32[32,640]{1,0:T(8,128)S(1)} %get-tuple-element.72), channel_id=1, source_target_pairs={{0,4},{4,0},{8,12},{12,8},{1,5},{5,1},{9,13},{13,9},{2,6},{6,2},{1... | collective-permute-start | bytes 245768 | tf_op jit(solution)/shard_map/ppermute | solution.py:77
  41.5 4.9 %collective-permute-start.10 = (f32[32,640]{1,0:T(8,128)S(1)}, f32[32,640]{1,0:T(8,128)S(1)}, u32[]{:S(2)}, u32[]{:S(2)}) collective-permute-start(f32[32,640]{1,0:T(8,128)S(1)} %fusion.1), channel_id=1, source_target_pairs={{0,32},{16,48},{32,0},{48,16},{64,96},{80,112},{96,64},{112,80},{1... | collective-permute-start | bytes 245768 | tf_op jit(solution)/shard_map/ppermute | solution.py:77
  44.2 4.5 %collective-permute-start.8 = (f32[32,640]{1,0:T(8,128)S(1)}, f32[32,640]{1,0:T(8,128)S(1)}, u32[]{:S(2)}, u32[]{:S(2)}) collective-permute-start(f32[32,640]{1,0:T(8,128)S(1)} %fusion.1), channel_id=1, source_target_pairs={{0,48},{16,32},{32,16},{48,0},{64,112},{80,96},{96,80},{112,64},{1... | collective-permute-start | bytes 245768 | tf_op jit(solution)/shard_map/ppermute | solution.py:77
  44.7 3.9 %collective-permute-start.9 = (f32[32,640]{1,0:T(8,128)S(1)}, f32[32,640]{1,0:T(8,128)S(1)}, u32[]{:S(2)}, u32[]{:S(2)}) collective-permute-start(f32[32,640]{1,0:T(8,128)S(1)} %fusion.1), channel_id=1, source_target_pairs={{0,16},{16,0},{32,48},{48,32},{64,80},{80,64},{96,112},{112,96},{1... | collective-permute-start | bytes 245768 | tf_op jit(solution)/shard_map/ppermute | solution.py:77
  48.7 3.6 %collective-permute-start.11 = (f32[32,640]{1,0:T(8,128)S(1)}, f32[32,640]{1,0:T(8,128)S(1)}, u32[]{:S(2)}, u32[]{:S(2)}) collective-permute-start(f32[32,640]{1,0:T(8,128)S(1)} %add_add_fusion), channel_id=1, source_target_pairs={{0,64},{1,65},{2,66},{3,67},{16,80},{17,81},{18,82},{19,83},{32,96... | collective-permute-start | bytes 245768 | tf_op jit(solution)/shard_map/ppermute | solution.py:77
  52.3 11.4 %collective-permute-start.12 = (f32[32,640]{1,0:T(8,128)S(1)}, f32[32,640]{1,0:T(8,128)S(1)}, u32[]{:S(2)}, u32[]{:S(2)}) collective-permute-start(f32[32,640]{1,0:T(8,128)S(1)} %add.81.own), channel_id=1, source_target_pairs={{0,66},{1,67},{2,64},{3,65},{16,82},{17,83},{18,80},{19,81},{32,98... | collective-permute-start | bytes 245768 | tf_op jit(solution)/shard_map/ppermute | solution.py:77
  60.5 6.5 %collective-permute-start.13 = (f32[32,640]{1,0:T(8,128)S(1)}, f32[32,640]{1,0:T(8,128)S(1)}, u32[]{:S(2)}, u32[]{:S(2)}) collective-permute-start(f32[32,640]{1,0:T(8,128)S(1)} %add.81.own), channel_id=1, source_target_pairs={{0,194},{1,195},{2,192},{3,193},{16,210},{17,211},{18,208},{19,209... | collective-permute-start | bytes 245768 | tf_op jit(solution)/shard_map/ppermute | solution.py:77
  60.5 6.5 %collective-permute-start.14 = (f32[32,640]{1,0:T(8,128)S(1)}, f32[32,640]{1,0:T(8,128)S(1)}, u32[]{:S(2)}, u32[]{:S(2)}) collective-permute-start(f32[32,640]{1,0:T(8,128)S(1)} %add.81.own), channel_id=1, source_target_pairs={{0,192},{1,193},{2,194},{3,195},{16,208},{17,209},{18,210},{19,211... | collective-permute-start | bytes 245768 | tf_op jit(solution)/shard_map/ppermute | solution.py:77
  67.7 3.3 %collective-permute-start.15 = (f32[1,640]{1,0:T(1,128)S(1)}, f32[1,640]{1,0:T(1,128)S(1)}, u32[]{:S(2)}, u32[]{:S(2)}) collective-permute-start(f32[1,640]{1,0:T(1,128)S(1)} %get-tuple-element.67), channel_id=1, source_target_pairs={{0,1},{1,0},{2,3},{3,2},{4,5},{5,4},{6,7},{7,6},{8,9},{9,8},{10,11... | collective-permute-start | bytes 7688 | tf_op jit(solution)/shard_map/ppermute | solution.py:77
  71.0 4.5 %collective-permute-start.16 = (f32[1,640]{1,0:T(1,128)S(1)}, f32[1,640]{1,0:T(1,128)S(1)}, u32[]{:S(2)}, u32[]{:S(2)}) collective-permute-start(f32[1,640]{1,0:T(1,128)S(1)} %add.82), channel_id=1, source_target_pairs={{0,8},{4,12},{8,0},{12,4},{1,9},{5,13},{9,1},{13,5},{2,10},{6,14},... | collective-permute-start | bytes 7688 | tf_op jit(solution)/shard_map/ppermute | solution.py:77
  71.2 4.3 %collective-permute-start.17 = (f32[1,640]{1,0:T(1,128)S(1)}, f32[1,640]{1,0:T(1,128)S(1)}, u32[]{:S(2)}, u32[]{:S(2)}) collective-permute-start(f32[1,640]{1,0:T(1,128)S(1)} %add.82), channel_id=1, source_target_pairs={{0,12},{4,8},{8,4},{12,0},{1,13},{5,9},{9,5},{13,1},{2,14},{6,10},... | collective-permute-start | bytes 7688 | tf_op jit(solution)/shard_map/ppermute | solution.py:77
  73.3 2.7 %collective-permute-start.18 = (f32[1,640]{1,0:T(1,128)S(1)}, f32[1,640]{1,0:T(1,128)S(1)}, u32[]{:S(2)}, u32[]{:S(2)}) collective-permute-start(f32[1,640]{1,0:T(1,128)S(1)} %add.82), channel_id=1, source_target_pairs={{0,4},{4,0},{8,12},{12,8},{1,5},{5,1},{9,13},{13,9},{2,6},{6,2},{1... | collective-permute-start | bytes 7688 | tf_op jit(solution)/shard_map/ppermute | solution.py:77

commit v7 on v6

--- a/solution.py
+++ b/solution.py
@@ -30,7 +30,8 @@
 F32 = jnp.float32
 ZERO = np.zeros((), BF)
 
-SHARES = 32
+REST = 40
+LINES = 144
 CORNERS = 16
 MSG = (C + CORNERS, HALO * 128)
 PAD = 640
@@ -134,15 +135,18 @@
     return Lanes((base, base + ref.shape[1], ref, base))
 
 
-def split_kernel(image_ref, own_ref, edge_ref, tall, select):
+def split_kernel(image_ref, own_ref, left_ref, right_ref, tall, select):
     tall[...] = image_ref[0].astype(F32).reshape(C * TILE_ROWS, 128)
     lane = lax.broadcasted_iota(jnp.int32, (128, 128), 1)
     col = lax.broadcasted_iota(jnp.int32, (128, 128), 0)
-    wanted = jnp.where(col < HALO, col + 4, jnp.where(col >= 126, col - 124, -1000))
+    wanted = jnp.where(col < HALO, col + 64, jnp.where(col >= 126, col - 126, -1000))
     for r in range(TILE_ROWS):
         own_ref[:, r * 128 : (r + 1) * 128] = tall[pl.ds(r, C, stride=TILE_ROWS), :].astype(BF)
-        select[r * 128 : (r + 1) * 128, :] = (lane - 4 * r == wanted).astype(F32).astype(BF)
-    edge_ref[...] = nn(own_ref[...], select[...]).astype(BF)
+        select[r * 128 : (r + 1) * 128, :] = (lane - 2 * r == wanted).astype(F32).astype(BF)
+    edges = nn(own_ref[...], select[...])
+    low, high = edges[:128], edges[128:]
+    right_ref[...] = jnp.where(lane < 64, low, pltpu.roll(high, 64, 1)).astype(BF)
+    left_ref[...] = jnp.where(lane < 64, pltpu.roll(low, 64, 1), high).astype(BF)
 
 
 def prepare_kernel(
@@ -209,13 +213,14 @@
 
 def rim_kernel(place, own_ref, odd_ref, even_ref, _, rim_ref, up_ref, down_ref):
     row, col = place[0], place[1]
-    on_left = lax.rem(lax.broadcasted_iota(jnp.int32, (C, 128), 1), 4) >= 2
-    odd_col = lax.rem(col, 2)
-    from_even = even_ref[...].astype(F32)
-    from_odd = odd_ref[...].astype(F32)
-    by_even = on_left.astype(jnp.int32) == odd_col
-    outside = (on_left & (col == 0)) | (~on_left & (col == 3))
-    rim = jnp.where(outside, 0.0, jnp.where(by_even, from_even, from_odd)).astype(BF)
+    lane = lax.broadcasted_iota(jnp.int32, (128, 128), 1)
+    odd_col = lax.rem(col, 2) == 1
+    odd, even = odd_ref[...].astype(F32), even_ref[...].astype(F32)
+    from_left = jnp.where(col == 0, 0.0, jnp.where(odd_col, even, odd))
+    from_right = jnp.where(col == 3, 0.0, jnp.where(odd_col, odd, even))
+    low = jnp.where(lane < 64, from_left, pltpu.roll(from_right, 64, 1))
+    high = jnp.where(lane < 64, pltpu.roll(from_left, 64, 1), from_right)
+    rim = jnp.concatenate([low, high], axis=0).astype(BF)
     rim_ref[...] = rim
     odd_row = lax.rem(row, 2)
     corner = lax.broadcasted_iota(jnp.int32, (CORNERS, 128), 0)
@@ -223,8 +228,7 @@
     for ref, low in ((up_ref, odd_row), (down_ref, 1 - odd_row)):
         first = (1 - low) * (TILE_ROWS - HALO)
         ref[0:C, :] = own_ref[:, pl.ds(pl.multiple_of(first * 128, 128), HALO * 128)]
-        row_of, pixel = lax.rem(corner, 4) // 2, lax.rem(corner, 2)
-        wanted = 4 * (first + row_of) + pixel + jnp.where(corner < 4, 2, 4)
+        wanted = 2 * first + jnp.where(corner < 4, corner, 64 + corner - 4)
         pick = ((source == wanted) & (corner < 8)).astype(F32).astype(BF)
         ref[C:, :] = nt(pick, rim).astype(BF)
 
@@ -247,10 +251,13 @@
 
 
 def put_rim(ref, rim, start, stop):
-    for b in range(TILE_ROWS + 1):
-        lane = (b + HALO) * COLS - HALO
-        if start <= lane and lane + 2 * HALO <= stop:
-            ref[:, lane - start : lane - start + 2 * HALO] = rim[:, 4 * b : 4 * b + 4]
+    for r in range(TILE_ROWS):
+        for source, lane in (
+            (2 * r, (r + HALO) * COLS),
+            (64 + 2 * r, (r + HALO + 1) * COLS - HALO),
+        ):
+            if start <= lane and lane + HALO <= stop:
+                ref[:, lane - start : lane - start + HALO] = rim[:, source : source + HALO]
 
 
 def enter(inputs, win_t, h1, ranges, mask):
@@ -352,6 +359,11 @@
             leave(y1, wide, wout_t2, h2b, y2, y2_pieces),
         ]
     )
+
+
+def rest_of(share):
+    group = lax.div(share, 8)
+    return 128 + 8 * lax.div(group, 3) + lax.rem(share, 8), lax.rem(group, 3)
 
 
 def kernel(
@@ -563,12 +575,21 @@
                 for j in range(6)
             ]
             block = parts.at[m_core ^ core, m_col ^ col]
-            for j in range(5):
-                value = jnp.where(lane < 128 - offset, lines[j], lines[j + 1])
-                if j == 4:
-                    value = jnp.where(lane < 40, value, jnp.where(lane == 40, loss, 0.0))
-                begin = m_far * 16 + low
-                block[begin : begin + 8, j * 128 : (j + 1) * 128] = value
+            for j in range(4):
+                begin = 32 * j + 16 * m_far + low
+                block[begin : begin + 8, :] = jnp.where(lane < 128 - offset, lines[j], lines[j + 1])
+            group = 2 * m_far + low // 8
+            begin, at = 128 + 8 * (group // 3), REST * (group % 3)
+            rest = [pltpu.roll(line, at, 1) if at else line for line in lines[4:6]]
+            value = jnp.where(lane - at < 128 - offset, rest[0], rest[1])
+            if group == 3:
+                value = jnp.where(lane < REST, value, jnp.where(lane == 127, loss, 0.0))
+                block[begin : begin + 8, :] = value
+            elif group == 2:
+                value = jnp.where(lane < at + REST, value, 0.0)
+                block[begin : begin + 8, at:] = value[:, at:]
+            else:
+                block[begin : begin + 8, at : at + REST] = value[:, at : at + REST]
 
     emit(
         [(own, seed)]
@@ -578,20 +599,35 @@
 
     pack_shares(0)
     mine = far * 16 + row
-    parts[0, 0, pl.ds(mine, 1), :] = parts[0, 0, pl.ds(mine, 1), :] + 9.0 * momentum_ref[...]
+    for j in range(4):
+        line = pl.ds(32 * j + mine, 1)
+        parts[0, 0, line, :] += 9.0 * momentum_ref[:, j * 128 : (j + 1) * 128]
+    line, turn = rest_of(mine)
+    rest = 9.0 * momentum_ref[:, 512:]
+    for k in range(3):
+        parts[0, 0, pl.ds(line, 1), :] += jnp.where(turn == k, pltpu.roll(rest, REST * k, 1) if k else rest, 0.0)
     keep_ref[...] = parts[0]
     send_ref[...] = parts[1]
 
 
-def total_kernel(place, own, got_a, got_b, got_c, row_ref, size_ref):
-    total = (own[...] + got_a[...]) + (got_b[...] + got_c[...])
-    lane = lax.broadcasted_iota(jnp.int32, (SHARES, PAD), 1)
-    kept = jnp.where(lane < SHARE, jnp.abs(total), 0.0)
+def total_kernel(place, own, got_a, got_b, got_c, row_ref, size_ref, total):
+    total[...] = (own[...] + got_a[...]) + (got_b[...] + got_c[...])
+    lane = lax.broadcasted_iota(jnp.int32, (LINES, 128), 1)
+    line = lax.broadcasted_iota(jnp.int32, (LINES, 128), 0)
+    kept = jnp.where((line >= LINES - 8) & (lane >= REST), 0.0, jnp.abs(total[...]))
     size = jnp.sum(jnp.sum(kept, axis=0, keepdims=True), axis=1, keepdims=True)
     size_ref[...] = jnp.broadcast_to(size, (1, PAD))
     mine = place[3] * 16 + place[0]
-    line = lax.broadcasted_iota(jnp.int32, (SHARES, PAD), 0)
-    row_ref[...] = jnp.sum(jnp.where(line == mine, total, 0.0), axis=0, keepdims=True)
+    for j in range(4):
+        row_ref[:, j * 128 : (j + 1) * 128] = total[pl.ds(32 * j + mine, 1), :]
+    at, turn = rest_of(mine)
+    rest = total[pl.ds(at, 1), :]
+    value = jnp.where(turn == 0, rest, 0.0)
+    for k in (1, 2):
+        value = value + jnp.where(turn == k, pltpu.roll(rest, 128 - REST * k, 1), 0.0)
+    lane = lax.broadcasted_iota(jnp.int32, (1, 128), 1)
+    loss = total[LINES - 1 : LINES, 127:128]
+    row_ref[:, 512:] = jnp.where(lane < REST, value, jnp.where(lane == REST, loss, 0.0))
 
 
 VMEM = pl.BlockSpec(memory_space=pltpu.VMEM)
@@ -606,9 +642,9 @@
 def split(image):
     return pl.pallas_call(
         split_kernel,
-        out_shape=(shape((C, TILE_ROWS * 128), BF), shape((C, 128), BF)),
+        out_shape=(shape((C, TILE_ROWS * 128), BF), shape((C // 2, 128), BF), shape((C // 2, 128), BF)),
         in_specs=[VMEM],
-        out_specs=(VMEM, VMEM),
+        out_specs=(VMEM,) * 3,
         scratch_shapes=[
             pltpu.VMEM((C * TILE_ROWS, 128), F32),
             pltpu.VMEM((TILE_ROWS * 128, 128), BF),
@@ -671,12 +707,12 @@
 def compute(place, flat, beyond, odd, even, table, momentum, mats, mids):
     return pl.pallas_call(
         kernel,
-        out_shape=(shape((4, SHARES, PAD), F32), shape((4, SHARES, PAD), F32)),
+        out_shape=(shape((4, LINES, 128), F32), shape((4, LINES, 128), F32)),
         in_specs=[SMEM] + [VMEM] * 28,
         out_specs=(VMEM, VMEM),
         scratch_shapes=[
             pltpu.VMEM((PARAM // 128 + 8, 128), F32),
-            pltpu.VMEM((2, 4, SHARES, PAD), F32),
+            pltpu.VMEM((2, 4, LINES, 128), F32),
             pltpu.VMEM((2, C, CHUNK), BF),
             pltpu.VMEM((2, MID, CHUNK + 256), BF),
             pltpu.VMEM((2, 3 * MID, CHUNK), BF),
@@ -703,7 +739,7 @@
     inside = real & (r >= 0) & (r < TILE_ROWS)
     tiles = [inside & (c >= t * TILE_COLS) & (c < (t + 1) * TILE_COLS) for t in range(2)]
     near = real & (r >= -1) & (r <= TILE_ROWS) & (c >= -1) & (c <= 2 * TILE_COLS)
-    lane = np.where(c < 0, 4 * r + c + 4, np.where(c >= 128, 4 * r + c - 124, -1000))
+    lane = np.where(c < 0, 2 * r + c + HALO, np.where(c >= 128, 64 + 2 * r + c - 128, -1000))
     lane = np.where(real & (r >= 0) & (r < TILE_ROWS), lane, -1000)
     return jnp.asarray(np.stack([*tiles, near, r, c, lane, 0 * r, 0 * r]).astype(np.float32))
 
@@ -715,9 +751,10 @@
     targets = (labels.reshape(2, 1) == jnp.arange(CLASSES, dtype=jnp.int32)).astype(F32)
     padded_momentum = jnp.pad(momentum, (0, PAD - SHARE)).reshape(1, PAD)
 
-    own, edge = split(image)
-    odd = lax.ppermute(edge, "col", neighbours(4, True, True))
-    even = lax.ppermute(edge, "col", neighbours(4, False))
+    own, left, right = split(image)
+    odd_col = col % 2 == 1
+    odd = lax.ppermute(jnp.where(odd_col, right, left), "col", neighbours(4, True, True))
+    even = lax.ppermute(jnp.where(odd_col, left, right), "col", neighbours(4, False))
     flat, spot, *mats = prepare(own, weights, table)
     beyond, up, down = rim(place, own, odd, even, mats[-1])
     odd = lax.ppermute(down, "row", neighbours(16, True))
@@ -737,6 +774,7 @@
         out_shape=(shape((1, PAD), F32), shape((1, PAD), F32)),
         in_specs=[SMEM] + [VMEM] * 4,
         out_specs=(VMEM, VMEM),
+        scratch_shapes=[pltpu.VMEM((LINES, 128), F32)],
         compiler_params=PARAMS,
     )(place, parts, *got)
     for stage in (CORE, X_RING):

time: 78 us -> 78.1 us (level)
  waiting for transfers between devices: 19.6 us -> 18.4 us
    ppermute x15, waiting for transfers between devices: 18.2 us -> 17.4 us  [received(): lax.ppermute(value, axis, pairs)]
  transfers between devices with their start and end apart: 19 -> 19, of which waited for: 11 -> 12; matrix products, arithmetic and copies ran while one was open for 2% -> 2% of each run, Pallas kernels for 7% -> 7%
where the time goes in v7:
time: 78.1 us; the launch traced here: 77.7 us
  starting transfers between devices  34.1 us (44%)
  Pallas kernels  18.9 us (24%)
  waiting for transfers between devices  18.4 us (24%)
  between operations  2.57 us (3%)
  local copies, waits for them, and re-layouts  2.03 us (3%)
  other arithmetic  1.56 us (2%)
    ppermute x15, starting transfers between devices, received(): lax.ppermute(value, axis, pairs)  25.8 us
    ppermute x15, waiting for transfers between devices, received(): lax.ppermute(value, axis, pairs)  17.4 us
    pallas_call x1, Pallas kernels, compute(): pl.pallas_call(kernel, out_shape=(shape((4, LINES, 128), F32), shape((4,...  10.8 us
    ppermute x1, starting transfers between devices, local(): even = lax.ppermute(up, 'row', neighbours(16, False))  4.26 us
    pallas_call x1, Pallas kernels, inner(): pl.pallas_call(inner_kernel, out_shape=[shape((rows, stop - start), BF) f...  3.83 us
    ppermute x1, starting transfers between devices, local(): lax.ppermute(jnp.where(odd_col, right, left), 'col', neighbours(4, True,...  3.39 us
    pallas_call x1, Pallas kernels, prepare(): pl.pallas_call(prepare_kernel, out_shape=[shape((C, LANES), BF), shape((1...  1.62 us
  transfers between devices with their start and end apart: 19, of which 12 were waited for; matrix products, arithmetic and copies ran while one was open for 2% of the time, Pallas kernels for 7%

profile of v7, /device:TPU:1, one launch (start us, length us, event | category | flops | bytes accessed | tf_op | source)
XLA Modules:
  0.0 77.7 jit_solution(8077454762138195506)
XLA Ops:
  0.7 1.4 %copy-done = bf16[1,256,24,128]{3,2,1,0:T(8,128)(2,1)S(1)} copy-done((bf16[1,256,24,128]{3,2,1,0:T(8,128)(2,1)S(1)}, bf16[1,256,24,128]{3,2,1,0:T(8,128)(2,1)}, u32[]{:S(2)}) %copy-start) | copy-done | bytes 1572888
  2.1 1.3 %shard_map.84 = (bf16[256,3072]{1,0:T(8,128)(2,1)S(1)}, bf16[128,128]{1,0:T(8,128)(2,1)S(1)}, bf16[128,128]{1,0:T(8,128)(2,1)S(1)}) custom-call(bf16[1,256,24,128]{3,2,1,0:T(8,128)(2,1)S(1)} %copy-done), custom_call_target="tpu_custom_call" | custom-call | tf_op jit(solution)/shard_map/pallas_call | solution.py:643
  3.3 3.4 %collective-permute-start = (bf16[128,128]{1,0:T(8,128)(2,1)S(1)}, bf16[128,128]{1,0:T(8,128)(2,1)S(1)}, u32[]{:S(2)}, u32[]{:S(2)}) collective-permute-start(bf16[128,128]{1,0:T(8,128)(2,1)S(1)} %get-tuple-element.78), channel_id=1, source_target_pairs={{4,8},{8,4},{0,12},{12,0},{5,9},{9,5},{1,13},{13,1},{6,10},{10,6},... | collective-permute-start | bytes 98312 | tf_op jit(solution)/shard_map/ppermute | solution.py:756
  6.7 0.0 collective-permute-start.1
  6.7 0.1 pad_add_fusion.place
  6.8 0.0 copy-start.3
  6.8 1.6 %shard_map.85 = (bf16[256,3840]{1,0:T(8,128)(2,1)S(1)}, bf16[128,3840]{1,0:T(8,128)(2,1)S(1)}, bf16[64,256]{1,0:T(8,128)(2,1)S(1)}, bf16[192,192]{1,0:T(8,128)(2...) custom-call(bf16[256,3072]{1,0:T(8,128)(2,1)S(1)} %get-tuple-element, ...), custom_call_target="tpu_custom_call" | custom-call | bytes 6000000 | tf_op jit(solution)/shard_map/pallas_call | solution.py:660
  8.5 0.0 collective-permute-done.odd_ref
  8.5 1.0 %collective-permute-done.1.even_ref = bf16[128,128]{1,0:T(8,128)(2,1)S(1)} collective-permute-done((bf16[128,128]{1,0:T(8,128)(2,1)S(1)}, bf16[128,128]{1,0:T(8,128)(2,1)S(1)}, u32[]{:S(2)}, u32[]{:S(2)}) %collective-permute-start.1) | collective-permute-done | bytes 32800 | tf_op jit(solution)/shard_map/ppermute | solution.py:757
  9.5 0.8 shard_map.86
  10.3 0.7 collective-permute-start.2
  10.9 4.3 %collective-permute-start.3 = (bf16[272,256]{1,0:T(8,128)(2,1)S(1)}, bf16[272,256]{1,0:T(8,128)(2,1)S(1)}, u32[]{:S(2)}, u32[]{:S(2)}) collective-permute-start(bf16[272,256]{1,0:T(8,128)(2,1)S(1)} %get-tuple-element.44), channel_id=1, source_target_pairs={{0,16},{16,0},{32,48},{48,32},{64,80},{80,64},{96,112},{112,96},{1... | collective-permute-start | bytes 417800 | tf_op jit(solution)/shard_map/ppermute | solution.py:761
  15.2 0.1 compare_convert_fusion.target_ref
  15.3 3.8 %shard_map.87 = (bf16[256,3328]{1,0:T(8,128)(2,1)S(1)}, bf16[64,3328]{1,0:T(8,128)(2,1)S(1)}, bf16[192,3072]{1,0:T(8,128)(2,1)S(1)}, bf16[64,2816]{1,0:T(8,128)(...) custom-call(s32[4]{0:T(128)S(1)} %pad_add_fusion.place, ...), custom_call_target="tpu_custom_call" | custom-call | flops 1000000000 | bytes 12000000 | tf_op jit(solution)/shard_map/pallas_call | solution.py:694
  19.1 0.0 collective-permute-done.2.odd_ref
  19.1 0.0 collective-permute-done.3.even_ref
  19.1 10.8 %shard_map.88 = (f32[4,144,128]{2,1,0:T(8,128)S(1)}, f32[4,144,128]{2,1,0:T(8,128)S(1)}) custom-call(s32[4]{0:T(128)S(1)} %pad_add_fusion.place, bf16[256,3840]{1,0:T(8,128)(2,1)S(1)} %get-tuple-element.38.flat_ref, bf16[256,128]{1,0:T(8,128)(2,1)S(1)} %get-tuple-element.42.rim_ref, bf16[272,256]{1,0:T(8,128)(2,1)S(1)} %collective-permute-done.2.odd_ref, ...), custom_call_target="tpu_custom_call" | custom-call | tf_op jit(solution)/shard_map/pallas_call | solution.py:708
  30.0 2.8 %collective-permute-start.4 = (f32[4,144,128]{2,1,0:T(8,128)S(1)}, f32[4,144,128]{2,1,0:T(8,128)S(1)}, u32[]{:S(2)}, u32[]{:S(2)}) collective-permute-start(f32[4,144,128]{2,1,0:T(8,128)S(1)} %get-tuple-element.67), channel_id=1, source_target_pairs={{0,1},{1,0},{2,3},{3,2},{4,5},{5,4},{6,7},{7,6},{8,9},{9,8},{10,11... | collective-permute-start | bytes 884744 | tf_op jit(solution)/shard_map/ppermute | solution.py:78
  32.8 1.2 %collective-permute-done.4 = f32[4,144,128]{2,1,0:T(8,128)S(1)} collective-permute-done((f32[4,144,128]{2,1,0:T(8,128)S(1)}, f32[4,144,128]{2,1,0:T(8,128)S(1)}, u32[]{:S(2)}, u32[]{:S(2)}) %collective-permute-start.4) | collective-permute-done | bytes 294944 | tf_op jit(solution)/shard_map/ppermute | solution.py:78
  34.0 0.6 collective-permute-start.5
  34.6 1.8 %collective-permute-start.6 = (f32[144,128]{1,0:T(8,128)S(1)}, f32[144,128]{1,0:T(8,128)S(1)}, u32[]{:S(2)}, u32[]{:S(2)}) collective-permute-start(f32[144,128]{1,0:T(8,128)S(1)} %get-tuple-element.75), channel_id=1, source_target_pairs={{0,12},{4,8},{8,4},{12,0},{1,13},{5,9},{9,5},{13,1},{2,14},{6,10},... | collective-permute-start | bytes 221192 | tf_op jit(solution)/shard_map/ppermute | solution.py:78
  36.5 0.3 collective-permute-start.7
  36.8 2.1 %collective-permute-done.5 = f32[144,128]{1,0:T(8,128)S(1)} collective-permute-done((f32[144,128]{1,0:T(8,128)S(1)}, f32[144,128]{1,0:T(8,128)S(1)}, u32[]{:S(2)}, u32[]{:S(2)}) %collective-permute-start.5) | collective-permute-done | bytes 73760 | tf_op jit(solution)/shard_map/ppermute | solution.py:78
  38.9 2.5 %collective-permute-done.6 = f32[144,128]{1,0:T(8,128)S(1)} collective-permute-done((f32[144,128]{1,0:T(8,128)S(1)}, f32[144,128]{1,0:T(8,128)S(1)}, u32[]{:S(2)}, u32[]{:S(2)}) %collective-permute-start.6) | collective-permute-done | bytes 73760 | tf_op jit(solution)/shard_map/ppermute | solution.py:78
  41.4 0.0 collective-permute-done.7
  41.4 2.7 %collective-permute-start.10 = (f32[144,128]{1,0:T(8,128)S(1)}, f32[144,128]{1,0:T(8,128)S(1)}, u32[]{:S(2)}, u32[]{:S(2)}) collective-permute-start(f32[144,128]{1,0:T(8,128)S(1)} %fusion.1), channel_id=1, source_target_pairs={{0,32},{16,48},{32,0},{48,16},{64,96},{80,112},{96,64},{112,80},{1... | collective-permute-start | bytes 221192 | tf_op jit(solution)/shard_map/ppermute | solution.py:78
  44.1 0.6 collective-permute-start.8
  44.7 0.0 collective-permute-start.9
  44.7 1.5 %collective-permute-done.10 = f32[144,128]{1,0:T(8,128)S(1)} collective-permute-done((f32[144,128]{1,0:T(8,128)S(1)}, f32[144,128]{1,0:T(8,128)S(1)}, u32[]{:S(2)}, u32[]{:S(2)}) %collective-permute-start.10) | collective-permute-done | bytes 73760 | tf_op jit(solution)/shard_map/ppermute | solution.py:78
  46.2 2.3 %collective-permute-done.8 = f32[144,128]{1,0:T(8,128)S(1)} collective-permute-done((f32[144,128]{1,0:T(8,128)S(1)}, f32[144,128]{1,0:T(8,128)S(1)}, u32[]{:S(2)}, u32[]{:S(2)}) %collective-permute-start.8) | collective-permute-done | bytes 73760 | tf_op jit(solution)/shard_map/ppermute | solution.py:78
  48.6 1.7 %collective-permute-start.11 = (f32[144,128]{1,0:T(8,128)S(1)}, f32[144,128]{1,0:T(8,128)S(1)}, u32[]{:S(2)}, u32[]{:S(2)}) collective-permute-start(f32[144,128]{1,0:T(8,128)S(1)} %add_add_fusion), channel_id=1, source_target_pairs={{0,64},{1,65},{2,66},{3,67},{16,80},{17,81},{18,82},{19,83},{32,96... | collective-permute-start | bytes 221192 | tf_op jit(solution)/shard_map/ppermute | solution.py:78
  50.3 1.7 %collective-permute-done.11 = f32[144,128]{1,0:T(8,128)S(1)} collective-permute-done((f32[144,128]{1,0:T(8,128)S(1)}, f32[144,128]{1,0:T(8,128)S(1)}, u32[]{:S(2)}, u32[]{:S(2)}) %collective-permute-start.11) | collective-permute-done | bytes 73760 | tf_op jit(solution)/shard_map/ppermute | solution.py:78
  52.1 7.9 %collective-permute-start.12 = (f32[144,128]{1,0:T(8,128)S(1)}, f32[144,128]{1,0:T(8,128)S(1)}, u32[]{:S(2)}, u32[]{:S(2)}) collective-permute-start(f32[144,128]{1,0:T(8,128)S(1)} %add.85.own), channel_id=1, source_target_pairs={{0,66},{1,67},{2,64},{3,65},{16,82},{17,83},{18,80},{19,81},{32,98... | collective-permute-start | bytes 221192 | tf_op jit(solution)/shard_map/ppermute | solution.py:78
  59.9 0.0 collective-permute-start.13
  59.9 1.7 %collective-permute-start.14 = (f32[144,128]{1,0:T(8,128)S(1)}, f32[144,128]{1,0:T(8,128)S(1)}, u32[]{:S(2)}, u32[]{:S(2)}) collective-permute-start(f32[144,128]{1,0:T(8,128)S(1)} %add.85.own), channel_id=1, source_target_pairs={{0,192},{1,193},{2,194},{3,195},{16,208},{17,209},{18,210},{19,211... | collective-permute-start | bytes 221192 | tf_op jit(solution)/shard_map/ppermute | solution.py:78
  61.6 0.1 collective-permute-done.12.got_a
  61.7 4.2 %collective-permute-done.13.got_b = f32[144,128]{1,0:T(8,128)S(1)} collective-permute-done((f32[144,128]{1,0:T(8,128)S(1)}, f32[144,128]{1,0:T(8,128)S(1)}, u32[]{:S(2)}, u32[]{:S(2)}) %collective-permute-start.13) | collective-permute-done | bytes 73760 | tf_op jit(solution)/shard_map/ppermute | solution.py:78
  65.9 0.7 shard_map.89
  66.6 3.0 %collective-permute-start.15 = (f32[1,640]{1,0:T(1,128)S(1)}, f32[1,640]{1,0:T(1,128)S(1)}, u32[]{:S(2)}, u32[]{:S(2)}) collective-permute-start(f32[1,640]{1,0:T(1,128)S(1)} %get-tuple-element.69), channel_id=1, source_target_pairs={{0,1},{1,0},{2,3},{3,2},{4,5},{5,4},{6,7},{7,6},{8,9},{9,8},{10,11... | collective-permute-start | bytes 7688 | tf_op jit(solution)/shard_map/ppermute | solution.py:78
  69.5 0.8 %collective-permute-done.15 = f32[1,640]{1,0:T(1,128)S(1)} collective-permute-done((f32[1,640]{1,0:T(1,128)S(1)}, f32[1,640]{1,0:T(1,128)S(1)}, u32[]{:S(2)}, u32[]{:S(2)}) %collective-permute-start.15) | collective-permute-done | bytes 2592 | tf_op jit(solution)/shard_map/ppermute | solution.py:78
  70.3 1.0 %collective-permute-start.16 = (f32[1,640]{1,0:T(1,128)S(1)}, f32[1,640]{1,0:T(1,128)S(1)}, u32[]{:S(2)}, u32[]{:S(2)}) collective-permute-start(f32[1,640]{1,0:T(1,128)S(1)} %add.86), channel_id=1, source_target_pairs={{0,8},{4,12},{8,0},{12,4},{1,9},{5,13},{9,1},{13,5},{2,10},{6,14},... | collective-permute-start | bytes 7688 | tf_op jit(solution)/shard_map/ppermute | solution.py:78
  71.4 1.7 %collective-permute-start.17 = (f32[1,640]{1,0:T(1,128)S(1)}, f32[1,640]{1,0:T(1,128)S(1)}, u32[]{:S(2)}, u32[]{:S(2)}) collective-permute-start(f32[1,640]{1,0:T(1,128)S(1)} %add.86), channel_id=1, source_target_pairs={{0,12},{4,8},{8,4},{12,0},{1,13},{5,9},{9,5},{13,1},{2,14},{6,10},... | collective-permute-start | bytes 7688 | tf_op jit(solution)/shard_map/ppermute | solution.py:78
  73.1 0.6 multiply_add_fusion
  73.7 0.6 slice.27
  74.9 0.0 collective-permute-done.16
  74.9 0.4 collective-permute-done.17
  75.3 0.5 collective-permute-done.18
  75.9 0.7 multiply_subtract_fusion
  (22 shorter events, 0.2 us)
Async XLA Ops:
  0.6 1.4 %copy-start = (bf16[1,256,24,128]{3,2,1,0:T(8,128)(2,1)S(1)}, bf16[1,256,24,128]{3,2,1,0:T(8,128)(2,1)}, u32[]{:S(2)}) copy-start(bf16[1,256,24,128]{3,2,1,0:T(8,128)(2,1)} %image_ref.1) | copy-start | bytes 4718596
  2.1 4.8 %copy-start.1 = (f32[141312]{0:T(1024)S(1)}, f32[141312]{0:T(1024)}, u32[]{:S(2)}) copy-start(f32[141312]{0:T(1024)} %param.7) | copy-start | bytes 1695748
  2.1 4.8 %copy-start.2 = (f32[8,3840]{1,0:T(8,128)S(1)}, f32[8,3840]{1,0:T(8,128)}, u32[]{:S(2)}) copy-start(f32[8,3840]{1,0:T(8,128)} %constant.72.clone.table) | copy-start | bytes 368644
  3.3 5.1 %collective-permute-start = (bf16[128,128]{1,0:T(8,128)(2,1)S(1)}, bf16[128,128]{1,0:T(8,128)(2,1)S(1)}, u32[]{:S(2)}, u32[]{:S(2)}) collective-permute-start(bf16[128,128]{1,0:T(8,128)(2,1)S(1)} %get-tuple-element.78), channel_id=1, source_target_pairs={{4,8},{8,4},{0,12},{12,0},{5,9},{9,5},{1,13},{13,1},{6,10},{10,6},... | collective-permute-start | bytes 98312 | tf_op jit(solution)/shard_map/ppermute | solution.py:756
  6.7 2.8 %collective-permute-start.1 = (bf16[128,128]{1,0:T(8,128)(2,1)S(1)}, bf16[128,128]{1,0:T(8,128)(2,1)S(1)}, u32[]{:S(2)}, u32[]{:S(2)}) collective-permute-start(bf16[128,128]{1,0:T(8,128)(2,1)S(1)} %get-tuple-element.77), channel_id=1, source_target_pairs={{0,4},{4,0},{8,12},{12,8},{1,5},{5,1},{9,13},{13,9},{2,6},{6,2},{1... | collective-permute-start | bytes 98312 | tf_op jit(solution)/shard_map/ppermute | solution.py:757
  6.8 8.4 %copy-start.4 = (s32[1,1,2]{2,1,0:T(1,128)S(1)}, s32[1,1,2]{2,1,0:T(1,128)}, u32[]{:S(2)}) copy-start(s32[1,1,2]{2,1,0:T(1,128)} %param.6) | copy-start | bytes 28
  6.8 8.5 %copy-start.3 = (f32[552]{0:T(1024)S(1)}, f32[552]{0:T(1024)}, u32[]{:S(2)}) copy-start(f32[552]{0:T(1024)} %param.8) | copy-start | bytes 6628
  10.3 8.9 %collective-permute-start.2 = (bf16[272,256]{1,0:T(8,128)(2,1)S(1)}, bf16[272,256]{1,0:T(8,128)(2,1)S(1)}, u32[]{:S(2)}, u32[]{:S(2)}) collective-permute-start(bf16[272,256]{1,0:T(8,128)(2,1)S(1)} %get-tuple-element.43), channel_id=1, source_target_pairs={{16,32},{32,16},{48,64},{64,48},{80,96},{96,80},{112,128},{128,112... | collective-permute-start | bytes 417800 | tf_op jit(solution)/shard_map/ppermute | solution.py:760
  10.9 8.2 %collective-permute-start.3 = (bf16[272,256]{1,0:T(8,128)(2,1)S(1)}, bf16[272,256]{1,0:T(8,128)(2,1)S(1)}, u32[]{:S(2)}, u32[]{:S(2)}) collective-permute-start(bf16[272,256]{1,0:T(8,128)(2,1)S(1)} %get-tuple-element.44), channel_id=1, source_target_pairs={{0,16},{16,0},{32,48},{48,32},{64,80},{80,64},{96,112},{112,96},{1... | collective-permute-start | bytes 417800 | tf_op jit(solution)/shard_map/ppermute | solution.py:761
  30.0 4.0 %collective-permute-start.4 = (f32[4,144,128]{2,1,0:T(8,128)S(1)}, f32[4,144,128]{2,1,0:T(8,128)S(1)}, u32[]{:S(2)}, u32[]{:S(2)}) collective-permute-start(f32[4,144,128]{2,1,0:T(8,128)S(1)} %get-tuple-element.67), channel_id=1, source_target_pairs={{0,1},{1,0},{2,3},{3,2},{4,5},{5,4},{6,7},{7,6},{8,9},{9,8},{10,11... | collective-permute-start | bytes 884744 | tf_op jit(solution)/shard_map/ppermute | solution.py:78
  34.0 4.9 %collective-permute-start.5 = (f32[144,128]{1,0:T(8,128)S(1)}, f32[144,128]{1,0:T(8,128)S(1)}, u32[]{:S(2)}, u32[]{:S(2)}) collective-permute-start(f32[144,128]{1,0:T(8,128)S(1)} %get-tuple-element.76), channel_id=1, source_target_pairs={{0,8},{4,12},{8,0},{12,4},{1,9},{5,13},{9,1},{13,5},{2,10},{6,14},... | collective-permute-start | bytes 221192 | tf_op jit(solution)/shard_map/ppermute | solution.py:78
  34.6 6.7 %collective-permute-start.6 = (f32[144,128]{1,0:T(8,128)S(1)}, f32[144,128]{1,0:T(8,128)S(1)}, u32[]{:S(2)}, u32[]{:S(2)}) collective-permute-start(f32[144,128]{1,0:T(8,128)S(1)} %get-tuple-element.75), channel_id=1, source_target_pairs={{0,12},{4,8},{8,4},{12,0},{1,13},{5,9},{9,5},{13,1},{2,14},{6,10},... | collective-permute-start | bytes 221192 | tf_op jit(solution)/shard_map/ppermute | solution.py:78
  36.5 4.9 %collective-permute-start.7 = (f32[144,128]{1,0:T(8,128)S(1)}, f32[144,128]{1,0:T(8,128)S(1)}, u32[]{:S(2)}, u32[]{:S(2)}) collective-permute-start(f32[144,128]{1,0:T(8,128)S(1)} %get-tuple-element.74), channel_id=1, source_target_pairs={{0,4},{4,0},{8,12},{12,8},{1,5},{5,1},{9,13},{13,9},{2,6},{6,2},{1... | collective-permute-start | bytes 221192 | tf_op jit(solution)/shard_map/ppermute | solution.py:78
  41.4 4.8 %collective-permute-start.10 = (f32[144,128]{1,0:T(8,128)S(1)}, f32[144,128]{1,0:T(8,128)S(1)}, u32[]{:S(2)}, u32[]{:S(2)}) collective-permute-start(f32[144,128]{1,0:T(8,128)S(1)} %fusion.1), channel_id=1, source_target_pairs={{0,32},{16,48},{32,0},{48,16},{64,96},{80,112},{96,64},{112,80},{1... | collective-permute-start | bytes 221192 | tf_op jit(solution)/shard_map/ppermute | solution.py:78
  44.1 4.4 %collective-permute-start.8 = (f32[144,128]{1,0:T(8,128)S(1)}, f32[144,128]{1,0:T(8,128)S(1)}, u32[]{:S(2)}, u32[]{:S(2)}) collective-permute-start(f32[144,128]{1,0:T(8,128)S(1)} %fusion.1), channel_id=1, source_target_pairs={{0,48},{16,32},{32,16},{48,0},{64,112},{80,96},{96,80},{112,64},{1... | collective-permute-start | bytes 221192 | tf_op jit(solution)/shard_map/ppermute | solution.py:78
  44.7 3.9 %collective-permute-start.9 = (f32[144,128]{1,0:T(8,128)S(1)}, f32[144,128]{1,0:T(8,128)S(1)}, u32[]{:S(2)}, u32[]{:S(2)}) collective-permute-start(f32[144,128]{1,0:T(8,128)S(1)} %fusion.1), channel_id=1, source_target_pairs={{0,16},{16,0},{32,48},{48,32},{64,80},{80,64},{96,112},{112,96},{1... | collective-permute-start | bytes 221192 | tf_op jit(solution)/shard_map/ppermute | solution.py:78
  48.6 3.5 %collective-permute-start.11 = (f32[144,128]{1,0:T(8,128)S(1)}, f32[144,128]{1,0:T(8,128)S(1)}, u32[]{:S(2)}, u32[]{:S(2)}) collective-permute-start(f32[144,128]{1,0:T(8,128)S(1)} %add_add_fusion), channel_id=1, source_target_pairs={{0,64},{1,65},{2,66},{3,67},{16,80},{17,81},{18,82},{19,83},{32,96... | collective-permute-start | bytes 221192 | tf_op jit(solution)/shard_map/ppermute | solution.py:78
  52.1 9.6 %collective-permute-start.12 = (f32[144,128]{1,0:T(8,128)S(1)}, f32[144,128]{1,0:T(8,128)S(1)}, u32[]{:S(2)}, u32[]{:S(2)}) collective-permute-start(f32[144,128]{1,0:T(8,128)S(1)} %add.85.own), channel_id=1, source_target_pairs={{0,66},{1,67},{2,64},{3,65},{16,82},{17,83},{18,80},{19,81},{32,98... | collective-permute-start | bytes 221192 | tf_op jit(solution)/shard_map/ppermute | solution.py:78
  59.9 6.0 %collective-permute-start.13 = (f32[144,128]{1,0:T(8,128)S(1)}, f32[144,128]{1,0:T(8,128)S(1)}, u32[]{:S(2)}, u32[]{:S(2)}) collective-permute-start(f32[144,128]{1,0:T(8,128)S(1)} %add.85.own), channel_id=1, source_target_pairs={{0,194},{1,195},{2,192},{3,193},{16,210},{17,211},{18,208},{19,209... | collective-permute-start | bytes 221192 | tf_op jit(solution)/shard_map/ppermute | solution.py:78
  59.9 6.0 %collective-permute-start.14 = (f32[144,128]{1,0:T(8,128)S(1)}, f32[144,128]{1,0:T(8,128)S(1)}, u32[]{:S(2)}, u32[]{:S(2)}) collective-permute-start(f32[144,128]{1,0:T(8,128)S(1)} %add.85.own), channel_id=1, source_target_pairs={{0,192},{1,193},{2,194},{3,195},{16,208},{17,209},{18,210},{19,211... | collective-permute-start | bytes 221192 | tf_op jit(solution)/shard_map/ppermute | solution.py:78
  66.6 3.8 %collective-permute-start.15 = (f32[1,640]{1,0:T(1,128)S(1)}, f32[1,640]{1,0:T(1,128)S(1)}, u32[]{:S(2)}, u32[]{:S(2)}) collective-permute-start(f32[1,640]{1,0:T(1,128)S(1)} %get-tuple-element.69), channel_id=1, source_target_pairs={{0,1},{1,0},{2,3},{3,2},{4,5},{5,4},{6,7},{7,6},{8,9},{9,8},{10,11... | collective-permute-start | bytes 7688 | tf_op jit(solution)/shard_map/ppermute | solution.py:78
  70.3 4.6 %collective-permute-start.16 = (f32[1,640]{1,0:T(1,128)S(1)}, f32[1,640]{1,0:T(1,128)S(1)}, u32[]{:S(2)}, u32[]{:S(2)}) collective-permute-start(f32[1,640]{1,0:T(1,128)S(1)} %add.86), channel_id=1, source_target_pairs={{0,8},{4,12},{8,0},{12,4},{1,9},{5,13},{9,1},{13,5},{2,10},{6,14},... | collective-permute-start | bytes 7688 | tf_op jit(solution)/shard_map/ppermute | solution.py:78
  71.4 3.9 %collective-permute-start.17 = (f32[1,640]{1,0:T(1,128)S(1)}, f32[1,640]{1,0:T(1,128)S(1)}, u32[]{:S(2)}, u32[]{:S(2)}) collective-permute-start(f32[1,640]{1,0:T(1,128)S(1)} %add.86), channel_id=1, source_target_pairs={{0,12},{4,8},{8,4},{12,0},{1,13},{5,9},{9,5},{13,1},{2,14},{6,10},... | collective-permute-start | bytes 7688 | tf_op jit(solution)/shard_map/ppermute | solution.py:78
  73.1 2.7 %collective-permute-start.18 = (f32[1,640]{1,0:T(1,128)S(1)}, f32[1,640]{1,0:T(1,128)S(1)}, u32[]{:S(2)}, u32[]{:S(2)}) collective-permute-start(f32[1,640]{1,0:T(1,128)S(1)} %add.86), channel_id=1, source_target_pairs={{0,4},{4,0},{8,12},{12,8},{1,5},{5,1},{9,13},{13,9},{2,6},{6,2},{1... | collective-permute-start | bytes 7688 | tf_op jit(solution)/shard_map/ppermute | solution.py:78
